TPU v7x, 1024 devices: a whole 4x8x16 slice. The times are simulated.
1024 devices in a mesh: grp: 16 (over y, core), dom: 64 (over z, x).
Axes of the slice: x: 4, y: 8, z: 16, core: 2. Of those that a mesh axis runs over, the one named last changes fastest.
Arguments:
- x_edges: float32 [2, 1572864], P(None, ('grp', 'dom')), may hold values from -6 to 6
- x_inner: float32 [2, 1048576], P(None, ('grp', 'dom')), may hold values from -6 to 6
- b_edges: float32 [2, 1572864], P(None, ('grp', 'dom')), may hold values from -6 to 6
- b_inner: float32 [2, 1048576], P(None, ('grp', 'dom')), may hold values from -6 to 6
- w_edges: float32 [2, 1572864], P(None, ('grp', 'dom')), may hold values from 0.05 to 0.3
- w_inner: float32 [2, 1048576], P(None, ('grp', 'dom')), may hold values from 0.05 to 0.3
- elem_edges: int32 [3, 1048576], P(None, ('grp', 'dom')), may hold values from 0 to 3199
- element_live: int32 [1048576], P(('grp', 'dom')), may hold values 0 or 1
- elem_matrix: float32 [8, 8, 1048576], P(None, None, ('grp', 'dom')), may hold values from -3.36 to 6, as said below
- projection: float32 [8, 6, 1048576], P(None, None, ('grp', 'dom')), may hold values from -2.5 to 2.5
- owner_counts: int32 [1024, 64], P(('grp', 'dom')), may hold values from 1 to 96, 3072 in all within a row
- aux_node: int32 [6291456], P(('grp', 'dom')), may hold values from 0 to 255
- aux_inverse: float32 [4096, 128, 128], P(('grp', 'dom')), may hold values from -0.22627416997969518 to 3, as said below
Outputs:
- x1_edges: float32 [2, 1572864], P(None, ('grp', 'dom'))
- x1_inner: float32 [2, 1048576], P(None, ('grp', 'dom'))
- r1_edges: float32 [2, 1572864], P(None, ('grp', 'dom'))
- r1_inner: float32 [2, 1048576], P(None, ('grp', 'dom'))
Inputs may be any that keep to these rules, and one draw needn't show every extreme that they name: `owner_counts`: every row sums to 3072. `elem_matrix`: symmetric in the first two dimensions. `aux_inverse`: symmetric in the last two dimensions.
All inputs are finite; a program needn't handle non-finite values. No bound on the sum of `element_live` on one device may be relied on, other than what follows from the above.
Results may differ from a plain program's by a relative error of at most 0.0003.
Values sent between devices are 32-bit elements; how exact they have to be, the bound alone decides.
No kernel may reach another device: no remote copies, remote signals or barrier semaphores. Data moves between devices by JAX's collectives and lax.ppermute only.
A program may use at most 32 MiB of HBM per device.

v0:
```python
import jax
import jax.numpy as jnp
from jax import lax
from jax.sharding import PartitionSpec as P


def with_halo(cells, sides, width):
    for axis, dim in sides:
        count = lax.axis_size(axis)
        ends = count - 1
        head = lax.slice_in_dim(cells, 0, width, axis=dim)
        tail = lax.slice_in_dim(cells, cells.shape[dim] - width, cells.shape[dim], axis=dim)
        cells = jnp.concatenate(
            [
                lax.ppermute(tail, axis, [(i, (i + 1) % count) for i in range(ends)]),
                cells,
                lax.ppermute(head, axis, [((i + 1) % count, i) for i in range(ends)]),
            ],
            axis=dim,
        )
    return cells


def gather_elements(extended, inner, local, signs):
    picked = jnp.transpose(extended[:, local], (1, 0, 2)) * signs
    return jnp.concatenate([picked.reshape(6, -1), inner], 0)


def scatter_partial(values, local, signs, width):
    parts = values[:6].reshape(3, 2, -1) * signs
    total = jnp.zeros((2, width), jnp.float32)
    return total.at[:, local].add(jnp.transpose(parts, (1, 0, 2)))


def element_apply(elem_matrix, live, extended, inner, local, signs):
    u = gather_elements(extended, inner, local, signs)
    return live * jnp.sum(elem_matrix * u[None, :, :], axis=1)


def extend_owned(owned, rim):
    return with_halo(owned, ((("grp", "dom"), 1),), rim)


def settle_owned(partial_value, rim, edge_count):
    ends = jnp.concatenate([partial_value[:, :rim], partial_value[:, -rim:]], 1)
    arrived = with_halo(ends, ((("grp", "dom"), 1),), rim)
    owned = partial_value[:, rim : rim + edge_count]
    owned = owned.at[:, :rim].add(arrived[:, :rim])
    return owned.at[:, -rim:].add(arrived[:, -rim:])


def auxiliary_correction(
    r_ext, r_inner, local, signs, live, projection, owner_counts, aux_node, aux_inverse
):
    elem_count = r_inner.shape[1]
    peers = owner_counts.shape[1]
    cap = 6 * elem_count // peers
    counts = owner_counts[0]
    u = gather_elements(r_ext, r_inner, local, signs)
    restricted = live * jnp.sum(projection * u[:, None, :], axis=0)
    vals = jnp.transpose(restricted.reshape(3, 2, elem_count), (1, 0, 2)).reshape(2, 3 * elem_count)
    ends = jnp.cumsum(counts)
    starts = ends - counts
    slot = jnp.arange(cap, dtype=jnp.int32)
    filled = slot[None, :] < counts[:, None]
    positions = jnp.clip(starts[:, None] + slot[None, :], 0, 3 * elem_count - 1)
    packed = jnp.where(filled[None, :, :], vals[:, positions], 0.0)
    arrived = lax.all_to_all(packed, "dom", split_axis=1, concat_axis=1, tiled=True)
    aux_count = elem_count // 4
    totals = jnp.zeros((2, aux_count), jnp.float32).at[:, aux_node].add(arrived.reshape(2, -1))
    groups = aux_inverse.shape[0]
    agg = aux_inverse.shape[1] // 2
    blocks = jnp.transpose(totals.reshape(2, groups, agg), (1, 0, 2)).reshape(groups, 2 * agg)
    solved = jnp.einsum("bij,bj->bi", aux_inverse, blocks, precision=lax.Precision.HIGHEST)
    solved = jnp.transpose(solved.reshape(groups, 2, agg), (1, 0, 2)).reshape(2, aux_count)
    outgoing = solved[:, aux_node].reshape(2, peers, cap)
    returned = lax.all_to_all(outgoing, "dom", split_axis=1, concat_axis=1, tiled=True).reshape(
        2, peers * cap
    )
    entry = jnp.arange(3 * elem_count, dtype=jnp.int32)
    owner = jnp.sum((entry[:, None] >= ends[None, :]).astype(jnp.int32), axis=1)
    flat = owner * cap + entry - starts[owner]
    picked = returned[:, flat]
    nodal = jnp.transpose(picked.reshape(2, 3, elem_count), (1, 0, 2)).reshape(6, elem_count)
    return live * jnp.sum(projection * nodal[None, :, :], axis=1)


def shards(
    x_edges,
    x_inner,
    b_edges,
    b_inner,
    w_edges,
    w_inner,
    elem_edges,
    element_live,
    elem_matrix,
    projection,
    owner_counts,
    aux_node,
    aux_inverse,
):
    edge_count = x_edges.shape[1]
    elem_count = x_inner.shape[1]
    rim = elem_count // 32
    width = edge_count + 2 * rim
    local = elem_edges // 2
    flip = (1 - 2 * (elem_edges % 2)).astype(jnp.float32)
    signs = jnp.stack([flip, jnp.ones_like(flip)], 1)
    live = element_live.astype(jnp.float32)[None, :]
    x_ext = extend_owned(x_edges, rim)
    y_elem = element_apply(elem_matrix, live, x_ext, x_inner, local, signs)
    y_edges = settle_owned(scatter_partial(y_elem, local, signs, width), rim, edge_count)
    r_edges = b_edges - y_edges
    r_inner = b_inner - y_elem[6:8]
    r_ext = extend_owned(r_edges, rim)
    p_elem = auxiliary_correction(
        r_ext, r_inner, local, signs, live, projection, owner_counts, aux_node, aux_inverse
    )
    p_edges = settle_owned(scatter_partial(p_elem, local, signs, width), rim, edge_count)
    z_edges = w_edges * r_edges + p_edges
    z_inner = w_inner * r_inner + p_elem[6:8]
    z_ext = extend_owned(z_edges, rim)
    az_elem = element_apply(elem_matrix, live, z_ext, z_inner, local, signs)
    az_edges = settle_owned(scatter_partial(az_elem, local, signs, width), rim, edge_count)
    r1_edges = r_edges - az_edges
    return (x_edges + z_edges, x_inner + z_inner, r1_edges, r_inner - az_elem[6:8])


def solution(mesh):
    in_specs = (
        P(None, ("grp", "dom")),
        P(None, ("grp", "dom")),
        P(None, ("grp", "dom")),
        P(None, ("grp", "dom")),
        P(None, ("grp", "dom")),
        P(None, ("grp", "dom")),
        P(None, ("grp", "dom")),
        P(("grp", "dom")),
        P(None, None, ("grp", "dom")),
        P(None, None, ("grp", "dom")),
        P(("grp", "dom"), None),
        P(("grp", "dom")),
        P(("grp", "dom"), None, None),
    )
    out_specs = (
        P(None, ("grp", "dom")),
        P(None, ("grp", "dom")),
        P(None, ("grp", "dom")),
        P(None, ("grp", "dom")),
    )
    return jax.shard_map(shards, mesh=mesh, in_specs=in_specs, out_specs=out_specs, check_vma=False)
```

profile of v0, /device:TPU:32, one launch (start us, length us, event | category | flops | bytes accessed | tf_op | source)
XLA Modules:
  0.0 377.2 jit_solution(16136000890416137840)
XLA Ops:
  1.5 3.4 collective-permute-start
  4.9 18.3 %collective-permute-start.1 = (f32[2,32]{1,0:T(2,128)S(1)}, f32[2,32]{1,0:T(2,128)S(1)}, u32[]{:S(2)}, u32[]{:S(2)}) collective-permute-start(f32[2,32]{1,0:T(2,128)S(1)} %get-tuple-element.173), channel_id=1, source_target_pairs={{1,0},{2,1},{3,2},{4,3},{5,4},{6,5},{7,6},{8,7},{9,8},{10,9},{11,1... | collective-permute-start | bytes 776 | tf_op jit(solution)/shard_map/ppermute | solution.py:17
  27.9 4.4 %compare_select_fusion.4 = (s32[3072,1]{0,1:T(1,128)S(1)}, s32[3072,1]{0,1:T(1,128)S(1)}) fusion(s32[]{:T(128)} %bitcast.82, s32[]{:T(128)} %bitcast.83, s32[]{:T(128)} %bitcast.84, s32[]{:T(128)} %bitcast.85, s32[]{:T(128)} %bitcast.86, s32[]{:T(128)} %bitcast.88, s32[]{:T(128)} %bitcast.87, s32[3072,1]{0,1:T(1,128)S(1)} %bitcast.137), kind=kLoop, calls=%fused_computation.95 | loop fusion | flops 46080 | bytes 36892 | tf_op jit(solution)/shard_map/gather | solution.py:82
  32.3 2.2 compare_reduce_fusion.56
  34.5 35.8 %select_select_fusion = s32[3072]{0:T(1024)S(1)} fusion(pred[3072]{0:T(1024)(128)(4,1)S(1)} %get-tuple-element.152, pred[3072]{0:T(1024)(128)(4,1)S(1)} %get-tuple-element.151, pred[3072]{0:T(1024)(128)(4,1)S(1)} %get-tuple-element.150, pred[3072]{0:T(1024)(128)(4,1)S(1)} %get-tuple-element.149, pred[3072]{0:T(1024)(128)(4,1)S(1)} %get-tuple-element.148, ...), kind=kLoop, calls=%fused_computation.138 | loop fusion | flops 175104 | bytes 199908 | tf_op jit(solution)/shard_map/gather | solution.py:82
  71.9 1.3 iota_compare_fusion.1
  73.2 1.0 copy.151
  75.0 1.2 copy.130
  76.2 9.3 %gather_fusion = f32[3072,2]{1,0:T(8,128)S(1)} fusion(f32[2,1600]{0,1:T(8,128)} %copy.130, s32[3072]{0:T(1024)S(1)} %broadcast_clamp_fusion.3), kind=kCustom, calls=%fused_computation | custom fusion | bytes 61440 | tf_op jit(solution)/shard_map/gather | solution.py:25
  86.4 1.7 copy.160
  88.0 17.4 %scatter_custom_fusion = f32[2,1600]{0,1:T(8,128)S(1)} fusion(s32[3072]{0:T(1024)S(1)} %reshape.474, f32[3072,2]{1,0:T(8,128)} %bitcast.130, f32[]{:T(128)} %constant.176.clone.1), kind=kCustom, calls=%fused_computation.19 | custom fusion | flops 6144 | bytes 13312 | tf_op jit(solution)/shard_map/scatter-add | solution.py:32
  105.5 1.9 collective-permute-start.2
  107.8 9.1 %collective-permute-start.3 = (f32[2,32]{0,1:T(8,128)S(1)}, f32[2,32]{0,1:T(8,128)S(1)}, u32[]{:S(2)}, u32[]{:S(2)}) collective-permute-start(f32[2,32]{0,1:T(8,128)S(1)} %get-tuple-element.163), channel_id=1, source_target_pairs={{1,0},{2,1},{3,2},{4,3},{5,4},{6,5},{7,6},{8,7},{9,8},{10,9},{11,1... | collective-permute-start | bytes 776 | tf_op jit(solution)/shard_map/ppermute | solution.py:17
  118.4 1.9 collective-permute-start.4
  120.3 9.1 %collective-permute-start.5 = (f32[2,32]{0,1:T(8,128)S(1)}, f32[2,32]{0,1:T(8,128)S(1)}, u32[]{:S(2)}, u32[]{:S(2)}) collective-permute-start(f32[2,32]{0,1:T(8,128)S(1)} %get-tuple-element.168), channel_id=1, source_target_pairs={{1,0},{2,1},{3,2},{4,3},{5,4},{6,5},{7,6},{8,7},{9,8},{10,9},{11,1... | collective-permute-start | bytes 776 | tf_op jit(solution)/shard_map/ppermute | solution.py:17
  129.4 1.4 collective-permute-done.5
  130.8 0.9 pad_maximum_fusion
  131.8 9.3 %gather_fusion.1 = f32[3072,2]{1,0:T(8,128)S(1)} fusion(f32[2,1600]{0,1:T(8,128)} %pad_maximum_fusion, s32[3072]{0:T(1024)S(1)} %broadcast_clamp_fusion.3), kind=kCustom, calls=%fused_computation.1 | custom fusion | bytes 61440 | tf_op jit(solution)/shard_map/gather | solution.py:25
  141.8 1.0 multiply_reduce_fusion.3
  143.3 20.9 %gather_fusion.2 = f32[6144,2]{1,0:T(8,128)} fusion(f32[2,3072]{0,1:T(8,128)S(1)} %bitcast.123, s32[6144]{0:T(1024)S(1)} %broadcast_clamp_fusion.1), kind=kCustom, calls=%fused_computation.2 | custom fusion | bytes 122880 | tf_op jit(solution)/shard_map/gather | solution.py:67
  164.2 2.4 copy.141
  167.3 7.9 %all-to-all-start = ((f32[2,64,96]{2,0,1:T(2,128)}), f32[2,64,96]{2,0,1:T(2,128)S(1)}, u32[]{:S(2)}, u32[]{:S(2)}) async-start(f32[2,64,96]{2,0,1:T(2,128)} %select_bitcast_fusion), calls=%async_computation | async-start | bytes 131072 | tf_op jit(solution)/shard_map/all_to_all | solution.py:68
  175.3 15.0 %all-to-all-done = f32[2,64,96]{2,0,1:T(2,128)S(1)} async-done(((f32[2,64,96]{2,0,1:T(2,128)}), f32[2,64,96]{2,0,1:T(2,128)S(1)}, u32[]{:S(2)}, u32[]{:S(2)}) %all-to-all-start) | async-done | bytes 49184 | tf_op jit(solution)/shard_map/all_to_all | solution.py:68
  190.4 2.2 copy.143
  192.7 33.5 %scatter_custom_fusion.1 = f32[2,256]{0,1:T(8,128)S(1)} fusion(s32[6144]{0:T(1024)S(1)} %get-tuple-element.170, f32[6144,2]{1,0:T(8,128)} %copy.143, f32[]{:T(128)} %constant.176.clone.1), kind=kCustom, calls=%fused_computation.30 | custom fusion | flops 12288 | bytes 2560 | tf_op jit(solution)/shard_map/scatter-add | solution.py:70
  227.1 20.9 %gather_fusion.3 = f32[6144,2]{1,0:T(8,128)} fusion(f32[2,256]{0,1:T(8,128)S(1)} %bitcast.124, s32[6144]{0:T(1024)S(1)} %get-tuple-element.169), kind=kCustom, calls=%fused_computation.3 | custom fusion | bytes 122880 | tf_op jit(solution)/shard_map/gather | solution.py:76
  248.0 3.0 copy.146
  251.0 4.6 %all-to-all-start.1 = ((f32[2,64,96]{2,0,1:T(2,128)}), f32[2,64,96]{2,0,1:T(2,128)S(1)}, u32[]{:S(2)}, u32[]{:S(2)}) async-start(f32[2,64,96]{2,0,1:T(2,128)} %copy.146), calls=%async_computation.1 | async-start | bytes 131072 | tf_op jit(solution)/shard_map/all_to_all | solution.py:77
  255.6 15.0 %all-to-all-done.1 = f32[2,64,96]{2,0,1:T(2,128)S(1)} async-done(((f32[2,64,96]{2,0,1:T(2,128)}), f32[2,64,96]{2,0,1:T(2,128)S(1)}, u32[]{:S(2)}, u32[]{:S(2)}) %all-to-all-start.1) | async-done | bytes 49184 | tf_op jit(solution)/shard_map/all_to_all | solution.py:77
  270.7 2.2 copy.147
  272.9 10.0 %gather_fusion.4 = f32[3072,2]{1,0:T(8,128)S(1)} fusion(f32[2,6144]{0,1:T(8,128)} %bitcast.120, s32[3072]{0:T(1024)S(1)} %broadcast_clamp_fusion.2), kind=kCustom, calls=%fused_computation.4 | custom fusion | bytes 61440 | tf_op jit(solution)/shard_map/gather | solution.py:83
  283.4 1.0 multiply_reduce_fusion.2
  284.4 1.7 copy.161
  286.1 17.4 %scatter_custom_fusion.2 = f32[2,1600]{0,1:T(8,128)S(1)} fusion(s32[3072]{0:T(1024)S(1)} %reshape.474, f32[3072,2]{1,0:T(8,128)} %bitcast.131, f32[]{:T(128)} %constant.176.clone.1), kind=kCustom, calls=%fused_computation.17 | custom fusion | flops 6144 | bytes 13312 | tf_op jit(solution)/shard_map/scatter-add | solution.py:32
  304.1 2.5 collective-permute-start.6
  306.6 1.0 copy.136
  308.3 8.5 %collective-permute-start.7 = (f32[2,32]{0,1:T(8,128)S(1)}, f32[2,32]{0,1:T(8,128)S(1)}, u32[]{:S(2)}, u32[]{:S(2)}) collective-permute-start(f32[2,32]{0,1:T(8,128)S(1)} %copy-done.9), channel_id=1, source_target_pairs={{1,0},{2,1},{3,2},{4,3},{5,4},{6,5},{7,6},{8,7},{9,8},{10,9},{11,1... | collective-permute-start | bytes 776 | tf_op jit(solution)/shard_map/ppermute | solution.py:17
  318.3 1.1 fusion.23
  319.3 1.9 collective-permute-start.8
  321.3 9.1 %collective-permute-start.9 = (f32[2,32]{0,1:T(8,128)S(1)}, f32[2,32]{0,1:T(8,128)S(1)}, u32[]{:S(2)}, u32[]{:S(2)}) collective-permute-start(f32[2,32]{0,1:T(8,128)S(1)} %get-tuple-element.166), channel_id=1, source_target_pairs={{1,0},{2,1},{3,2},{4,3},{5,4},{6,5},{7,6},{8,7},{9,8},{10,9},{11,1... | collective-permute-start | bytes 776 | tf_op jit(solution)/shard_map/ppermute | solution.py:17
  331.0 2.0 copy.156
  333.0 0.9 pad_maximum_fusion.1
  333.9 9.3 %gather_fusion.5 = f32[3072,2]{1,0:T(8,128)S(1)} fusion(f32[2,1600]{0,1:T(8,128)} %pad_maximum_fusion.1, s32[3072]{0:T(1024)S(1)} %broadcast_clamp_fusion.3), kind=kCustom, calls=%fused_computation.5 | custom fusion | bytes 61440 | tf_op jit(solution)/shard_map/gather | solution.py:25
  344.1 1.7 copy.162
  345.7 17.4 %scatter_custom_fusion.3 = f32[2,1600]{0,1:T(8,128)S(1)} fusion(s32[3072]{0:T(1024)S(1)} %reshape.474, f32[3072,2]{1,0:T(8,128)} %bitcast.129, f32[]{:T(128)} %constant.176.clone.1), kind=kCustom, calls=%fused_computation.15 | custom fusion | flops 6144 | bytes 13312 | tf_op jit(solution)/shard_map/scatter-add | solution.py:32
  363.2 1.9 collective-permute-start.10
  365.8 9.1 %collective-permute-start.11 = (f32[2,32]{0,1:T(8,128)S(1)}, f32[2,32]{0,1:T(8,128)S(1)}, u32[]{:S(2)}, u32[]{:S(2)}) collective-permute-start(f32[2,32]{0,1:T(8,128)S(1)} %get-tuple-element.159), channel_id=1, source_target_pairs={{1,0},{2,1},{3,2},{4,3},{5,4},{6,5},{7,6},{8,7},{9,8},{10,9},{11,1... | collective-permute-start | bytes 776 | tf_op jit(solution)/shard_map/ppermute | solution.py:17
  376.4 0.9 copy.157
  (120 shorter events, 20.3 us)
Async XLA Ops:
  0.6 225.7 %copy-start = (f32[4,128,128]{2,1,0:T(8,128)S(1)}, f32[4,128,128]{2,1,0:T(8,128)}, u32[]{:S(2)}) copy-start(f32[4,128,128]{2,1,0:T(8,128)} %param.37) | copy-start | bytes 786436
  0.6 74.2 %copy-start.3 = (f32[2,1536]{1,0:T(2,128)S(1)}, f32[2,1536]{1,0:T(2,128)}, u32[]{:S(2)}) copy-start(f32[2,1536]{1,0:T(2,128)} %param.25) | copy-start | bytes 36868
  0.7 73.5 %copy-start.13 = (s32[1024]{0:T(1024)S(1)}, s32[1024]{0:T(1024)}, u32[]{:S(2)}) copy-start(s32[1024]{0:T(1024)} %param.32) | copy-start | bytes 12292
  1.5 73.4 %collective-permute-start = (f32[2,32]{1,0:T(2,128)S(1)}, f32[2,32]{1,0:T(2,128)S(1)}, u32[]{:S(2)}, u32[]{:S(2)}) collective-permute-start(f32[2,32]{1,0:T(2,128)S(1)} %get-tuple-element.174), channel_id=1, source_target_pairs={{0,1},{1,2},{2,3},{3,4},{4,5},{5,6},{6,7},{7,8},{8,9},{9,10},{10,1... | collective-permute-start | bytes 776 | tf_op jit(solution)/shard_map/ppermute | solution.py:15
  4.9 70.0 %collective-permute-start.1 = (f32[2,32]{1,0:T(2,128)S(1)}, f32[2,32]{1,0:T(2,128)S(1)}, u32[]{:S(2)}, u32[]{:S(2)}) collective-permute-start(f32[2,32]{1,0:T(2,128)S(1)} %get-tuple-element.173), channel_id=1, source_target_pairs={{1,0},{2,1},{3,2},{4,3},{5,4},{6,5},{7,6},{8,7},{9,8},{10,9},{11,1... | collective-permute-start | bytes 776 | tf_op jit(solution)/shard_map/ppermute | solution.py:17
  74.2 12.0 %copy-start.6 = (f32[2,1024]{1,0:T(2,128)S(1)}, f32[2,1024]{1,0:T(2,128)}, u32[]{:S(2)}) copy-start(f32[2,1024]{1,0:T(2,128)} %param.26) | copy-start | bytes 24580
  74.2 12.0 %copy-start.1 = (f32[8,8,1024]{2,1,0:T(8,128)S(1)}, f32[8,8,1024]{2,1,0:T(8,128)}, u32[]{:S(2)}) copy-start(f32[8,8,1024]{2,1,0:T(8,128)} %param.33) | copy-start | bytes 786436
  86.1 21.3 %copy-start.10 = (f32[2,1536]{1,0:T(2,128)S(1)}, f32[2,1536]{1,0:T(2,128)}, u32[]{:S(2)}) copy-start(f32[2,1536]{1,0:T(2,128)} %param.27) | copy-start | bytes 36868
  105.5 11.4 %collective-permute-start.2 = (f32[2,32]{0,1:T(8,128)S(1)}, f32[2,32]{0,1:T(8,128)S(1)}, u32[]{:S(2)}, u32[]{:S(2)}) collective-permute-start(f32[2,32]{0,1:T(8,128)S(1)} %get-tuple-element.164), channel_id=1, source_target_pairs={{0,1},{1,2},{2,3},{3,4},{4,5},{5,6},{6,7},{7,8},{8,9},{9,10},{10,1... | collective-permute-start | bytes 776 | tf_op jit(solution)/shard_map/ppermute | solution.py:15
  107.8 21.6 %copy-start.11 = (f32[2,1024]{1,0:T(2,128)S(1)}, f32[2,1024]{1,0:T(2,128)}, u32[]{:S(2)}) copy-start(f32[2,1024]{1,0:T(2,128)} %param.28) | copy-start | bytes 24580
  107.8 10.5 %collective-permute-start.3 = (f32[2,32]{0,1:T(8,128)S(1)}, f32[2,32]{0,1:T(8,128)S(1)}, u32[]{:S(2)}, u32[]{:S(2)}) collective-permute-start(f32[2,32]{0,1:T(8,128)S(1)} %get-tuple-element.163), channel_id=1, source_target_pairs={{1,0},{2,1},{3,2},{4,3},{5,4},{6,5},{7,6},{8,7},{9,8},{10,9},{11,1... | collective-permute-start | bytes 776 | tf_op jit(solution)/shard_map/ppermute | solution.py:17
  118.4 11.0 %collective-permute-start.4 = (f32[2,32]{0,1:T(8,128)S(1)}, f32[2,32]{0,1:T(8,128)S(1)}, u32[]{:S(2)}, u32[]{:S(2)}) collective-permute-start(f32[2,32]{0,1:T(8,128)S(1)} %get-tuple-element.167), channel_id=1, source_target_pairs={{0,1},{1,2},{2,3},{3,4},{4,5},{5,6},{6,7},{7,8},{8,9},{9,10},{10,1... | collective-permute-start | bytes 776 | tf_op jit(solution)/shard_map/ppermute | solution.py:15
  120.3 10.5 %collective-permute-start.5 = (f32[2,32]{0,1:T(8,128)S(1)}, f32[2,32]{0,1:T(8,128)S(1)}, u32[]{:S(2)}, u32[]{:S(2)}) collective-permute-start(f32[2,32]{0,1:T(8,128)S(1)} %get-tuple-element.168), channel_id=1, source_target_pairs={{1,0},{2,1},{3,2},{4,3},{5,4},{6,5},{7,6},{8,7},{9,8},{10,9},{11,1... | collective-permute-start | bytes 776 | tf_op jit(solution)/shard_map/ppermute | solution.py:17
  164.2 2.4 copy-start.5
  164.2 11.0 %copy-start.8 = (s32[6144]{0:T(1024)S(1)}, s32[6144]{0:T(1024)}, u32[]{:S(2)}) copy-start(s32[6144]{0:T(1024)} %param.36) | copy-start | bytes 73732
  167.3 23.0 %all-to-all-start = ((f32[2,64,96]{2,0,1:T(2,128)}), f32[2,64,96]{2,0,1:T(2,128)S(1)}, u32[]{:S(2)}, u32[]{:S(2)}) async-start(f32[2,64,96]{2,0,1:T(2,128)} %select_bitcast_fusion), calls=%async_computation | async-start | bytes 131072 | tf_op jit(solution)/shard_map/all_to_all | solution.py:68
  248.0 7.6 %copy-start.4 = (s32[3072,1]{0,1:T(1,128)S(1)}, s32[3072,1]{0,1:T(1,128)}, u32[]{:S(2)}) copy-start(s32[3072,1]{0,1:T(1,128)} %compare_select_fusion.1) | copy-start | bytes 36868
  251.0 19.7 %all-to-all-start.1 = ((f32[2,64,96]{2,0,1:T(2,128)}), f32[2,64,96]{2,0,1:T(2,128)S(1)}, u32[]{:S(2)}, u32[]{:S(2)}) async-start(f32[2,64,96]{2,0,1:T(2,128)} %copy.146), calls=%async_computation.1 | async-start | bytes 131072 | tf_op jit(solution)/shard_map/all_to_all | solution.py:77
  304.1 12.7 %collective-permute-start.6 = (f32[2,32]{0,1:T(8,128)}, f32[2,32]{0,1:T(8,128)S(1)}, u32[]{:S(2)}, u32[]{:S(2)}) collective-permute-start(f32[2,32]{0,1:T(8,128)} %get-tuple-element.162), channel_id=1, source_target_pairs={{0,1},{1,2},{2,3},{3,4},{4,5},{5,6},{6,7},{7,8},{8,9},{9,10},{10,1... | collective-permute-start | bytes 776 | tf_op jit(solution)/shard_map/ppermute | solution.py:15
  307.6 0.7 copy-start.9
  308.3 9.9 %collective-permute-start.7 = (f32[2,32]{0,1:T(8,128)S(1)}, f32[2,32]{0,1:T(8,128)S(1)}, u32[]{:S(2)}, u32[]{:S(2)}) collective-permute-start(f32[2,32]{0,1:T(8,128)S(1)} %copy-done.9), channel_id=1, source_target_pairs={{1,0},{2,1},{3,2},{4,3},{5,4},{6,5},{7,6},{8,7},{9,8},{10,9},{11,1... | collective-permute-start | bytes 776 | tf_op jit(solution)/shard_map/ppermute | solution.py:17
  318.3 12.1 %copy-start.7 = (f32[2,1024]{1,0:T(2,128)S(1)}, f32[2,1024]{1,0:T(2,128)}, u32[]{:S(2)}) copy-start(f32[2,1024]{1,0:T(2,128)} %param.26) | copy-start | bytes 24580
  318.3 12.1 %copy-start.12 = (f32[2,1024]{1,0:T(2,128)S(1)}, f32[2,1024]{1,0:T(2,128)}, u32[]{:S(2)}) copy-start(f32[2,1024]{1,0:T(2,128)} %param.30) | copy-start | bytes 24580
  319.3 13.6 %collective-permute-start.8 = (f32[2,32]{0,1:T(8,128)S(1)}, f32[2,32]{0,1:T(8,128)S(1)}, u32[]{:S(2)}, u32[]{:S(2)}) collective-permute-start(f32[2,32]{0,1:T(8,128)S(1)} %get-tuple-element.165), channel_id=1, source_target_pairs={{0,1},{1,2},{2,3},{3,4},{4,5},{5,6},{6,7},{7,8},{8,9},{9,10},{10,1... | collective-permute-start | bytes 776 | tf_op jit(solution)/shard_map/ppermute | solution.py:15
  321.3 11.7 %collective-permute-start.9 = (f32[2,32]{0,1:T(8,128)S(1)}, f32[2,32]{0,1:T(8,128)S(1)}, u32[]{:S(2)}, u32[]{:S(2)}) collective-permute-start(f32[2,32]{0,1:T(8,128)S(1)} %get-tuple-element.166), channel_id=1, source_target_pairs={{1,0},{2,1},{3,2},{4,3},{5,4},{6,5},{7,6},{8,7},{9,8},{10,9},{11,1... | collective-permute-start | bytes 776 | tf_op jit(solution)/shard_map/ppermute | solution.py:17
  333.0 10.9 %copy-start.2 = (f32[8,8,1024]{2,1,0:T(8,128)S(1)}, f32[8,8,1024]{2,1,0:T(8,128)}, u32[]{:S(2)}) copy-start(f32[8,8,1024]{2,1,0:T(8,128)} %param.33) | copy-start | bytes 786436
  363.2 11.7 %collective-permute-start.10 = (f32[2,32]{0,1:T(8,128)S(1)}, f32[2,32]{0,1:T(8,128)S(1)}, u32[]{:S(2)}, u32[]{:S(2)}) collective-permute-start(f32[2,32]{0,1:T(8,128)S(1)} %get-tuple-element.160), channel_id=1, source_target_pairs={{0,1},{1,2},{2,3},{3,4},{4,5},{5,6},{6,7},{7,8},{8,9},{9,10},{10,1... | collective-permute-start | bytes 776 | tf_op jit(solution)/shard_map/ppermute | solution.py:15
  365.8 10.5 %collective-permute-start.11 = (f32[2,32]{0,1:T(8,128)S(1)}, f32[2,32]{0,1:T(8,128)S(1)}, u32[]{:S(2)}, u32[]{:S(2)}) collective-permute-start(f32[2,32]{0,1:T(8,128)S(1)} %get-tuple-element.159), channel_id=1, source_target_pairs={{1,0},{2,1},{3,2},{4,3},{5,4},{6,5},{7,6},{8,7},{9,8},{10,9},{11,1... | collective-permute-start | bytes 776 | tf_op jit(solution)/shard_map/ppermute | solution.py:17
where the time goes:
time: 379 us; the launch traced here: 377 us
  other arithmetic  142 us (37%)
  local copies, waits for them, and re-layouts  110 us (29%)
  starting transfers between devices  89.1 us (24%)
  waiting for transfers between devices  34 us (9%)
    ppermute x6, starting transfers between devices, with_halo(): lax.ppermute(head, axis, [((i + 1) % count, i) for i in range(ends)])  63 us
    scatter-add x3, other arithmetic, scatter_partial(): return total.at[:, local].add(jnp.transpose(parts, (1, 0, 2)))  52.3 us
    gather x3, other arithmetic, auxiliary_correction(): flat = owner * cap + entry - starts[owner]  42.5 us
    scatter-add x1, other arithmetic, auxiliary_correction(): jnp.zeros((2, aux_count), jnp.float32).at[:, aux_node]  33.5 us
    gather x6, local copies, waits for them, and re-layouts, gather_elements(): picked = jnp.transpose(extended[:, local], (1, 0, 2)) * signs  29.6 us
    gather x2, local copies, waits for them, and re-layouts, auxiliary_correction(): packed = jnp.where(filled[None, :, :], vals[:, positions], 0.0)  23.3 us
    gather x1, local copies, waits for them, and re-layouts, auxiliary_correction(): outgoing = solved[:, aux_node].reshape(2, peers, cap)  20.9 us
    all_to_all x1, waiting for transfers between devices, auxiliary_correction(): lax.all_to_all(packed, 'dom', split_axis=1, concat_axis=1, tiled=True)  15 us
  transfers between devices with their start and end apart: 14, of which 6 were waited for; matrix products, arithmetic and copies ran while one was open for 15% of the time, Pallas kernels for 0%

commit v1 on v0

v1 whole, which is shorter than its diff:
```python
import functools

import jax
import jax.numpy as jnp
from jax import lax
from jax.experimental import pallas as pl
from jax.experimental.pallas import tpu as pltpu
from jax.sharding import PartitionSpec as P

LANES = 128
VMEM_LIMIT = 24 * 2**20


def iota(shape, dim):
    return lax.broadcasted_iota(jnp.int32, shape, dim)


def edge_places(edges_ref, rim, width):
    places = []
    for k in range(3):
        coded = edges_ref[k : k + 1, :]
        flip = (1 - 2 * (coded & 1)).astype(jnp.float32)
        place = (coded >> 1) - rim
        place = jnp.where(place < 0, place + width, place)
        places.append((place >> 7, place & (LANES - 1), flip))
    return places


def gather_moments(table, inner, places):
    count = inner.shape[1]
    row = iota((8, LANES), 0)
    wide = iota((8, count), 0)
    total = jnp.concatenate([jnp.zeros((6, count), jnp.float32), inner], 0)
    for k, (high, low, flip) in enumerate(places):
        columns = []
        for at in range(0, count, LANES):
            low_b = jnp.broadcast_to(low[:, at : at + LANES], (8, LANES))
            high_b = jnp.broadcast_to(high[:, at : at + LANES], (8, LANES))
            found = jnp.zeros((8, LANES), jnp.float32)
            for g in range(table.shape[0] // 8):
                picked = jnp.take_along_axis(table[8 * g : 8 * g + 8], low_b, axis=1)
                found = found + jnp.where(high_b == 4 * g + (row >> 1), picked, 0.0)
            found = found + pltpu.roll(found, 4, 0)
            columns.append(found + pltpu.roll(found, 2, 0))
        found = jnp.concatenate(columns, 1)
        found = found * jnp.where(wide == 2 * k, flip, 1.0)
        total = jnp.where((wide >> 1) == k, found, total)
    return total


def scatter_moments(values, places, rows):
    count = values.shape[1]
    wide = iota((8, count), 0)
    tall = iota((LANES, count), 0)
    total = jnp.zeros((2 * rows, LANES), jnp.float32)
    for k, (high, low, flip) in enumerate(places):
        part = jnp.where((wide >> 1) == k, values, 0.0)
        part = part * jnp.where(wide == 2 * k, flip, 1.0)
        part = part + pltpu.roll(part, 4, 0)
        part = part + pltpu.roll(part, 2, 0)
        coarse = part.astype(jnp.bfloat16).astype(jnp.float32)
        spread = []
        for piece in (coarse, part - coarse):
            for g in range(rows // 8):
                spread.append(jnp.where(high == 4 * g + (wide >> 1), piece, 0.0))
        spread = jnp.concatenate(spread, 0).astype(jnp.bfloat16)
        hot = jnp.where(tall == low, 1.0, 0.0).astype(jnp.bfloat16)
        total = total + lax.dot_general(
            spread, hot, (((1,), (1,)), ((), ())), preferred_element_type=jnp.float32
        )
    return total[:rows] + total[rows:]


def apply_matrix(matrix_ref, live, u):
    y = matrix_ref[0] * u[0:1]
    for j in range(1, 8):
        y = y + matrix_ref[j] * u[j : j + 1]
    return y * live


def rim_row(from_left, from_right, rim):
    lane = iota(from_left.shape, 1)
    low = jnp.where(lane < rim, from_right, 0.0)
    return jnp.where((lane >= rim) & (lane < 2 * rim), pltpu.roll(from_left, 64, 1), low)


def settle(partial, last, from_left, from_right, rim):
    lane = iota((2, LANES), 1)
    head = partial[0:2] + jnp.where(lane < rim, from_left[2:4], 0.0)
    tail = partial[last : last + 2] + jnp.where(
        lane >= LANES - rim, pltpu.roll(from_right[2:4], 64, 1), 0.0
    )
    ends = partial[last + 2 : last + 4] + rim_row(from_left[0:2], from_right[0:2], rim)
    return head, tail, ends


def load_table(table_ref, edges, ends):
    blocks = edges.shape[1] // LANES
    for h in range(blocks):
        table_ref[2 * h : 2 * h + 2, :] = edges[:, h * LANES : (h + 1) * LANES]
    table_ref[2 * blocks : 2 * blocks + 2, :] = ends
    rest = table_ref.shape[0] - 2 * blocks - 2
    table_ref[2 * blocks + 2 :, :] = jnp.zeros((rest, LANES), jnp.float32)


def residual_kernel(
    rim, x_ref, inner_ref, left_ref, right_ref, edges_ref, live_ref, matrix_ref,
    y_ref, y_inner_ref, to_left_ref, to_right_ref, table_ref,
):
    rows = table_ref.shape[0]
    edge_count = x_ref.shape[1]
    last = 2 * (edge_count // LANES) - 2
    load_table(table_ref, x_ref[...], rim_row(left_ref[0:2], right_ref[0:2], rim))
    places = edge_places(edges_ref, rim, edge_count + 2 * rim)
    live = live_ref[...].astype(jnp.float32)
    u = gather_moments(table_ref[...], inner_ref[...], places)
    y = apply_matrix(matrix_ref, live, u)
    y_inner_ref[...] = y[6:8]
    y_ref[...] = scatter_moments(y, places, rows)
    to_right_ref[...] = y_ref[last : last + 4, :]
    to_left_ref[0:2, :] = y_ref[0:2, :]
    to_left_ref[2:4, :] = y_ref[last + 2 : last + 4, :]


def restrict_kernel(
    rim, y_ref, y_inner_ref, b_ref, b_inner_ref, left_ref, right_ref, from_left_ref,
    from_right_ref, edges_ref, live_ref, projection_ref, counts_ref,
    r_ref, r_inner_ref, packed_ref, vals_ref,
):
    edge_count = b_ref.shape[1]
    count = b_inner_ref.shape[1]
    last = 2 * (edge_count // LANES) - 2
    head, tail, ends = settle(y_ref, last, from_left_ref[...], from_right_ref[...], rim)
    exists = rim_row(left_ref[6:8], right_ref[6:8], rim)
    load_table(r_ref, b_ref[...], rim_row(left_ref[2:4], right_ref[2:4], rim))
    r_ref[0:2, :] = r_ref[0:2, :] - head
    r_ref[2:last, :] = r_ref[2:last, :] - y_ref[2:last, :]
    r_ref[last : last + 2, :] = r_ref[last : last + 2, :] - tail
    r_ref[last + 2 : last + 4, :] = exists * (r_ref[last + 2 : last + 4, :] - ends)
    r_inner = b_inner_ref[...] - y_inner_ref[...]
    r_inner_ref[...] = r_inner
    places = edge_places(edges_ref, rim, edge_count + 2 * rim)
    live = live_ref[...].astype(jnp.float32)
    u = gather_moments(r_ref[...], r_inner, places)
    a = projection_ref[0] * u[0:1]
    for m in range(1, 8):
        a = a + projection_ref[m] * u[m : m + 1]
    a = a * live
    for k in range(3):
        vals_ref[:, k * count : (k + 1) * count] = a[2 * k : 2 * k + 2]
    vals_ref[:, 3 * count :] = jnp.zeros((2, LANES), jnp.float32)
    lane = iota((2, LANES), 1)
    start = jnp.int32(0)
    for q in range(packed_ref.shape[0]):
        amount = counts_ref[0, q]
        shift = start & (LANES - 1)
        base = pl.multiple_of(start - shift, LANES)
        back = (LANES - shift) & (LANES - 1)
        first = pltpu.roll(vals_ref[:, pl.ds(base, LANES)], back, 1)
        second = pltpu.roll(vals_ref[:, pl.ds(base + LANES, LANES)], back, 1)
        chosen = jnp.where(lane < LANES - shift, first, second)
        packed_ref[q] = jnp.where(lane < amount, chosen, 0.0)
        start = start + amount


def solve_kernel(arrived_ref, nodes_ref, inverse_ref, out_ref):
    peers = arrived_ref.shape[0]
    groups = inverse_ref.shape[0]
    agg = inverse_ref.shape[1] // 2
    row = iota((8, LANES), 0)
    tall = iota((agg, LANES), 0)
    nodes = nodes_ref[...]
    block, place = nodes >> 6, nodes & (agg - 1)
    total = jnp.zeros((16, agg), jnp.float32)
    span = 16
    for first in range(0, peers, span):
        coarse_parts, fine_parts, hots = [], [], []
        for d in range(first, first + span):
            value = jnp.where(
                row < 4,
                jnp.broadcast_to(arrived_ref[d, 0:1, :], (8, LANES)),
                jnp.broadcast_to(arrived_ref[d, 1:2, :], (8, LANES)),
            )
            value = jnp.where((row & 3) == block[d : d + 1], value, 0.0)
            coarse = value.astype(jnp.bfloat16).astype(jnp.float32)
            coarse_parts.append(coarse)
            fine_parts.append(value - coarse)
            hots.append(jnp.where(tall == place[d : d + 1], 1.0, 0.0))
        spread = jnp.concatenate(
            [jnp.concatenate(coarse_parts, 1), jnp.concatenate(fine_parts, 1)], 0
        ).astype(jnp.bfloat16)
        hot = jnp.concatenate(hots, 1).astype(jnp.bfloat16)
        total = total + lax.dot_general(
            spread, hot, (((1,), (1,)), ((), ())), preferred_element_type=jnp.float32
        )
    g = total[:8] + total[8:]
    vectors = jnp.concatenate([g, pltpu.roll(g, 4, 0)], 1)
    table = jnp.zeros((8, LANES), jnp.float32)
    for b in range(groups):
        h = lax.dot_general(
            vectors, inverse_ref[b], (((1,), (0,)), ((), ())),
            precision=lax.Precision.HIGHEST, preferred_element_type=jnp.float32,
        )[b : b + 1]
        h = jnp.broadcast_to(h, (8, LANES))
        table = jnp.where(row == 2 * b, h, table)
        table = jnp.where(row == 2 * b + 1, pltpu.roll(h, agg, 1), table)
    for d in range(peers):
        low = jnp.broadcast_to(place[d : d + 1], (8, LANES))
        found = jnp.take_along_axis(table, low, axis=1)
        found = jnp.where((row >> 1) == block[d : d + 1], found, 0.0)
        found = found + pltpu.roll(found, 4, 0)
        found = found + pltpu.roll(found, 2, 0)
        out_ref[d] = found[0:2]


def prolong_kernel(
    rim, edge_count, returned_ref, edges_ref, live_ref, projection_ref, counts_ref,
    p_ref, p_inner_ref, to_left_ref, to_right_ref, vals_ref,
):
    rows = p_ref.shape[0]
    count = live_ref.shape[1]
    last = 2 * (edge_count // LANES) - 2
    lane = iota((2, LANES), 1)
    start = jnp.int32(0)
    for q in range(returned_ref.shape[0]):
        shift = start & (LANES - 1)
        base = pl.multiple_of(start - shift, LANES)
        moved = pltpu.roll(returned_ref[q], shift, 1)
        here = pl.ds(base, LANES)
        vals_ref[:, here] = jnp.where(lane >= shift, moved, vals_ref[:, here])
        vals_ref[:, pl.ds(base + LANES, LANES)] = moved
        start = start + counts_ref[0, q]
    nodal = jnp.concatenate([vals_ref[:, k * count : (k + 1) * count] for k in range(3)], 0)
    live = live_ref[...].astype(jnp.float32)
    p = [jnp.sum(projection_ref[m] * nodal, axis=0, keepdims=True) for m in range(8)]
    p = jnp.concatenate(p, 0) * live
    places = edge_places(edges_ref, rim, edge_count + 2 * rim)
    p_inner_ref[...] = p[6:8]
    p_ref[...] = scatter_moments(p, places, rows)
    to_right_ref[...] = p_ref[last : last + 4, :]
    to_left_ref[0:2, :] = p_ref[0:2, :]
    to_left_ref[2:4, :] = p_ref[last + 2 : last + 4, :]


def update_kernel(
    rim, p_ref, p_inner_ref, r_ref, r_inner_ref, x_ref, inner_ref, w_ref, w_inner_ref,
    left_ref, right_ref, from_left_ref, from_right_ref, edges_ref, live_ref, matrix_ref,
    x1_ref, x1_inner_ref, r1_ref, r1_inner_ref, ends_ref, table_ref,
):
    rows = table_ref.shape[0]
    edge_count = x_ref.shape[1]
    blocks = edge_count // LANES
    last = 2 * blocks - 2
    head, tail, ends = settle(p_ref, last, from_left_ref[...], from_right_ref[...], rim)
    exists = rim_row(left_ref[6:8], right_ref[6:8], rim)
    load_table(table_ref, w_ref[...], rim_row(left_ref[4:6], right_ref[4:6], rim))
    table_ref[...] = table_ref[...] * r_ref[...]
    table_ref[0:2, :] = table_ref[0:2, :] + head
    table_ref[2:last, :] = table_ref[2:last, :] + p_ref[2:last, :]
    table_ref[last : last + 2, :] = table_ref[last : last + 2, :] + tail
    table_ref[last + 2 : last + 4, :] = exists * (table_ref[last + 2 : last + 4, :] + ends)
    z_inner = w_inner_ref[...] * r_inner_ref[...] + p_inner_ref[...]
    for h in range(blocks):
        here = slice(h * LANES, (h + 1) * LANES)
        x1_ref[:, here] = x_ref[:, here] + table_ref[2 * h : 2 * h + 2, :]
    x1_inner_ref[...] = inner_ref[...] + z_inner
    places = edge_places(edges_ref, rim, edge_count + 2 * rim)
    live = live_ref[...].astype(jnp.float32)
    u = gather_moments(table_ref[...], z_inner, places)
    y = apply_matrix(matrix_ref, live, u)
    r1_inner_ref[...] = r_inner_ref[...] - y[6:8]
    table_ref[...] = scatter_moments(y, places, rows)
    for h in range(blocks):
        r1_ref[:, h * LANES : (h + 1) * LANES] = (
            r_ref[2 * h : 2 * h + 2, :] - table_ref[2 * h : 2 * h + 2, :]
        )
    ends_ref[...] = table_ref[last + 2 : last + 4, :]


def finish_kernel(rim, partial_ref, from_left_ref, from_right_ref, r1_ref):
    edge_count = partial_ref.shape[1]
    lane = iota((2, LANES), 1)
    r1_ref[...] = partial_ref[...]
    r1_ref[:, :LANES] = partial_ref[:, :LANES] - jnp.where(lane < rim, from_left_ref[...], 0.0)
    r1_ref[:, edge_count - LANES :] = partial_ref[:, edge_count - LANES :] - jnp.where(
        lane >= LANES - rim, pltpu.roll(from_right_ref[...], 64, 1), 0.0
    )


def local_call(kernel, outs, in_smem=(), scratch=(), name=None):
    def call(*args):
        specs = [
            pl.BlockSpec(memory_space=pltpu.SMEM if i in in_smem else pltpu.VMEM)
            for i in range(len(args))
        ]
        shapes = [jax.ShapeDtypeStruct(s, jnp.float32) for s in outs]
        return pl.pallas_call(
            kernel,
            out_shape=shapes,
            in_specs=specs,
            out_specs=[pl.BlockSpec(memory_space=pltpu.VMEM)] * len(outs),
            scratch_shapes=[pltpu.VMEM(s, jnp.float32) for s in scratch],
            compiler_params=pltpu.CompilerParams(vmem_limit_bytes=VMEM_LIMIT),
            name=name,
        )(*args)

    return call


def neighbours(to_left, to_right):
    axis = ("grp", "dom")
    ends = lax.axis_size(axis) - 1
    from_left = lax.ppermute(to_right, axis, [(i, i + 1) for i in range(ends)])
    from_right = lax.ppermute(to_left, axis, [(i + 1, i) for i in range(ends)])
    return from_left, from_right


def shards(
    x_edges,
    x_inner,
    b_edges,
    b_inner,
    w_edges,
    w_inner,
    elem_edges,
    element_live,
    elem_matrix,
    projection,
    owner_counts,
    aux_node,
    aux_inverse,
):
    edge_count = x_edges.shape[1]
    elem_count = x_inner.shape[1]
    rim = elem_count // 32
    peers = owner_counts.shape[1]
    cap = aux_node.shape[0] // peers
    rows = -(-2 * (edge_count // LANES + 1) // 8) * 8
    live = element_live.reshape(1, elem_count)
    ones = jnp.ones((2, LANES), jnp.float32)
    fields = (x_edges, b_edges, w_edges)
    heads = jnp.concatenate([f[:, :LANES] for f in fields] + [ones], 0)
    tails = jnp.concatenate([f[:, edge_count - LANES :] for f in fields] + [ones], 0)
    left, right = neighbours(heads, tails)
    nodes = jnp.pad(aux_node.reshape(peers, cap), ((0, 0), (0, LANES - cap)))
    table = (rows, LANES)
    inner = (2, elem_count)
    message = (4, LANES)
    slots = (peers, 2, LANES)

    y, y_inner, to_left, to_right = local_call(
        functools.partial(residual_kernel, rim), [table, inner, message, message],
        scratch=[table], name="residual",
    )(x_edges, x_inner, left, right, elem_edges, live, elem_matrix)
    from_left, from_right = neighbours(to_left, to_right)
    r, r_inner, packed = local_call(
        functools.partial(restrict_kernel, rim), [table, inner, slots], in_smem=(11,),
        scratch=[(2, 3 * elem_count + LANES)], name="restrict",
    )(
        y, y_inner, b_edges, b_inner, left, right, from_left, from_right, elem_edges, live,
        projection, owner_counts,
    )
    arrived = lax.all_to_all(packed, "dom", split_axis=0, concat_axis=0, tiled=True)
    (outgoing,) = local_call(solve_kernel, [slots], name="solve")(arrived, nodes, aux_inverse)
    returned = lax.all_to_all(outgoing, "dom", split_axis=0, concat_axis=0, tiled=True)
    p, p_inner, to_left, to_right = local_call(
        functools.partial(prolong_kernel, rim, edge_count), [table, inner, message, message],
        in_smem=(4,), scratch=[(2, 3 * elem_count + LANES)], name="prolong",
    )(returned, elem_edges, live, projection, owner_counts)
    from_left, from_right = neighbours(to_left, to_right)
    x1_edges, x1_inner, r1_part, r1_inner, ends = local_call(
        functools.partial(update_kernel, rim),
        [x_edges.shape, inner, x_edges.shape, inner, (2, LANES)],
        scratch=[table], name="update",
    )(
        p, p_inner, r, r_inner, x_edges, x_inner, w_edges, w_inner, left, right, from_left,
        from_right, elem_edges, live, elem_matrix,
    )
    from_left, from_right = neighbours(ends, ends)
    (r1_edges,) = local_call(
        functools.partial(finish_kernel, rim), [x_edges.shape], name="finish"
    )(r1_part, from_left, from_right)
    return x1_edges, x1_inner, r1_edges, r1_inner


def solution(mesh):
    edges = P(None, ("grp", "dom"))
    in_specs = (edges,) * 7 + (
        P(("grp", "dom")),
        P(None, None, ("grp", "dom")),
        P(None, None, ("grp", "dom")),
        P(("grp", "dom"), None),
        P(("grp", "dom")),
        P(("grp", "dom"), None, None),
    )
    return jax.shard_map(
        shards, mesh=mesh, in_specs=in_specs, out_specs=(edges,) * 4, check_vma=False
    )
```

time: 379 us -> 116 us (0.31)
  other arithmetic: 142 us -> 0.07 us
  local copies, waits for them, and re-layouts: 110 us -> 3.37 us
  starting transfers between devices: 89.1 us -> 64.4 us
  blocking collectives: 0 us -> 19.1 us
  waiting for transfers between devices: 34 us -> 20.1 us
  Pallas kernels: 0 us -> 7.26 us
    scatter-add x10 -> x0, other arithmetic: 87.5 us -> none  [the longest x3 52.3 us: scatter_partial(): return total.at[:, local].add(jnp.transpose(parts, (1, 0, 2)))]
    gather x14 -> x0, local copies, waits for them, and re-layouts: 86.7 us -> none  [the longest x6 29.6 us: gather_elements(): picked = jnp.transpose(extended[:, local], (1, 0, 2)) * signs]
    gather x7 -> x0, other arithmetic: 42.5 us -> none  [the longest x3 42.5 us: auxiliary_correction(): flat = owner * cap + entry - starts[owner]]
    ppermute x12 -> x8, starting transfers between devices: 76.6 us -> 54.7 us  [the longest x4 45 us: neighbours(): from_right = lax.ppermute(to_left, axis, [(i + 1, i) for i in range(ends)])]
    all_to_all x0 -> x1, blocking collectives: none -> 19.1 us  [shards(): lax.all_to_all(outgoing, 'dom', split_axis=0, concat_axis=0, tiled=True)]
    all_to_all x2 -> x1, waiting for transfers between devices: 30.1 us -> 15.2 us  [shards(): lax.all_to_all(packed, 'dom', split_axis=0, concat_axis=0, tiled=True)]
    pallas_call x0 -> x6, Pallas kernels: none -> 7.26 us  [call(): pl.pallas_call(kernel, out_shape=shapes, in_specs=specs, out_specs=[pl.Bl...]
    reshape x13 -> x1, local copies, waits for them, and re-layouts: 6.19 us -> 0.07 us  [shards(): nodes = jnp.pad(aux_node.reshape(peers, cap), ((0, 0), (0, LANES - cap)))]
  transfers between devices with their start and end apart: 14 -> 9, of which waited for: 6 -> 5; matrix products, arithmetic and copies ran while one was open for 15% -> 0% of each run, Pallas kernels for 0% -> 0%
where the time goes in v1:
time: 116 us; the launch traced here: 115 us
  starting transfers between devices  64.4 us (56%)
  waiting for transfers between devices  20.1 us (17%)
  blocking collectives  19.1 us (16%)
  Pallas kernels  7.26 us (6%)
  local copies, waits for them, and re-layouts  3.37 us (3%)
    ppermute x4, starting transfers between devices, neighbours(): from_right = lax.ppermute(to_left, axis, [(i + 1, i) for i in range(ends)])  45 us
    all_to_all x1, blocking collectives, shards(): lax.all_to_all(outgoing, 'dom', split_axis=0, concat_axis=0, tiled=True)  19.1 us
    all_to_all x1, waiting for transfers between devices, shards(): lax.all_to_all(packed, 'dom', split_axis=0, concat_axis=0, tiled=True)  15.2 us
    ppermute x4, starting transfers between devices, neighbours(): from_left = lax.ppermute(to_right, axis, [(i, i + 1) for i in range(ends)])  9.74 us
    all_to_all x1, starting transfers between devices, shards(): lax.all_to_all(packed, 'dom', split_axis=0, concat_axis=0, tiled=True)  9.68 us
    pallas_call x6, Pallas kernels, call(): pl.pallas_call(kernel, out_shape=shapes, in_specs=specs, out_specs=[pl.Bl...  7.26 us
    ppermute x4, waiting for transfers between devices, neighbours(): from_right = lax.ppermute(to_left, axis, [(i + 1, i) for i in range(ends)])  4.95 us
  transfers between devices with their start and end apart: 9, of which 5 were waited for; matrix products, arithmetic and copies ran while one was open for 0% of the time, Pallas kernels for 0%

profile of v1, /device:TPU:32, one launch (start us, length us, event | category | flops | bytes accessed | tf_op | source)
XLA Modules:
  0.0 115.2 jit_solution(10070043117638309245)
XLA Ops:
  0.6 0.7 fusion.2
  1.3 0.7 fusion
  2.1 0.1 pad.12.clone
  2.2 0.1 maximum_maximum_fusion.1
  2.2 3.5 %collective-permute-start = (f32[8,128]{1,0:T(8,128)S(1)}, f32[8,128]{1,0:T(8,128)S(1)}, u32[]{:S(2)}, u32[]{:S(2)}) collective-permute-start(f32[8,128]{1,0:T(8,128)S(1)} %get-tuple-element.43), channel_id=1, source_target_pairs={{0,1},{1,2},{2,3},{3,4},{4,5},{5,6},{6,7},{7,8},{8,9},{9,10},{10,1... | collective-permute-start | bytes 12296 | tf_op jit(solution)/shard_map/ppermute | solution.py:313
  5.8 18.3 %collective-permute-start.1 = (f32[8,128]{1,0:T(8,128)S(1)}, f32[8,128]{1,0:T(8,128)S(1)}, u32[]{:S(2)}, u32[]{:S(2)}) collective-permute-start(f32[8,128]{1,0:T(8,128)S(1)} %get-tuple-element.42), channel_id=1, source_target_pairs={{1,0},{2,1},{3,2},{4,3},{5,4},{6,5},{7,6},{8,7},{9,8},{10,9},{11,1... | collective-permute-start | bytes 12296 | tf_op jit(solution)/shard_map/ppermute | solution.py:314
  24.0 0.0 collective-permute-done.left_ref
  24.0 1.3 %collective-permute-done.1.right_ref = f32[8,128]{1,0:T(8,128)S(1)} collective-permute-done((f32[8,128]{1,0:T(8,128)S(1)}, f32[8,128]{1,0:T(8,128)S(1)}, u32[]{:S(2)}, u32[]{:S(2)}) %collective-permute-start.1) | collective-permute-done | bytes 4128 | tf_op jit(solution)/shard_map/ppermute | solution.py:314
  25.3 0.0 copy-done.6
  25.3 0.0 copy-done.5
  25.3 0.0 copy-done.3
  25.3 0.0 copy-done.4
  25.4 0.0 copy-start
  25.4 0.9 copy-done
  26.3 0.7 residual.1
  27.0 1.9 %collective-permute-start.2 = (f32[4,128]{1,0:T(4,128)S(1)}, f32[4,128]{1,0:T(4,128)S(1)}, u32[]{:S(2)}, u32[]{:S(2)}) collective-permute-start(f32[4,128]{1,0:T(4,128)S(1)} %get-tuple-element.22), channel_id=1, source_target_pairs={{0,1},{1,2},{2,3},{3,4},{4,5},{5,6},{6,7},{7,8},{8,9},{9,10},{10,1... | collective-permute-start | bytes 6152 | tf_op jit(solution)/shard_map/ppermute | solution.py:313
  28.9 9.1 %collective-permute-start.3 = (f32[4,128]{1,0:T(4,128)S(1)}, f32[4,128]{1,0:T(4,128)S(1)}, u32[]{:S(2)}, u32[]{:S(2)}) collective-permute-start(f32[4,128]{1,0:T(4,128)S(1)} %get-tuple-element.23), channel_id=1, source_target_pairs={{1,0},{2,1},{3,2},{4,3},{5,4},{6,5},{7,6},{8,7},{9,8},{10,9},{11,1... | collective-permute-start | bytes 6152 | tf_op jit(solution)/shard_map/ppermute | solution.py:314
  38.0 0.0 copy-done.12
  38.0 0.0 copy-start.8
  38.0 0.0 copy-start.9
  38.0 0.1 copy.17.projection_ref
  38.1 0.0 collective-permute-done.2.from_left_ref
  38.2 1.1 collective-permute-done.3.from_right_ref
  39.3 0.0 copy-done.8
  39.3 0.0 copy-done.9
  39.3 0.6 copy-done.11
  39.9 1.8 %restrict.1 = (f32[32,128]{1,0:T(8,128)S(1)}, f32[2,1024]{1,0:T(2,128)S(1)}, f32[64,2,128]{2,1,0:T(2,128)}) custom-call(f32[32,128]{1,0:T(8,128)S(1)} %get-tuple-element.20.y_ref, f32[2,1024]{1,0:T(2,128)S(1)} %get-tuple-element.21.y_inner_ref, f32[2,1536]{1,0:T(2,128)S(1)} %copy-done.8, f32[2,1024]{1,0:T(2,128)S(1)} %copy-done.9, ...), custom_call_target="tpu_custom_call" | custom-call | tf_op jit(solution)/shard_map/restrict/pallas_call | solution.py:297
  41.7 9.7 %all-to-all-start = ((f32[64,2,128]{2,1,0:T(2,128)}), f32[64,2,128]{2,1,0:T(2,128)S(1)}, u32[]{:S(2)}, u32[]{:S(2)}) async-start(f32[64,2,128]{2,1,0:T(2,128)} %get-tuple-element.24), calls=%async_computation | async-start | bytes 131072 | tf_op jit(solution)/shard_map/all_to_all | solution.py:363
  51.4 0.0 copy-done.13
  51.4 0.1 reshape.15
  51.5 15.2 %all-to-all-done.arrived_ref = f32[64,2,128]{2,1,0:T(2,128)S(1)} async-done(((f32[64,2,128]{2,1,0:T(2,128)}), f32[64,2,128]{2,1,0:T(2,128)S(1)}, u32[]{:S(2)}, u32[]{:S(2)}) %all-to-all-start) | async-done | bytes 65568 | tf_op jit(solution)/shard_map/all_to_all | solution.py:363
  66.7 0.0 copy-done.2
  66.7 1.5 %solve.1 = f32[64,2,128]{2,1,0:T(2,128)S(1)} custom-call(f32[64,2,128]{2,1,0:T(2,128)S(1)} %all-to-all-done.arrived_ref, s32[64,128]{1,0:T(8,128)S(1)} %pad.4.nodes_ref, f32[4,128,128]{2,1,0:T(8,128)S(1)} %copy-done.2), custom_call_target="tpu_custom_call" | custom-call | tf_op jit(solution)/shard_map/solve/pallas_call | solution.py:297
  68.2 0.0 copy-start.1
  68.2 19.1 %all_to_all.10.returned_ref = f32[64,2,128]{2,1,0:T(2,128)S(1)} all-to-all(f32[64,2,128]{2,1,0:T(2,128)S(1)} %solve.1), channel_id=1, replica_groups=mesh['grp'=16,'dom'=64] {'dom'}, dimensions={0} | all-to-all | bytes 131072 | tf_op jit(solution)/shard_map/all_to_all | solution.py:365
  87.3 1.5 %prolong.1 = (f32[32,128]{1,0:T(8,128)S(1)}, f32[2,1024]{1,0:T(2,128)S(1)}, f32[4,128]{1,0:T(4,128)S(1)}, f32[4,128]{1,0:T(4,128)S(1)}) custom-call(f32[64,2,128]{2,1,0:T(2,128)S(1)} %all_to_all.10.returned_ref, s32[3,1024]{1,0:T(4,128)S(1)} %copy-done.3, s32[1,1024]{1,0:T(1,128)S(1)} %bitcast.3, f32[8,6,1024]{2,1,0:T(8,128)S(1)} %copy.17.projection_ref, ...), custom_call_target="tpu_custom_call" | custom-call | tf_op jit(solution)/shard_map/prolong/pallas_call | solution.py:297
  88.8 0.0 copy-start.10
  88.8 2.4 %collective-permute-start.4 = (f32[4,128]{1,0:T(4,128)S(1)}, f32[4,128]{1,0:T(4,128)S(1)}, u32[]{:S(2)}, u32[]{:S(2)}) collective-permute-start(f32[4,128]{1,0:T(4,128)S(1)} %get-tuple-element.29), channel_id=1, source_target_pairs={{0,1},{1,2},{2,3},{3,4},{4,5},{5,6},{6,7},{7,8},{8,9},{9,10},{10,1... | collective-permute-start | bytes 6152 | tf_op jit(solution)/shard_map/ppermute | solution.py:313
  91.2 8.6 %collective-permute-start.5 = (f32[4,128]{1,0:T(4,128)S(1)}, f32[4,128]{1,0:T(4,128)S(1)}, u32[]{:S(2)}, u32[]{:S(2)}) collective-permute-start(f32[4,128]{1,0:T(4,128)S(1)} %get-tuple-element.30), channel_id=1, source_target_pairs={{1,0},{2,1},{3,2},{4,3},{5,4},{6,5},{7,6},{8,7},{9,8},{10,9},{11,1... | collective-permute-start | bytes 6152 | tf_op jit(solution)/shard_map/ppermute | solution.py:314
  99.8 0.0 collective-permute-done.4.from_left_ref
  99.8 1.3 %collective-permute-done.5.from_right_ref = f32[4,128]{1,0:T(4,128)S(1)} collective-permute-done((f32[4,128]{1,0:T(4,128)S(1)}, f32[4,128]{1,0:T(4,128)S(1)}, u32[]{:S(2)}, u32[]{:S(2)}) %collective-permute-start.5) | collective-permute-done | bytes 2080 | tf_op jit(solution)/shard_map/ppermute | solution.py:314
  101.1 0.0 copy-done.10
  101.1 1.2 %update.1 = (f32[2,1536]{1,0:T(2,128)}, f32[2,1024]{1,0:T(2,128)}, f32[2,1536]{1,0:T(2,128)S(1)}, f32[2,1024]{1,0:T(2,128)}, f32[2,128]{1,0:T(2,128)S(1)}) custom-call(f32[32,128]{1,0:T(8,128)S(1)} %get-tuple-element.25.p_ref, f32[2,1024]{1,0:T(2,128)S(1)} %get-tuple-element.26.p_inner_ref, f32[32,128]{1,0:T(8,128)S(1)} %get-tuple-element.27.r_ref, ...), custom_call_target="tpu_custom_call" | custom-call | tf_op jit(solution)/shard_map/update/pallas_call | solution.py:297
  102.3 1.9 %collective-permute-start.6 = (f32[2,128]{1,0:T(2,128)S(1)}, f32[2,128]{1,0:T(2,128)S(1)}, u32[]{:S(2)}, u32[]{:S(2)}) collective-permute-start(f32[2,128]{1,0:T(2,128)S(1)} %get-tuple-element.34), channel_id=1, source_target_pairs={{0,1},{1,2},{2,3},{3,4},{4,5},{5,6},{6,7},{7,8},{8,9},{9,10},{10,1... | collective-permute-start | bytes 3080 | tf_op jit(solution)/shard_map/ppermute | solution.py:313
  104.2 9.1 %collective-permute-start.7 = (f32[2,128]{1,0:T(2,128)S(1)}, f32[2,128]{1,0:T(2,128)S(1)}, u32[]{:S(2)}, u32[]{:S(2)}) collective-permute-start(f32[2,128]{1,0:T(2,128)S(1)} %get-tuple-element.34), channel_id=1, source_target_pairs={{1,0},{2,1},{3,2},{4,3},{5,4},{6,5},{7,6},{8,7},{9,8},{10,9},{11,1... | collective-permute-start | bytes 3080 | tf_op jit(solution)/shard_map/ppermute | solution.py:314
  113.3 0.0 collective-permute-done.6.from_left_ref
  113.3 1.3 %collective-permute-done.7.from_right_ref = f32[2,128]{1,0:T(2,128)S(1)} collective-permute-done((f32[2,128]{1,0:T(2,128)S(1)}, f32[2,128]{1,0:T(2,128)S(1)}, u32[]{:S(2)}, u32[]{:S(2)}) %collective-permute-start.7) | collective-permute-done | bytes 1056 | tf_op jit(solution)/shard_map/ppermute | solution.py:314
  114.5 0.7 finish.1
  (13 shorter events, 0.0 us)
Async XLA Ops:
  1.3 24.0 %copy-start.6 = (f32[2,1024]{1,0:T(2,128)S(1)}, f32[2,1024]{1,0:T(2,128)}, u32[]{:S(2)}) copy-start(f32[2,1024]{1,0:T(2,128)} %inner_ref.3) | copy-start | bytes 24580
  2.1 23.3 %copy-start.5 = (f32[2,1536]{1,0:T(2,128)S(1)}, f32[2,1536]{1,0:T(2,128)}, u32[]{:S(2)}) copy-start(f32[2,1536]{1,0:T(2,128)} %x_ref.3) | copy-start | bytes 36868
  2.2 23.2 %copy-start.3 = (s32[3,1024]{1,0:T(4,128)S(1)}, s32[3,1024]{1,0:T(4,128)}, u32[]{:S(2)}) copy-start(s32[3,1024]{1,0:T(4,128)} %edges_ref.7) | copy-start | bytes 36868
  2.2 23.1 %copy-start.4 = (s32[1024]{0:T(1024)S(1)}, s32[1024]{0:T(1024)}, u32[]{:S(2)}) copy-start(s32[1024]{0:T(1024)} %param.20) | copy-start | bytes 12292
  2.2 21.8 %collective-permute-start = (f32[8,128]{1,0:T(8,128)S(1)}, f32[8,128]{1,0:T(8,128)S(1)}, u32[]{:S(2)}, u32[]{:S(2)}) collective-permute-start(f32[8,128]{1,0:T(8,128)S(1)} %get-tuple-element.43), channel_id=1, source_target_pairs={{0,1},{1,2},{2,3},{3,4},{4,5},{5,6},{6,7},{7,8},{8,9},{9,10},{10,1... | collective-permute-start | bytes 12296 | tf_op jit(solution)/shard_map/ppermute | solution.py:313
  5.8 19.6 %collective-permute-start.1 = (f32[8,128]{1,0:T(8,128)S(1)}, f32[8,128]{1,0:T(8,128)S(1)}, u32[]{:S(2)}, u32[]{:S(2)}) collective-permute-start(f32[8,128]{1,0:T(8,128)S(1)} %get-tuple-element.42), channel_id=1, source_target_pairs={{1,0},{2,1},{3,2},{4,3},{5,4},{6,5},{7,6},{8,7},{9,8},{10,9},{11,1... | collective-permute-start | bytes 12296 | tf_op jit(solution)/shard_map/ppermute | solution.py:314
  25.4 1.0 copy-start
  26.3 11.7 %copy-start.12 = (f32[8,6,1024]{2,0,1:T(8,128)S(1)}, f32[8,6,1024]{2,0,1:T(8,128)}, u32[]{:S(2)}) copy-start(f32[8,6,1024]{2,0,1:T(8,128)} %param.22) | copy-start | bytes 589828
  27.0 11.2 %collective-permute-start.2 = (f32[4,128]{1,0:T(4,128)S(1)}, f32[4,128]{1,0:T(4,128)S(1)}, u32[]{:S(2)}, u32[]{:S(2)}) collective-permute-start(f32[4,128]{1,0:T(4,128)S(1)} %get-tuple-element.22), channel_id=1, source_target_pairs={{0,1},{1,2},{2,3},{3,4},{4,5},{5,6},{6,7},{7,8},{8,9},{9,10},{10,1... | collective-permute-start | bytes 6152 | tf_op jit(solution)/shard_map/ppermute | solution.py:313
  28.9 10.4 %collective-permute-start.3 = (f32[4,128]{1,0:T(4,128)S(1)}, f32[4,128]{1,0:T(4,128)S(1)}, u32[]{:S(2)}, u32[]{:S(2)}) collective-permute-start(f32[4,128]{1,0:T(4,128)S(1)} %get-tuple-element.23), channel_id=1, source_target_pairs={{1,0},{2,1},{3,2},{4,3},{5,4},{6,5},{7,6},{8,7},{9,8},{10,9},{11,1... | collective-permute-start | bytes 6152 | tf_op jit(solution)/shard_map/ppermute | solution.py:314
  38.0 1.3 %copy-start.8 = (f32[2,1536]{1,0:T(2,128)S(1)}, f32[2,1536]{1,0:T(2,128)}, u32[]{:S(2)}) copy-start(f32[2,1536]{1,0:T(2,128)} %b_ref.1) | copy-start | bytes 36868
  38.0 1.3 %copy-start.9 = (f32[2,1024]{1,0:T(2,128)S(1)}, f32[2,1024]{1,0:T(2,128)}, u32[]{:S(2)}) copy-start(f32[2,1024]{1,0:T(2,128)} %b_inner_ref.1) | copy-start | bytes 24580
  39.3 0.7 copy-start.11
  39.9 26.8 %copy-start.2 = (f32[4,128,128]{2,1,0:T(8,128)S(1)}, f32[4,128,128]{2,1,0:T(8,128)}, u32[]{:S(2)}) copy-start(f32[4,128,128]{2,1,0:T(8,128)} %inverse_ref.1) | copy-start | bytes 786436
  41.7 9.7 %copy-start.13 = (s32[6144]{0:T(1024)S(1)}, s32[6144]{0:T(1024)}, u32[]{:S(2)}) copy-start(s32[6144]{0:T(1024)} %param.24) | copy-start | bytes 73732
  41.7 25.0 %all-to-all-start = ((f32[64,2,128]{2,1,0:T(2,128)}), f32[64,2,128]{2,1,0:T(2,128)S(1)}, u32[]{:S(2)}, u32[]{:S(2)}) async-start(f32[64,2,128]{2,1,0:T(2,128)} %get-tuple-element.24), calls=%async_computation | async-start | bytes 131072 | tf_op jit(solution)/shard_map/all_to_all | solution.py:363
  68.2 32.9 %copy-start.1 = (f32[8,8,1024]{2,1,0:T(8,128)S(1)}, f32[8,8,1024]{2,1,0:T(8,128)}, u32[]{:S(2)}) copy-start(f32[8,8,1024]{2,1,0:T(8,128)} %matrix_ref.3) | copy-start | bytes 786436
  87.3 13.8 %copy-start.7 = (f32[2,1536]{1,0:T(2,128)S(1)}, f32[2,1536]{1,0:T(2,128)}, u32[]{:S(2)}) copy-start(f32[2,1536]{1,0:T(2,128)} %w_ref.1) | copy-start | bytes 36868
  88.8 12.3 %copy-start.10 = (f32[2,1024]{1,0:T(2,128)S(1)}, f32[2,1024]{1,0:T(2,128)}, u32[]{:S(2)}) copy-start(f32[2,1024]{1,0:T(2,128)} %w_inner_ref.1) | copy-start | bytes 24580
  88.8 11.0 %collective-permute-start.4 = (f32[4,128]{1,0:T(4,128)S(1)}, f32[4,128]{1,0:T(4,128)S(1)}, u32[]{:S(2)}, u32[]{:S(2)}) collective-permute-start(f32[4,128]{1,0:T(4,128)S(1)} %get-tuple-element.29), channel_id=1, source_target_pairs={{0,1},{1,2},{2,3},{3,4},{4,5},{5,6},{6,7},{7,8},{8,9},{9,10},{10,1... | collective-permute-start | bytes 6152 | tf_op jit(solution)/shard_map/ppermute | solution.py:313
  91.2 9.9 %collective-permute-start.5 = (f32[4,128]{1,0:T(4,128)S(1)}, f32[4,128]{1,0:T(4,128)S(1)}, u32[]{:S(2)}, u32[]{:S(2)}) collective-permute-start(f32[4,128]{1,0:T(4,128)S(1)} %get-tuple-element.30), channel_id=1, source_target_pairs={{1,0},{2,1},{3,2},{4,3},{5,4},{6,5},{7,6},{8,7},{9,8},{10,9},{11,1... | collective-permute-start | bytes 6152 | tf_op jit(solution)/shard_map/ppermute | solution.py:314
  102.3 11.0 %collective-permute-start.6 = (f32[2,128]{1,0:T(2,128)S(1)}, f32[2,128]{1,0:T(2,128)S(1)}, u32[]{:S(2)}, u32[]{:S(2)}) collective-permute-start(f32[2,128]{1,0:T(2,128)S(1)} %get-tuple-element.34), channel_id=1, source_target_pairs={{0,1},{1,2},{2,3},{3,4},{4,5},{5,6},{6,7},{7,8},{8,9},{9,10},{10,1... | collective-permute-start | bytes 3080 | tf_op jit(solution)/shard_map/ppermute | solution.py:313
  104.2 10.4 %collective-permute-start.7 = (f32[2,128]{1,0:T(2,128)S(1)}, f32[2,128]{1,0:T(2,128)S(1)}, u32[]{:S(2)}, u32[]{:S(2)}) collective-permute-start(f32[2,128]{1,0:T(2,128)S(1)} %get-tuple-element.34), channel_id=1, source_target_pairs={{1,0},{2,1},{3,2},{4,3},{5,4},{6,5},{7,6},{8,7},{9,8},{10,9},{11,1... | collective-permute-start | bytes 3080 | tf_op jit(solution)/shard_map/ppermute | solution.py:314

commit v2 on v1

v2 whole, which is shorter than its diff:
```python
import functools

import jax
import jax.numpy as jnp
from jax import lax
from jax.experimental import pallas as pl
from jax.experimental.pallas import tpu as pltpu
from jax.sharding import PartitionSpec as P

LANES = 128
VMEM_LIMIT = 24 * 2**20


def iota(shape, dim):
    return lax.broadcasted_iota(jnp.int32, shape, dim)


def edge_places(edges_ref, rim, width):
    places = []
    for k in range(3):
        coded = edges_ref[k : k + 1, :]
        flip = (1 - 2 * (coded & 1)).astype(jnp.float32)
        place = (coded >> 1) - rim
        place = jnp.where(place < 0, place + width, place)
        places.append((place >> 7, place & (LANES - 1), flip))
    return places


def row_highs(blocks):
    row = iota((8, LANES), 0)
    return [4 * g + (row >> 1) for g in range(-(-(blocks + 1) // 4))]


def end_highs(blocks):
    row = iota((8, LANES), 0)
    rims = jnp.where(row < 6, blocks, -1)
    return [jnp.where(row < 2, 0, jnp.where(row < 4, blocks - 1, rims))]


def widen(mask_rows, count):
    return jnp.concatenate([mask_rows] * (count // LANES), 1)


def gather_moments(groups, highs, inner, places):
    count = inner.shape[1]
    wide = iota((8, count), 0)
    total = jnp.concatenate([jnp.zeros((6, count), jnp.float32), inner], 0)
    for k, (high, low, flip) in enumerate(places):
        columns = []
        for at in range(0, count, LANES):
            low_b = jnp.broadcast_to(low[:, at : at + LANES], (8, LANES))
            high_b = jnp.broadcast_to(high[:, at : at + LANES], (8, LANES))
            found = jnp.zeros((8, LANES), jnp.float32)
            for group, at_high in zip(groups, highs):
                picked = jnp.take_along_axis(group, low_b, axis=1)
                found = found + jnp.where(high_b == at_high, picked, 0.0)
            found = found + pltpu.roll(found, 4, 0)
            columns.append(found + pltpu.roll(found, 2, 0))
        found = jnp.concatenate(columns, 1)
        found = found * jnp.where(wide == 2 * k, flip, 1.0)
        total = jnp.where((wide >> 1) == k, found, total)
    return total


def scatter_moments(values, places, hot_ref, highs):
    count = values.shape[1]
    rows = 8 * len(highs)
    wide = iota((8, count), 0)
    total = jnp.zeros((2 * rows, LANES), jnp.float32)
    for k, (high, low, flip) in enumerate(places):
        part = jnp.where((wide >> 1) == k, values, 0.0)
        part = part * jnp.where(wide == 2 * k, flip, 1.0)
        part = part + pltpu.roll(part, 4, 0)
        part = part + pltpu.roll(part, 2, 0)
        coarse = part.astype(jnp.bfloat16).astype(jnp.float32)
        spread = []
        for piece in (coarse, part - coarse):
            for at_high in highs:
                spread.append(jnp.where(high == widen(at_high, count), piece, 0.0))
        spread = jnp.concatenate(spread, 0).astype(jnp.bfloat16)
        total = total + lax.dot_general(
            spread, hot_ref[:, k * count : (k + 1) * count], (((1,), (1,)), ((), ())),
            preferred_element_type=jnp.float32,
        )
    return total[:rows] + total[rows:]


def apply_matrix(matrix_ref, live_ref, u):
    y = matrix_ref[0] * u[0:1]
    for j in range(1, 8):
        y = y + matrix_ref[j] * u[j : j + 1]
    return y * live_ref[...].astype(jnp.float32)


def restrict(projection_ref, live_ref, u):
    a = [jnp.sum(projection_ref[n] * u, axis=0, keepdims=True) for n in range(6)]
    return jnp.concatenate(a, 0) * live_ref[...].astype(jnp.float32)


def rim_row(from_left, from_right, rim):
    lane = iota(from_left.shape, 1)
    low = jnp.where(lane < rim, from_right, 0.0)
    return jnp.where((lane >= rim) & (lane < 2 * rim), pltpu.roll(from_left, 64, 1), low)


def arrivals(left, right, rim):
    lane = iota((2, LANES), 1)
    head = jnp.where(lane < rim, left, 0.0)
    return head, jnp.where(lane >= LANES - rim, pltpu.roll(right, 64, 1), 0.0)


def by_side(even_ref, via_odd, via_even):
    even = even_ref[0 : via_odd.shape[0], :] > 0.5
    return jnp.where(even, via_odd, via_even), jnp.where(even, via_even, via_odd)


def load_table(table_ref, edges_ref):
    blocks = edges_ref.shape[1] // LANES
    for h in range(blocks):
        table_ref[2 * h : 2 * h + 2, :] = edges_ref[:, h * LANES : (h + 1) * LANES]
    rest = table_ref.shape[0] - 2 * blocks
    table_ref[2 * blocks :, :] = jnp.zeros((rest, LANES), jnp.float32)


def table_groups(table_ref):
    return [table_ref[8 * g : 8 * g + 8, :] for g in range(table_ref.shape[0] // 8)]


def own_kernel(
    rim, x_ref, inner_ref, edges_ref, live_ref, matrix_ref, y_ref, hot_ref, table_ref
):
    edge_count = x_ref.shape[1]
    count = inner_ref.shape[1]
    load_table(table_ref, x_ref)
    places = edge_places(edges_ref, rim, edge_count + 2 * rim)
    tall = iota((LANES, count), 0)
    for k, (_, low, _) in enumerate(places):
        hot = jnp.where(tall == low, 1.0, 0.0).astype(jnp.bfloat16)
        hot_ref[:, k * count : (k + 1) * count] = hot
    highs = row_highs(edge_count // LANES)
    u = gather_moments(table_groups(table_ref), highs, inner_ref[...], places)
    y_ref[...] = apply_matrix(matrix_ref, live_ref, u)


def residual_kernel(
    rim, even_ref, via_odd_ref, via_even_ref, own_ref, b_ref, w_ref, edges_ref, live_ref,
    matrix_ref, hot_ref, y_ref, ends_ref, exists_ref, odd_ref, even_out_ref,
):
    edge_count = b_ref.shape[1]
    blocks = edge_count // LANES
    count = own_ref.shape[1]
    left, right = by_side(even_ref, via_odd_ref[...], via_even_ref[...])
    exists_ref[...] = rim_row(left[2:4], right[2:4], rim)
    none = jnp.zeros((2, LANES), jnp.float32)
    change = jnp.concatenate([none, none, rim_row(left[0:2], right[0:2], rim), none], 0)
    places = edge_places(edges_ref, rim, edge_count + 2 * rim)
    highs = end_highs(blocks)
    u = gather_moments([change], highs, jnp.zeros((2, count), jnp.float32), places)
    y = own_ref[...] + apply_matrix(matrix_ref, live_ref, u)
    y_ref[...] = y
    ends = scatter_moments(y, places, hot_ref, highs)
    ends_ref[...] = ends
    tail = slice(edge_count - LANES, edge_count)
    to_left = jnp.concatenate([ends[0:2], ends[4:6], b_ref[:, :LANES], w_ref[:, :LANES]], 0)
    to_right = jnp.concatenate([ends[2:4], ends[4:6], b_ref[:, tail], w_ref[:, tail]], 0)
    odd_ref[...], even_out_ref[...] = by_side(even_ref, to_left, to_right)


def partial_kernel(
    rim, y_ref, b_ref, b_inner_ref, edges_ref, live_ref, projection_ref, hot_ref,
    r_ref, r_inner_ref, a_ref,
):
    edge_count = b_ref.shape[1]
    blocks = edge_count // LANES
    places = edge_places(edges_ref, rim, edge_count + 2 * rim)
    highs = row_highs(blocks)
    load_table(r_ref, b_ref)
    total = scatter_moments(y_ref[...], places, hot_ref, highs)
    row = iota(total.shape, 0)
    r_ref[...] = r_ref[...] - jnp.where(row < 2 * blocks, total, 0.0)
    r_inner = b_inner_ref[...] - y_ref[6:8, :]
    r_inner_ref[...] = r_inner
    u = gather_moments(table_groups(r_ref), highs, r_inner, places)
    a_ref[...] = restrict(projection_ref, live_ref, u)


def restrict_kernel(
    rim, edge_count, even_ref, via_odd_ref, via_even_ref, ends_ref, exists_ref, part_ref, a_ref,
    edges_ref, live_ref, projection_ref, counts_ref, r_ref, s_rim_ref, packed_ref, vals_ref,
):
    blocks = edge_count // LANES
    count = a_ref.shape[1]
    left, right = by_side(even_ref, via_odd_ref[...], via_even_ref[...])
    head, tail = arrivals(left[2:4], right[2:4], rim)
    exists = exists_ref[...]
    settled = ends_ref[4:6, :] + rim_row(left[0:2], right[0:2], rim)
    r_rim = exists * (rim_row(left[4:6], right[4:6], rim) - settled)
    change = jnp.concatenate([-head, -tail, r_rim, jnp.zeros((2, LANES), jnp.float32)], 0)
    s_rim_ref[...] = rim_row(left[6:8], right[6:8], rim) * r_rim
    places = edge_places(edges_ref, rim, edge_count + 2 * rim)
    u = gather_moments(
        [change], end_highs(blocks), jnp.zeros((2, count), jnp.float32), places
    )
    a = a_ref[...] + restrict(projection_ref, live_ref, u)
    for k in range(3):
        vals_ref[:, k * count : (k + 1) * count] = a[2 * k : 2 * k + 2]
    vals_ref[:, 3 * count :] = jnp.zeros((2, LANES), jnp.float32)
    lane = iota((2, LANES), 1)
    start = jnp.int32(0)
    for q in range(packed_ref.shape[0]):
        amount = counts_ref[0, q]
        shift = start & (LANES - 1)
        base = pl.multiple_of(start - shift, LANES)
        back = (LANES - shift) & (LANES - 1)
        first = pltpu.roll(vals_ref[:, pl.ds(base, LANES)], back, 1)
        second = pltpu.roll(vals_ref[:, pl.ds(base + LANES, LANES)], back, 1)
        chosen = jnp.where(lane < LANES - shift, first, second)
        packed_ref[q] = jnp.where(lane < amount, chosen, 0.0)
        start = start + amount
    r_ref[...] = part_ref[...]
    last = 2 * blocks - 2
    r_ref[0:2, :] = r_ref[0:2, :] - head
    r_ref[last : last + 2, :] = r_ref[last : last + 2, :] - tail


def slots_kernel(nodes_ref, hot_ref):
    agg = hot_ref.shape[0]
    place = nodes_ref[...] & (agg - 1)
    tall = iota((agg, LANES), 0)
    for d in range(nodes_ref.shape[0]):
        hot = jnp.where(tall == place[d : d + 1], 1.0, 0.0).astype(jnp.bfloat16)
        hot_ref[:, d * LANES : (d + 1) * LANES] = hot


def solve_kernel(arrived_ref, nodes_ref, hot_ref, inverse_ref, out_ref):
    peers = arrived_ref.shape[0]
    groups = inverse_ref.shape[0]
    agg = inverse_ref.shape[1] // 2
    row = iota((8, LANES), 0)
    nodes = nodes_ref[...]
    block, place = nodes >> 6, nodes & (agg - 1)
    total = jnp.zeros((16, agg), jnp.float32)
    span = 16
    for first in range(0, peers, span):
        coarse_parts, fine_parts = [], []
        for d in range(first, first + span):
            value = jnp.where(
                row < 4,
                jnp.broadcast_to(arrived_ref[d, 0:1, :], (8, LANES)),
                jnp.broadcast_to(arrived_ref[d, 1:2, :], (8, LANES)),
            )
            value = jnp.where((row & 3) == block[d : d + 1], value, 0.0)
            coarse = value.astype(jnp.bfloat16).astype(jnp.float32)
            coarse_parts.append(coarse)
            fine_parts.append(value - coarse)
        spread = jnp.concatenate(
            [jnp.concatenate(coarse_parts, 1), jnp.concatenate(fine_parts, 1)], 0
        ).astype(jnp.bfloat16)
        hot = hot_ref[:, first * LANES : (first + span) * LANES]
        total = total + lax.dot_general(
            spread, hot, (((1,), (1,)), ((), ())), preferred_element_type=jnp.float32
        )
    g = total[:8] + total[8:]
    vectors = jnp.concatenate([g, pltpu.roll(g, 4, 0)], 1)
    table = jnp.zeros((8, LANES), jnp.float32)
    for b in range(groups):
        h = lax.dot_general(
            vectors, inverse_ref[b], (((1,), (0,)), ((), ())),
            precision=lax.Precision.HIGHEST, preferred_element_type=jnp.float32,
        )[b : b + 1]
        h = jnp.broadcast_to(h, (8, LANES))
        table = jnp.where(row == 2 * b, h, table)
        table = jnp.where(row == 2 * b + 1, pltpu.roll(h, agg, 1), table)
    for d in range(peers):
        low = jnp.broadcast_to(place[d : d + 1], (8, LANES))
        found = jnp.take_along_axis(table, low, axis=1)
        found = jnp.where((row >> 1) == block[d : d + 1], found, 0.0)
        found = found + pltpu.roll(found, 4, 0)
        found = found + pltpu.roll(found, 2, 0)
        out_ref[d] = found[0:2]


def prolong_kernel(
    rim, edge_count, even_ref, returned_ref, edges_ref, live_ref, projection_ref, counts_ref,
    hot_ref, p_ref, ends_ref, odd_ref, even_out_ref, vals_ref,
):
    count = live_ref.shape[1]
    lane = iota((2, LANES), 1)
    start = jnp.int32(0)
    for q in range(returned_ref.shape[0]):
        shift = start & (LANES - 1)
        base = pl.multiple_of(start - shift, LANES)
        moved = pltpu.roll(returned_ref[q], shift, 1)
        here = pl.ds(base, LANES)
        vals_ref[:, here] = jnp.where(lane >= shift, moved, vals_ref[:, here])
        vals_ref[:, pl.ds(base + LANES, LANES)] = moved
        start = start + counts_ref[0, q]
    nodal = jnp.concatenate([vals_ref[:, k * count : (k + 1) * count] for k in range(3)], 0)
    p = projection_ref[0] * nodal[0:1]
    for n in range(1, 6):
        p = p + projection_ref[n] * nodal[n : n + 1]
    p = p * live_ref[...].astype(jnp.float32)
    p_ref[...] = p
    places = edge_places(edges_ref, rim, edge_count + 2 * rim)
    ends = scatter_moments(p, places, hot_ref, end_highs(edge_count // LANES))
    ends_ref[...] = ends
    to_left = jnp.concatenate([ends[0:2], ends[4:6]], 0)
    to_right = jnp.concatenate([ends[2:4], ends[4:6]], 0)
    odd_ref[...], even_out_ref[...] = by_side(even_ref, to_left, to_right)


def smooth_kernel(
    rim, p_ref, r_ref, r_inner_ref, inner_ref, w_ref, w_inner_ref, edges_ref, live_ref,
    matrix_ref, hot_ref, z_ref, x1_inner_ref, y_ref,
):
    edge_count = w_ref.shape[1]
    blocks = edge_count // LANES
    places = edge_places(edges_ref, rim, edge_count + 2 * rim)
    highs = row_highs(blocks)
    total = scatter_moments(p_ref[...], places, hot_ref, highs)
    row = iota(total.shape, 0)
    load_table(z_ref, w_ref)
    z_ref[...] = z_ref[...] * r_ref[...] + jnp.where(row < 2 * blocks, total, 0.0)
    z_inner = w_inner_ref[...] * r_inner_ref[...] + p_ref[6:8, :]
    x1_inner_ref[...] = inner_ref[...] + z_inner
    u = gather_moments(table_groups(z_ref), highs, z_inner, places)
    y_ref[...] = apply_matrix(matrix_ref, live_ref, u)


def update_kernel(
    rim, edge_count, even_ref, via_odd_ref, via_even_ref, ends_ref, exists_ref, s_rim_ref,
    part_ref, edges_ref, live_ref, matrix_ref, hot_ref, y_ref, change_ref, rims_ref,
):
    count = part_ref.shape[1]
    left, right = by_side(even_ref, via_odd_ref[...], via_even_ref[...])
    head, tail = arrivals(left[2:4], right[2:4], rim)
    settled = ends_ref[4:6, :] + rim_row(left[0:2], right[0:2], rim)
    z_rim = s_rim_ref[...] + exists_ref[...] * settled
    change = jnp.concatenate([head, tail, z_rim, jnp.zeros((2, LANES), jnp.float32)], 0)
    change_ref[...] = change
    places = edge_places(edges_ref, rim, edge_count + 2 * rim)
    highs = end_highs(edge_count // LANES)
    u = gather_moments([change], highs, jnp.zeros((2, count), jnp.float32), places)
    y = part_ref[...] + apply_matrix(matrix_ref, live_ref, u)
    y_ref[...] = y
    rims_ref[...] = scatter_moments(y, places, hot_ref, highs)[4:6]


def output_kernel(
    rim, y_ref, change_ref, z_ref, r_ref, r_inner_ref, x_ref, edges_ref, hot_ref,
    x1_ref, r1_ref, r1_inner_ref,
):
    edge_count = x_ref.shape[1]
    blocks = edge_count // LANES
    places = edge_places(edges_ref, rim, edge_count + 2 * rim)
    total = scatter_moments(y_ref[...], places, hot_ref, row_highs(blocks))
    r1_inner_ref[...] = r_inner_ref[...] - y_ref[6:8, :]
    for h in range(blocks):
        here = slice(h * LANES, (h + 1) * LANES)
        rows = slice(2 * h, 2 * h + 2)
        z = z_ref[rows, :]
        if h == 0:
            z = z + change_ref[0:2, :]
        if h == blocks - 1:
            z = z + change_ref[2:4, :]
        x1_ref[:, here] = x_ref[:, here] + z
        r1_ref[:, here] = r_ref[rows, :] - total[rows]


def finish_kernel(rim, even_ref, part_ref, via_odd_ref, via_even_ref, r1_ref):
    edge_count = part_ref.shape[1]
    left, right = by_side(even_ref, via_odd_ref[...], via_even_ref[...])
    head, tail = arrivals(left, right, rim)
    last = slice(edge_count - LANES, edge_count)
    r1_ref[...] = part_ref[...]
    r1_ref[:, :LANES] = part_ref[:, :LANES] - head
    r1_ref[:, last] = part_ref[:, last] - tail


def local_call(kernel, outs, in_smem=(), scratch=(), name=None):
    def call(*args):
        specs = [
            pl.BlockSpec(memory_space=pltpu.SMEM if i in in_smem else pltpu.VMEM)
            for i in range(len(args))
        ]
        shapes = [jax.ShapeDtypeStruct(*(s if s[-1] == jnp.bfloat16 else (s, jnp.float32)))
                  for s in outs]
        return pl.pallas_call(
            kernel,
            out_shape=shapes,
            in_specs=specs,
            out_specs=[pl.BlockSpec(memory_space=pltpu.VMEM)] * len(outs),
            scratch_shapes=[pltpu.VMEM(s, jnp.float32) for s in scratch],
            compiler_params=pltpu.CompilerParams(vmem_limit_bytes=VMEM_LIMIT),
            cost_estimate=pl.CostEstimate(
                flops=10**8, bytes_accessed=2 * 10**6, transcendentals=0
            ),
            name=name,
        )(*args)

    return call


def swap(odd, even):
    axis = ("grp", "dom")
    count = lax.axis_size(axis)

    def pairs(first):
        lows = range(first, count - 1, 2)
        return [(i, i + 1) for i in lows] + [(i + 1, i) for i in lows]

    return lax.ppermute(odd, axis, pairs(1)), lax.ppermute(even, axis, pairs(0))


def shards(
    x_edges,
    x_inner,
    b_edges,
    b_inner,
    w_edges,
    w_inner,
    elem_edges,
    element_live,
    elem_matrix,
    projection,
    owner_counts,
    aux_node,
    aux_inverse,
):
    edge_count = x_edges.shape[1]
    elem_count = x_inner.shape[1]
    rim = elem_count // 32
    peers = owner_counts.shape[1]
    cap = aux_node.shape[0] // peers
    agg = aux_inverse.shape[1] // 2
    rows = -(-2 * (edge_count // LANES + 1) // 8) * 8
    live = element_live.reshape(1, elem_count)
    projection = jnp.transpose(projection, (1, 0, 2))
    is_even = lax.axis_index(("grp", "dom")) % 2 == 0
    even = jnp.where(is_even, jnp.ones((8, LANES), jnp.float32), 0.0)
    ones = jnp.ones((2, LANES), jnp.float32)
    x_head, x_tail = x_edges[:, :LANES], x_edges[:, edge_count - LANES :]
    via_odd, via_even = swap(
        jnp.concatenate([jnp.where(is_even, x_head, x_tail), ones], 0),
        jnp.concatenate([jnp.where(is_even, x_tail, x_head), ones], 0),
    )
    nodes = jnp.pad(aux_node.reshape(peers, cap), ((0, 0), (0, LANES - cap)))
    table = (rows, LANES)
    group = (8, LANES)
    inner = (2, elem_count)
    moments = (8, elem_count)
    slots = (peers, 2, LANES)
    hots = ((LANES, 3 * elem_count), jnp.bfloat16)
    lists = (2, 3 * elem_count + LANES)

    own, hot = local_call(
        functools.partial(own_kernel, rim), [moments, hots], scratch=[table], name="own"
    )(x_edges, x_inner, elem_edges, live, elem_matrix)
    y, ends, exists, odd_out, even_out = local_call(
        functools.partial(residual_kernel, rim), [moments, group, (2, LANES), group, group],
        name="residual",
    )(
        even, via_odd, via_even, own, b_edges, w_edges, elem_edges, live, elem_matrix, hot
    )
    via_odd, via_even = swap(odd_out, even_out)
    r, r_inner, a = local_call(
        functools.partial(partial_kernel, rim), [table, inner, (6, elem_count)], name="partial"
    )(y, b_edges, b_inner, elem_edges, live, projection, hot)
    r, s_rim, packed = local_call(
        functools.partial(restrict_kernel, rim, edge_count), [table, (2, LANES), slots],
        in_smem=(10,), scratch=[lists], name="restrict",
    )(
        even, via_odd, via_even, ends, exists, r, a, elem_edges, live, projection, owner_counts
    )
    arrived = lax.all_to_all(packed, "dom", split_axis=0, concat_axis=0, tiled=True)
    (slots_hot,) = local_call(
        slots_kernel, [((agg, peers * LANES), jnp.bfloat16)], name="slots"
    )(nodes)
    (outgoing,) = local_call(solve_kernel, [slots], name="solve")(
        arrived, nodes, slots_hot, aux_inverse
    )
    returned = lax.all_to_all(outgoing, "dom", split_axis=0, concat_axis=0, tiled=True)
    p, ends, odd_out, even_out = local_call(
        functools.partial(prolong_kernel, rim, edge_count),
        [moments, group, (4, LANES), (4, LANES)], in_smem=(5,), scratch=[lists], name="prolong",
    )(even, returned, elem_edges, live, projection, owner_counts, hot)
    via_odd, via_even = swap(odd_out, even_out)
    z, x1_inner, az = local_call(
        functools.partial(smooth_kernel, rim), [table, inner, moments], name="smooth"
    )(p, r, r_inner, x_inner, w_edges, w_inner, elem_edges, live, elem_matrix, hot)
    az, change, rims = local_call(
        functools.partial(update_kernel, rim, edge_count), [moments, group, (2, LANES)],
        name="update",
    )(
        even, via_odd, via_even, ends, exists, s_rim, az, elem_edges, live, elem_matrix, hot
    )
    via_odd, via_even = swap(rims, rims)
    x1_edges, r1_part, r1_inner = local_call(
        functools.partial(output_kernel, rim), [x_edges.shape, x_edges.shape, inner],
        name="output",
    )(az, change, z, r, r_inner, x_edges, elem_edges, hot)
    (r1_edges,) = local_call(
        functools.partial(finish_kernel, rim), [x_edges.shape], name="finish"
    )(even, r1_part, via_odd, via_even)
    return x1_edges, x1_inner, r1_edges, r1_inner


def solution(mesh):
    edges = P(None, ("grp", "dom"))
    in_specs = (edges,) * 7 + (
        P(("grp", "dom")),
        P(None, None, ("grp", "dom")),
        P(None, None, ("grp", "dom")),
        P(("grp", "dom"), None),
        P(("grp", "dom")),
        P(("grp", "dom"), None, None),
    )
    return jax.shard_map(
        shards, mesh=mesh, in_specs=in_specs, out_specs=(edges,) * 4, check_vma=False
    )
```

time: 116 us -> 108 us (0.931)
  starting transfers between devices: 64.4 us -> 47.7 us
  waiting for transfers between devices: 20.1 us -> 27.9 us
  Pallas kernels: 7.26 us -> 9.55 us
    ppermute x8, starting transfers between devices: 54.7 us -> 41 us  [the longest x4 31.9 us: swap(): lax.ppermute(odd, axis, pairs(1))]
    ppermute x8, waiting for transfers between devices: 4.96 us -> 13.1 us  [the longest x4 10.9 us: swap(): lax.ppermute(odd, axis, pairs(1))]
    all_to_all x1, starting transfers between devices: 9.68 us -> 6.66 us  [shards(): lax.all_to_all(packed, 'dom', split_axis=0, concat_axis=0, tiled=True)]
    pallas_call x6 -> x11, Pallas kernels: 7.26 us -> 9.55 us  [call(): pl.pallas_call(kernel, out_shape=shapes, in_specs=specs, out_specs=[pl.Bl...]
    slice x2 -> x0, local copies, waits for them, and re-layouts: 1.44 us -> none  [shards(): heads = jnp.concatenate([f[:, :LANES] for f in fields] + [ones], 0)]
    unnamed x29 -> x28, local copies, waits for them, and re-layouts: 1.77 us -> 2.33 us
  transfers between devices with their start and end apart: 9 -> 9, of which waited for: 5 -> 5; matrix products, arithmetic and copies ran while one was open for 0% -> 0% of each run, Pallas kernels for 0% -> 3%
where the time goes in v2:
time: 108 us; the launch traced here: 107 us
  starting transfers between devices  47.7 us (44%)
  waiting for transfers between devices  27.9 us (26%)
  blocking collectives  19 us (18%)
  Pallas kernels  9.55 us (9%)
  local copies, waits for them, and re-layouts  2.43 us (2%)
    ppermute x4, starting transfers between devices, swap(): lax.ppermute(odd, axis, pairs(1))  31.9 us
    all_to_all x1, blocking collectives, shards(): lax.all_to_all(outgoing, 'dom', split_axis=0, concat_axis=0, tiled=True)  19 us
    all_to_all x1, waiting for transfers between devices, shards(): lax.all_to_all(packed, 'dom', split_axis=0, concat_axis=0, tiled=True)  14.9 us
    ppermute x4, waiting for transfers between devices, swap(): lax.ppermute(odd, axis, pairs(1))  10.9 us
    pallas_call x11, Pallas kernels, call(): pl.pallas_call(kernel, out_shape=shapes, in_specs=specs, out_specs=[pl.Bl...  9.55 us
    ppermute x4, starting transfers between devices, swap(): lax.ppermute(even, axis, pairs(0))  9.11 us
    all_to_all x1, starting transfers between devices, shards(): lax.all_to_all(packed, 'dom', split_axis=0, concat_axis=0, tiled=True)  6.66 us
    unnamed x28, local copies, waits for them, and re-layouts  2.33 us
  transfers between devices with their start and end apart: 9, of which 5 were waited for; matrix products, arithmetic and copies ran while one was open for 0% of the time, Pallas kernels for 3%

profile of v2, /device:TPU:32, one launch (start us, length us, event | category | flops | bytes accessed | tf_op | source)
XLA Modules:
  0.0 107.5 jit_solution(15489032434270261806)
XLA Ops:
  0.6 0.0 copy-start.8
  0.6 0.0 copy-start.3
  0.7 0.7 copy-done.8
  1.4 0.0 copy-start.5
  1.4 19.7 %collective-permute-start = (f32[4,128]{1,0:T(4,128)S(1)}, f32[4,128]{1,0:T(4,128)S(1)}, u32[]{:S(2)}, u32[]{:S(2)}) collective-permute-start(f32[4,128]{1,0:T(4,128)S(1)} %concatenate.6), channel_id=1, source_target_pairs={{1,2},{3,4},{5,6},{7,8},{9,10},{11,12},{13,14},{15,16},{17,18},{19... | collective-permute-start | bytes 6152 | tf_op jit(solution)/shard_map/ppermute | solution.py:412
  21.1 1.9 %collective-permute-start.1 = (f32[4,128]{1,0:T(4,128)S(1)}, f32[4,128]{1,0:T(4,128)S(1)}, u32[]{:S(2)}, u32[]{:S(2)}) collective-permute-start(f32[4,128]{1,0:T(4,128)S(1)} %concatenate.7), channel_id=1, source_target_pairs={{0,1},{2,3},{4,5},{6,7},{8,9},{10,11},{12,13},{14,15},{16,17},{18,... | collective-permute-start | bytes 6152 | tf_op jit(solution)/shard_map/ppermute | solution.py:412
  23.1 0.0 copy-done.3
  23.1 0.0 copy-done.10
  23.1 0.0 copy-done.5
  23.1 0.0 copy-start
  23.1 0.9 copy-done
  24.1 0.4 own.1
  24.5 0.0 collective-permute-done.via_odd_ref
  24.5 2.1 %collective-permute-done.1.via_even_ref = f32[4,128]{1,0:T(4,128)S(1)} collective-permute-done((f32[4,128]{1,0:T(4,128)S(1)}, f32[4,128]{1,0:T(4,128)S(1)}, u32[]{:S(2)}, u32[]{:S(2)}) %collective-permute-start.1) | collective-permute-done | bytes 2080 | tf_op jit(solution)/shard_map/ppermute | solution.py:412
  26.6 0.0 copy-done.1
  26.6 0.0 copy-done.6
  26.6 0.0 copy-done.7
  26.6 0.0 copy-start.2
  26.6 0.0 copy-start.9
  26.7 0.5 residual.1
  27.1 4.9 %collective-permute-start.2 = (f32[8,128]{1,0:T(8,128)S(1)}, f32[8,128]{1,0:T(8,128)S(1)}, u32[]{:S(2)}, u32[]{:S(2)}) collective-permute-start(f32[8,128]{1,0:T(8,128)S(1)} %get-tuple-element.32), channel_id=1, source_target_pairs={{1,2},{3,4},{5,6},{7,8},{9,10},{11,12},{13,14},{15,16},{17,18},{19... | collective-permute-start | bytes 12296 | tf_op jit(solution)/shard_map/ppermute | solution.py:412
  32.0 1.9 %collective-permute-start.3 = (f32[8,128]{1,0:T(8,128)S(1)}, f32[8,128]{1,0:T(8,128)S(1)}, u32[]{:S(2)}, u32[]{:S(2)}) collective-permute-start(f32[8,128]{1,0:T(8,128)S(1)} %get-tuple-element.33), channel_id=1, source_target_pairs={{0,1},{2,3},{4,5},{6,7},{8,9},{10,11},{12,13},{14,15},{16,17},{18,... | collective-permute-start | bytes 12296 | tf_op jit(solution)/shard_map/ppermute | solution.py:412
  33.9 0.0 copy-done.2
  34.0 0.7 partial.1
  34.6 2.9 %collective-permute-done.2.via_odd_ref = f32[8,128]{1,0:T(8,128)S(1)} collective-permute-done((f32[8,128]{1,0:T(8,128)S(1)}, f32[8,128]{1,0:T(8,128)S(1)}, u32[]{:S(2)}, u32[]{:S(2)}) %collective-permute-start.2) | collective-permute-done | bytes 4128 | tf_op jit(solution)/shard_map/ppermute | solution.py:412
  37.5 0.0 collective-permute-done.3.via_even_ref
  37.5 0.7 copy-done.12
  38.2 1.7 %restrict.1 = (f32[32,128]{1,0:T(8,128)S(1)}, f32[2,128]{1,0:T(2,128)S(1)}, f32[64,2,128]{2,1,0:T(2,128)}) custom-call(f32[8,128]{1,0:T(8,128)S(1)} %select_n.29.even_ref, f32[8,128]{1,0:T(8,128)S(1)} %collective-permute-done.2.via_odd_ref, f32[8,128]{1,0:T(8,128)S(1)} %collective-permute-done.3.via_even_ref, f32[8,128]{1,0:T(8,128)S(1)} %get-tuple-element.34.ends_ref, ...), custom_call_target="tpu_custom_call" | custom-call | flops 100000000 | bytes 2000000 | tf_op jit(solution)/shard_map/restrict/pallas_call | solution.py:388
  39.9 6.7 %all-to-all-start = ((f32[64,2,128]{2,1,0:T(2,128)}), f32[64,2,128]{2,1,0:T(2,128)S(1)}, u32[]{:S(2)}, u32[]{:S(2)}) async-start(f32[64,2,128]{2,1,0:T(2,128)} %get-tuple-element.39), calls=%async_computation | async-start | bytes 131072 | tf_op jit(solution)/shard_map/all_to_all | solution.py:475
  46.6 0.1 reshape.15
  46.7 0.0 copy-start.4
  46.7 0.2 slots.1.hot_ref
  46.9 14.9 %all-to-all-done.arrived_ref = f32[64,2,128]{2,1,0:T(2,128)S(1)} async-done(((f32[64,2,128]{2,1,0:T(2,128)}), f32[64,2,128]{2,1,0:T(2,128)S(1)}, u32[]{:S(2)}, u32[]{:S(2)}) %all-to-all-start) | async-done | bytes 65568 | tf_op jit(solution)/shard_map/all_to_all | solution.py:475
  61.8 1.5 %solve.1 = f32[64,2,128]{2,1,0:T(2,128)S(1)} custom-call(f32[64,2,128]{2,1,0:T(2,128)S(1)} %all-to-all-done.arrived_ref, s32[64,128]{1,0:T(8,128)S(1)} %pad.6.nodes_ref, bf16[64,8192]{1,0:T(8,128)(2,1)S(1)} %slots.1.hot_ref, f32[4,128,128]{2,1,0:T(8,128)S(1)} %copy-done.4), custom_call_target="tpu_custom_call" | custom-call | flops 100000000 | bytes 2000000 | tf_op jit(solution)/shard_map/solve/pallas_call | solution.py:388
  63.3 19.0 %all_to_all.10.returned_ref = f32[64,2,128]{2,1,0:T(2,128)S(1)} all-to-all(f32[64,2,128]{2,1,0:T(2,128)S(1)} %solve.1), channel_id=1, replica_groups=mesh['grp'=16,'dom'=64] {'dom'}, dimensions={0} | all-to-all | bytes 131072 | tf_op jit(solution)/shard_map/all_to_all | solution.py:482
  82.3 1.3 %prolong.1 = (f32[8,1024]{1,0:T(8,128)S(1)}, f32[8,128]{1,0:T(8,128)S(1)}, f32[4,128]{1,0:T(4,128)S(1)}, f32[4,128]{1,0:T(4,128)S(1)}) custom-call(f32[8,128]{1,0:T(8,128)S(1)} %select_n.29.even_ref, f32[64,2,128]{2,1,0:T(2,128)S(1)} %all_to_all.10.returned_ref, s32[3,1024]{1,0:T(4,128)S(1)} %copy-done.3, s32[1,1024]{1,0:T(1,128)S(1)} %bitcast.9, ...), custom_call_target="tpu_custom_call" | custom-call | flops 100000000 | bytes 2000000 | tf_op jit(solution)/shard_map/prolong/pallas_call | solution.py:388
  83.6 2.1 %collective-permute-start.4 = (f32[4,128]{1,0:T(4,128)S(1)}, f32[4,128]{1,0:T(4,128)S(1)}, u32[]{:S(2)}, u32[]{:S(2)}) collective-permute-start(f32[4,128]{1,0:T(4,128)S(1)} %get-tuple-element.40), channel_id=1, source_target_pairs={{1,2},{3,4},{5,6},{7,8},{9,10},{11,12},{13,14},{15,16},{17,18},{19... | collective-permute-start | bytes 6152 | tf_op jit(solution)/shard_map/ppermute | solution.py:412
  85.7 3.3 %collective-permute-start.5 = (f32[4,128]{1,0:T(4,128)S(1)}, f32[4,128]{1,0:T(4,128)S(1)}, u32[]{:S(2)}, u32[]{:S(2)}) collective-permute-start(f32[4,128]{1,0:T(4,128)S(1)} %get-tuple-element.41), channel_id=1, source_target_pairs={{0,1},{2,3},{4,5},{6,7},{8,9},{10,11},{12,13},{14,15},{16,17},{18,... | collective-permute-start | bytes 6152 | tf_op jit(solution)/shard_map/ppermute | solution.py:412
  89.0 1.2 %smooth.1 = (f32[32,128]{1,0:T(8,128)S(1)}, f32[2,1024]{1,0:T(2,128)}, f32[8,1024]{1,0:T(8,128)S(1)}) custom-call(f32[8,1024]{1,0:T(8,128)S(1)} %get-tuple-element.44.p_ref, f32[32,128]{1,0:T(8,128)S(1)} %get-tuple-element.45.r_ref, f32[2,1024]{1,0:T(2,128)S(1)} %get-tuple-element.46.r_inner_ref, f32[2,1024]{1,0:T(2,128)S(1)} %copy-done.10, ...), custom_call_target="tpu_custom_call" | custom-call | flops 100000000 | bytes 2000000 | tf_op jit(solution)/shard_map/smooth/pallas_call | solution.py:388
  90.2 3.9 %collective-permute-done.4.via_odd_ref = f32[4,128]{1,0:T(4,128)S(1)} collective-permute-done((f32[4,128]{1,0:T(4,128)S(1)}, f32[4,128]{1,0:T(4,128)S(1)}, u32[]{:S(2)}, u32[]{:S(2)}) %collective-permute-start.4) | collective-permute-done | bytes 2080 | tf_op jit(solution)/shard_map/ppermute | solution.py:412
  94.1 0.0 collective-permute-done.5.via_even_ref
  94.1 0.5 update.1
  94.5 1.9 %collective-permute-start.7 = (f32[2,128]{1,0:T(2,128)S(1)}, f32[2,128]{1,0:T(2,128)S(1)}, u32[]{:S(2)}, u32[]{:S(2)}) collective-permute-start(f32[2,128]{1,0:T(2,128)S(1)} %get-tuple-element.54), channel_id=1, source_target_pairs={{0,1},{2,3},{4,5},{6,7},{8,9},{10,11},{12,13},{14,15},{16,17},{18,... | collective-permute-start | bytes 3080 | tf_op jit(solution)/shard_map/ppermute | solution.py:412
  96.5 5.2 %collective-permute-start.6 = (f32[2,128]{1,0:T(2,128)S(1)}, f32[2,128]{1,0:T(2,128)S(1)}, u32[]{:S(2)}, u32[]{:S(2)}) collective-permute-start(f32[2,128]{1,0:T(2,128)S(1)} %get-tuple-element.54), channel_id=1, source_target_pairs={{1,2},{3,4},{5,6},{7,8},{9,10},{11,12},{13,14},{15,16},{17,18},{19... | collective-permute-start | bytes 3080 | tf_op jit(solution)/shard_map/ppermute | solution.py:412
  101.7 0.9 output.1
  102.6 0.0 collective-permute-done.7.via_even_ref
  102.6 4.2 %collective-permute-done.6.via_odd_ref = f32[2,128]{1,0:T(2,128)S(1)} collective-permute-done((f32[2,128]{1,0:T(2,128)S(1)}, f32[2,128]{1,0:T(2,128)S(1)}, u32[]{:S(2)}, u32[]{:S(2)}) %collective-permute-start.6) | collective-permute-done | bytes 1056 | tf_op jit(solution)/shard_map/ppermute | solution.py:412
  106.8 0.7 finish.1
  (16 shorter events, 0.0 us)
Async XLA Ops:
  0.6 0.7 copy-start.8
  0.6 22.4 %copy-start.3 = (s32[3,1024]{1,0:T(4,128)S(1)}, s32[3,1024]{1,0:T(4,128)}, u32[]{:S(2)}) copy-start(s32[3,1024]{1,0:T(4,128)} %edges_ref.15) | copy-start | bytes 36868
  1.3 21.7 %copy-start.10 = (f32[2,1024]{1,0:T(2,128)S(1)}, f32[2,1024]{1,0:T(2,128)}, u32[]{:S(2)}) copy-start(f32[2,1024]{1,0:T(2,128)} %inner_ref.3) | copy-start | bytes 24580
  1.4 21.7 %copy-start.5 = (s32[1024]{0:T(1024)S(1)}, s32[1024]{0:T(1024)}, u32[]{:S(2)}) copy-start(s32[1024]{0:T(1024)} %param.20) | copy-start | bytes 12292
  1.4 23.1 %collective-permute-start = (f32[4,128]{1,0:T(4,128)S(1)}, f32[4,128]{1,0:T(4,128)S(1)}, u32[]{:S(2)}, u32[]{:S(2)}) collective-permute-start(f32[4,128]{1,0:T(4,128)S(1)} %concatenate.6), channel_id=1, source_target_pairs={{1,2},{3,4},{5,6},{7,8},{9,10},{11,12},{13,14},{15,16},{17,18},{19... | collective-permute-start | bytes 6152 | tf_op jit(solution)/shard_map/ppermute | solution.py:412
  21.1 5.5 %collective-permute-start.1 = (f32[4,128]{1,0:T(4,128)S(1)}, f32[4,128]{1,0:T(4,128)S(1)}, u32[]{:S(2)}, u32[]{:S(2)}) collective-permute-start(f32[4,128]{1,0:T(4,128)S(1)} %concatenate.7), channel_id=1, source_target_pairs={{0,1},{2,3},{4,5},{6,7},{8,9},{10,11},{12,13},{14,15},{16,17},{18,... | collective-permute-start | bytes 6152 | tf_op jit(solution)/shard_map/ppermute | solution.py:412
  23.1 1.0 copy-start
  24.0 2.6 %copy-start.1 = (f32[8,8,1024]{2,1,0:T(8,128)S(1)}, f32[8,8,1024]{2,1,0:T(8,128)}, u32[]{:S(2)}) copy-start(f32[8,8,1024]{2,1,0:T(8,128)} %matrix_ref.7) | copy-start | bytes 786436
  24.0 2.6 %copy-start.6 = (f32[2,1536]{1,0:T(2,128)S(1)}, f32[2,1536]{1,0:T(2,128)}, u32[]{:S(2)}) copy-start(f32[2,1536]{1,0:T(2,128)} %b_ref.3) | copy-start | bytes 36868
  24.1 2.6 %copy-start.7 = (f32[2,1536]{1,0:T(2,128)S(1)}, f32[2,1536]{1,0:T(2,128)}, u32[]{:S(2)}) copy-start(f32[2,1536]{1,0:T(2,128)} %w_ref.3) | copy-start | bytes 36868
  26.6 7.3 %copy-start.2 = (f32[8,6,1024]{2,0,1:T(8,128)S(1)}, f32[8,6,1024]{2,0,1:T(8,128)}, u32[]{:S(2)}) copy-start(f32[8,6,1024]{2,0,1:T(8,128)} %param.22) | copy-start | bytes 589828
  26.6 7.3 %copy-start.9 = (f32[2,1024]{1,0:T(2,128)S(1)}, f32[2,1024]{1,0:T(2,128)}, u32[]{:S(2)}) copy-start(f32[2,1024]{1,0:T(2,128)} %b_inner_ref.1) | copy-start | bytes 24580
  27.1 10.4 %collective-permute-start.2 = (f32[8,128]{1,0:T(8,128)S(1)}, f32[8,128]{1,0:T(8,128)S(1)}, u32[]{:S(2)}, u32[]{:S(2)}) collective-permute-start(f32[8,128]{1,0:T(8,128)S(1)} %get-tuple-element.32), channel_id=1, source_target_pairs={{1,2},{3,4},{5,6},{7,8},{9,10},{11,12},{13,14},{15,16},{17,18},{19... | collective-permute-start | bytes 12296 | tf_op jit(solution)/shard_map/ppermute | solution.py:412
  32.0 5.5 %collective-permute-start.3 = (f32[8,128]{1,0:T(8,128)S(1)}, f32[8,128]{1,0:T(8,128)S(1)}, u32[]{:S(2)}, u32[]{:S(2)}) collective-permute-start(f32[8,128]{1,0:T(8,128)S(1)} %get-tuple-element.33), channel_id=1, source_target_pairs={{0,1},{2,3},{4,5},{6,7},{8,9},{10,11},{12,13},{14,15},{16,17},{18,... | collective-permute-start | bytes 12296 | tf_op jit(solution)/shard_map/ppermute | solution.py:412
  37.5 0.7 copy-start.12
  39.9 6.7 %copy-start.13 = (s32[6144]{0:T(1024)S(1)}, s32[6144]{0:T(1024)}, u32[]{:S(2)}) copy-start(s32[6144]{0:T(1024)} %param.24) | copy-start | bytes 73732
  39.9 21.9 %all-to-all-start = ((f32[64,2,128]{2,1,0:T(2,128)}), f32[64,2,128]{2,1,0:T(2,128)S(1)}, u32[]{:S(2)}, u32[]{:S(2)}) async-start(f32[64,2,128]{2,1,0:T(2,128)} %get-tuple-element.39), calls=%async_computation | async-start | bytes 131072 | tf_op jit(solution)/shard_map/all_to_all | solution.py:475
  46.7 15.1 %copy-start.4 = (f32[4,128,128]{2,1,0:T(8,128)S(1)}, f32[4,128,128]{2,1,0:T(8,128)}, u32[]{:S(2)}) copy-start(f32[4,128,128]{2,1,0:T(8,128)} %inverse_ref.1) | copy-start | bytes 786436
  83.6 5.4 %copy-start.11 = (f32[2,1024]{1,0:T(2,128)S(1)}, f32[2,1024]{1,0:T(2,128)}, u32[]{:S(2)}) copy-start(f32[2,1024]{1,0:T(2,128)} %w_inner_ref.1) | copy-start | bytes 24580
  83.6 10.5 %collective-permute-start.4 = (f32[4,128]{1,0:T(4,128)S(1)}, f32[4,128]{1,0:T(4,128)S(1)}, u32[]{:S(2)}, u32[]{:S(2)}) collective-permute-start(f32[4,128]{1,0:T(4,128)S(1)} %get-tuple-element.40), channel_id=1, source_target_pairs={{1,2},{3,4},{5,6},{7,8},{9,10},{11,12},{13,14},{15,16},{17,18},{19... | collective-permute-start | bytes 6152 | tf_op jit(solution)/shard_map/ppermute | solution.py:412
  85.7 8.4 %collective-permute-start.5 = (f32[4,128]{1,0:T(4,128)S(1)}, f32[4,128]{1,0:T(4,128)S(1)}, u32[]{:S(2)}, u32[]{:S(2)}) collective-permute-start(f32[4,128]{1,0:T(4,128)S(1)} %get-tuple-element.41), channel_id=1, source_target_pairs={{0,1},{2,3},{4,5},{6,7},{8,9},{10,11},{12,13},{14,15},{16,17},{18,... | collective-permute-start | bytes 6152 | tf_op jit(solution)/shard_map/ppermute | solution.py:412
  94.5 8.1 %collective-permute-start.7 = (f32[2,128]{1,0:T(2,128)S(1)}, f32[2,128]{1,0:T(2,128)S(1)}, u32[]{:S(2)}, u32[]{:S(2)}) collective-permute-start(f32[2,128]{1,0:T(2,128)S(1)} %get-tuple-element.54), channel_id=1, source_target_pairs={{0,1},{2,3},{4,5},{6,7},{8,9},{10,11},{12,13},{14,15},{16,17},{18,... | collective-permute-start | bytes 3080 | tf_op jit(solution)/shard_map/ppermute | solution.py:412
  96.5 10.3 %collective-permute-start.6 = (f32[2,128]{1,0:T(2,128)S(1)}, f32[2,128]{1,0:T(2,128)S(1)}, u32[]{:S(2)}, u32[]{:S(2)}) collective-permute-start(f32[2,128]{1,0:T(2,128)S(1)} %get-tuple-element.54), channel_id=1, source_target_pairs={{1,2},{3,4},{5,6},{7,8},{9,10},{11,12},{13,14},{15,16},{17,18},{19... | collective-permute-start | bytes 3080 | tf_op jit(solution)/shard_map/ppermute | solution.py:412

commit v3 on v2

--- a/solution.py
+++ b/solution.py
@@ -79,7 +79,7 @@
                 spread.append(jnp.where(high == widen(at_high, count), piece, 0.0))
         spread = jnp.concatenate(spread, 0).astype(jnp.bfloat16)
         total = total + lax.dot_general(
-            spread, hot_ref[:, k * count : (k + 1) * count], (((1,), (1,)), ((), ())),
+            spread, hot_ref[k * count : (k + 1) * count, :], (((1,), (0,)), ((), ())),
             preferred_element_type=jnp.float32,
         )
     return total[:rows] + total[rows:]
@@ -93,8 +93,16 @@
 
 
 def restrict(projection_ref, live_ref, u):
-    a = [jnp.sum(projection_ref[n] * u, axis=0, keepdims=True) for n in range(6)]
-    return jnp.concatenate(a, 0) * live_ref[...].astype(jnp.float32)
+    columns = []
+    for at in range(0, u.shape[1], LANES):
+        first = at // 2
+        a = projection_ref[first : first + 8, :] * u[0:1, at : at + LANES]
+        for m in range(1, 8):
+            rows = slice(first + 8 * m, first + 8 * m + 8)
+            a = a + projection_ref[rows, :] * u[m : m + 1, at : at + LANES]
+        columns.append(a)
+    a = jnp.concatenate(columns, 1)
+    return a * live_ref[...].astype(jnp.float32)
 
 
 def rim_row(from_left, from_right, rim):
@@ -126,31 +134,47 @@
     return [table_ref[8 * g : 8 * g + 8, :] for g in range(table_ref.shape[0] // 8)]
 
 
-def own_kernel(
-    rim, x_ref, inner_ref, edges_ref, live_ref, matrix_ref, y_ref, hot_ref, table_ref
-):
+def stage_kernel(rim, count_in, *refs):
+    sources, (staged, rest) = refs[:count_in], (refs[count_in : 2 * count_in], refs[2 * count_in :])
+    by_moment_ref, y_ref, hot_ref, table_ref, sems = rest
+    x_ref, inner_ref, edges_ref, live_ref, matrix_ref, projection_ref = staged[:6]
+    copies = [
+        pltpu.make_async_copy(source, target, sems.at[i])
+        for i, (source, target) in enumerate(zip(sources, staged))
+    ]
+    for copy in copies:
+        copy.start()
+    for copy in copies[:4]:
+        copy.wait()
     edge_count = x_ref.shape[1]
     count = inner_ref.shape[1]
     load_table(table_ref, x_ref)
     places = edge_places(edges_ref, rim, edge_count + 2 * rim)
     tall = iota((LANES, count), 0)
     for k, (_, low, _) in enumerate(places):
-        hot = jnp.where(tall == low, 1.0, 0.0).astype(jnp.bfloat16)
-        hot_ref[:, k * count : (k + 1) * count] = hot
+        hot = jnp.transpose(jnp.where(tall == low, 1.0, 0.0))
+        hot_ref[k * count : (k + 1) * count, :] = hot.astype(jnp.bfloat16)
     highs = row_highs(edge_count // LANES)
     u = gather_moments(table_groups(table_ref), highs, inner_ref[...], places)
+    for copy in copies[4:]:
+        copy.wait()
     y_ref[...] = apply_matrix(matrix_ref, live_ref, u)
+    by_moment_ref[...] = jnp.zeros(by_moment_ref.shape, jnp.float32)
+    for n in range(projection_ref.shape[0]):
+        for at in range(0, count, LANES):
+            rows = pl.ds(at // 2 + n, 8, stride=8)
+            by_moment_ref[rows, :] = projection_ref[n, :, at : at + LANES]
 
 
 def residual_kernel(
     rim, even_ref, via_odd_ref, via_even_ref, own_ref, b_ref, w_ref, edges_ref, live_ref,
-    matrix_ref, hot_ref, y_ref, ends_ref, exists_ref, odd_ref, even_out_ref,
+    matrix_ref, hot_ref, y_ref, ends_ref, odd_ref, even_out_ref,
 ):
     edge_count = b_ref.shape[1]
     blocks = edge_count // LANES
     count = own_ref.shape[1]
+    tail = slice(edge_count - LANES, edge_count)
     left, right = by_side(even_ref, via_odd_ref[...], via_even_ref[...])
-    exists_ref[...] = rim_row(left[2:4], right[2:4], rim)
     none = jnp.zeros((2, LANES), jnp.float32)
     change = jnp.concatenate([none, none, rim_row(left[0:2], right[0:2], rim), none], 0)
     places = edge_places(edges_ref, rim, edge_count + 2 * rim)
@@ -160,15 +184,14 @@
     y_ref[...] = y
     ends = scatter_moments(y, places, hot_ref, highs)
     ends_ref[...] = ends
-    tail = slice(edge_count - LANES, edge_count)
     to_left = jnp.concatenate([ends[0:2], ends[4:6], b_ref[:, :LANES], w_ref[:, :LANES]], 0)
     to_right = jnp.concatenate([ends[2:4], ends[4:6], b_ref[:, tail], w_ref[:, tail]], 0)
     odd_ref[...], even_out_ref[...] = by_side(even_ref, to_left, to_right)
 
 
 def partial_kernel(
-    rim, y_ref, b_ref, b_inner_ref, edges_ref, live_ref, projection_ref, hot_ref,
-    r_ref, r_inner_ref, a_ref,
+    rim, y_ref, b_ref, b_inner_ref, edges_ref, live_ref, projection_ref, hot_ref, nodes_ref,
+    inverse_ref, counts_ref, r_ref, r_inner_ref, a_ref, slots_ref, parts_ref,
 ):
     edge_count = b_ref.shape[1]
     blocks = edge_count // LANES
@@ -182,6 +205,18 @@
     r_inner_ref[...] = r_inner
     u = gather_moments(table_groups(r_ref), highs, r_inner, places)
     a_ref[...] = restrict(projection_ref, live_ref, u)
+    agg = slots_ref.shape[1]
+    place = nodes_ref[...] & (agg - 1)
+    tall = iota((agg, LANES), 0)
+    for d in range(nodes_ref.shape[0]):
+        hot = jnp.transpose(jnp.where(tall == place[d : d + 1], 1.0, 0.0))
+        slots_ref[d * LANES : (d + 1) * LANES, :] = hot.astype(jnp.bfloat16)
+    size = inverse_ref.shape[1]
+    for b in range(inverse_ref.shape[0]):
+        coarse = inverse_ref[b].astype(jnp.bfloat16)
+        fine = (inverse_ref[b] - coarse.astype(jnp.float32)).astype(jnp.bfloat16)
+        parts_ref[:size, b * size : (b + 1) * size] = coarse
+        parts_ref[size:, b * size : (b + 1) * size] = fine
 
 
 def restrict_kernel(
@@ -223,22 +258,11 @@
     r_ref[last : last + 2, :] = r_ref[last : last + 2, :] - tail
 
 
-def slots_kernel(nodes_ref, hot_ref):
-    agg = hot_ref.shape[0]
-    place = nodes_ref[...] & (agg - 1)
-    tall = iota((agg, LANES), 0)
-    for d in range(nodes_ref.shape[0]):
-        hot = jnp.where(tall == place[d : d + 1], 1.0, 0.0).astype(jnp.bfloat16)
-        hot_ref[:, d * LANES : (d + 1) * LANES] = hot
-
-
-def solve_kernel(arrived_ref, nodes_ref, hot_ref, inverse_ref, out_ref):
-    peers = arrived_ref.shape[0]
-    groups = inverse_ref.shape[0]
-    agg = inverse_ref.shape[1] // 2
+def solve_kernel(arrived_ref, nodes_ref, slots_ref, parts_ref, out_ref):
+    peers, agg = nodes_ref.shape[0], slots_ref.shape[1]
+    groups = parts_ref.shape[1] // (2 * agg)
     row = iota((8, LANES), 0)
-    nodes = nodes_ref[...]
-    block, place = nodes >> 6, nodes & (agg - 1)
+    block = nodes_ref[...] >> 6
     total = jnp.zeros((16, agg), jnp.float32)
     span = 16
     for first in range(0, peers, span):
@@ -246,8 +270,8 @@
         for d in range(first, first + span):
             value = jnp.where(
                 row < 4,
-                jnp.broadcast_to(arrived_ref[d, 0:1, :], (8, LANES)),
-                jnp.broadcast_to(arrived_ref[d, 1:2, :], (8, LANES)),
+                jnp.broadcast_to(arrived_ref[2 * d : 2 * d + 1, :], (8, LANES)),
+                jnp.broadcast_to(arrived_ref[2 * d + 1 : 2 * d + 2, :], (8, LANES)),
             )
             value = jnp.where((row & 3) == block[d : d + 1], value, 0.0)
             coarse = value.astype(jnp.bfloat16).astype(jnp.float32)
@@ -256,28 +280,34 @@
         spread = jnp.concatenate(
             [jnp.concatenate(coarse_parts, 1), jnp.concatenate(fine_parts, 1)], 0
         ).astype(jnp.bfloat16)
-        hot = hot_ref[:, first * LANES : (first + span) * LANES]
         total = total + lax.dot_general(
-            spread, hot, (((1,), (1,)), ((), ())), preferred_element_type=jnp.float32
+            spread, slots_ref[first * LANES : (first + span) * LANES, :],
+            (((1,), (0,)), ((), ())), preferred_element_type=jnp.float32,
         )
     g = total[:8] + total[8:]
     vectors = jnp.concatenate([g, pltpu.roll(g, 4, 0)], 1)
-    table = jnp.zeros((8, LANES), jnp.float32)
-    for b in range(groups):
-        h = lax.dot_general(
-            vectors, inverse_ref[b], (((1,), (0,)), ((), ())),
-            precision=lax.Precision.HIGHEST, preferred_element_type=jnp.float32,
-        )[b : b + 1]
-        h = jnp.broadcast_to(h, (8, LANES))
-        table = jnp.where(row == 2 * b, h, table)
-        table = jnp.where(row == 2 * b + 1, pltpu.roll(h, agg, 1), table)
-    for d in range(peers):
-        low = jnp.broadcast_to(place[d : d + 1], (8, LANES))
-        found = jnp.take_along_axis(table, low, axis=1)
-        found = jnp.where((row >> 1) == block[d : d + 1], found, 0.0)
-        found = found + pltpu.roll(found, 4, 0)
-        found = found + pltpu.roll(found, 2, 0)
-        out_ref[d] = found[0:2]
+    coarse = vectors.astype(jnp.bfloat16).astype(jnp.float32)
+    fine = vectors - coarse
+    sides = jnp.concatenate(
+        [jnp.concatenate([coarse, coarse], 1), jnp.concatenate([fine, jnp.zeros_like(fine)], 1)], 0
+    ).astype(jnp.bfloat16)
+    solved = lax.dot_general(
+        sides, parts_ref[...], (((1,), (0,)), ((), ())), preferred_element_type=jnp.float32
+    )
+    solved = solved[:8] + solved[8:]
+    tables = [
+        jnp.broadcast_to(solved[b : b + 1, b * LANES : (b + 1) * LANES], (8, LANES))
+        for b in range(groups)
+    ]
+    for first in range(0, peers, 8):
+        here = nodes_ref[first : first + 8, :]
+        owner, place = here >> 6, here & (agg - 1)
+        for c in range(2):
+            found = jnp.zeros((8, LANES), jnp.float32)
+            for b in range(groups):
+                picked = jnp.take_along_axis(tables[b], place + c * agg, axis=1)
+                found = jnp.where(owner == b, picked, found)
+            out_ref[pl.ds(2 * first + c, 8, stride=2), :] = found
 
 
 def prolong_kernel(
@@ -292,7 +322,7 @@
         base = pl.multiple_of(start - shift, LANES)
         moved = pltpu.roll(returned_ref[q], shift, 1)
         here = pl.ds(base, LANES)
-        vals_ref[:, here] = jnp.where(lane >= shift, moved, vals_ref[:, here])
+        pltpu.store(vals_ref.at[:, here], moved, mask=lane >= shift)
         vals_ref[:, pl.ds(base + LANES, LANES)] = moved
         start = start + counts_ref[0, q]
     nodal = jnp.concatenate([vals_ref[:, k * count : (k + 1) * count] for k in range(3)], 0)
@@ -329,7 +359,7 @@
 
 def update_kernel(
     rim, edge_count, even_ref, via_odd_ref, via_even_ref, ends_ref, exists_ref, s_rim_ref,
-    part_ref, edges_ref, live_ref, matrix_ref, hot_ref, y_ref, change_ref, rims_ref,
+    part_ref, edges_ref, live_ref, matrix_ref, hot_ref, y_ref, change_ref, odd_ref, even_out_ref,
 ):
     count = part_ref.shape[1]
     left, right = by_side(even_ref, via_odd_ref[...], via_even_ref[...])
@@ -343,7 +373,9 @@
     u = gather_moments([change], highs, jnp.zeros((2, count), jnp.float32), places)
     y = part_ref[...] + apply_matrix(matrix_ref, live_ref, u)
     y_ref[...] = y
-    rims_ref[...] = scatter_moments(y, places, hot_ref, highs)[4:6]
+    rims = scatter_moments(y, places, hot_ref, highs)[4:6]
+    odd_ref[...] = rims
+    even_out_ref[...] = rims
 
 
 def output_kernel(
@@ -377,20 +409,22 @@
     r1_ref[:, last] = part_ref[:, last] - tail
 
 
-def local_call(kernel, outs, in_smem=(), scratch=(), name=None):
+def local_call(kernel, outs, in_smem=(), in_place=False, scratch=(), sems=0, name=None):
     def call(*args):
-        specs = [
-            pl.BlockSpec(memory_space=pltpu.SMEM if i in in_smem else pltpu.VMEM)
-            for i in range(len(args))
+        spaces = [pltpu.SMEM if i in in_smem else pltpu.VMEM for i in range(len(args))]
+        if in_place:
+            spaces = [pltpu.HBM] * len(args)
+        shapes = [
+            jax.ShapeDtypeStruct(*(o if isinstance(o[0], tuple) else (o, jnp.float32)))
+            for o in outs
         ]
-        shapes = [jax.ShapeDtypeStruct(*(s if s[-1] == jnp.bfloat16 else (s, jnp.float32)))
-                  for s in outs]
+        extra = [pltpu.SemaphoreType.DMA((sems,))] if sems else []
         return pl.pallas_call(
             kernel,
             out_shape=shapes,
-            in_specs=specs,
+            in_specs=[pl.BlockSpec(memory_space=space) for space in spaces],
             out_specs=[pl.BlockSpec(memory_space=pltpu.VMEM)] * len(outs),
-            scratch_shapes=[pltpu.VMEM(s, jnp.float32) for s in scratch],
+            scratch_shapes=[pltpu.VMEM(s, jnp.float32) for s in scratch] + extra,
             compiler_params=pltpu.CompilerParams(vmem_limit_bytes=VMEM_LIMIT),
             cost_estimate=pl.CostEstimate(
                 flops=10**8, bytes_accessed=2 * 10**6, transcendentals=0
@@ -435,14 +469,17 @@
     agg = aux_inverse.shape[1] // 2
     rows = -(-2 * (edge_count // LANES + 1) // 8) * 8
     live = element_live.reshape(1, elem_count)
-    projection = jnp.transpose(projection, (1, 0, 2))
-    is_even = lax.axis_index(("grp", "dom")) % 2 == 0
-    even = jnp.where(is_even, jnp.ones((8, LANES), jnp.float32), 0.0)
+    strip = lax.axis_index(("grp", "dom"))
+    even = jnp.where(strip % 2 == 0, jnp.ones((8, LANES), jnp.float32), 0.0)
+    lane = iota((2, LANES), 1)
+    is_last = strip == lax.axis_size(("grp", "dom")) - 1
+    exists = jnp.where(lane < rim, jnp.where(is_last, 0.0, 1.0), jnp.where(strip == 0, 0.0, 1.0))
+    exists = jnp.where(lane < 2 * rim, exists, 0.0)
+    x_head, x_tail = x_edges[:, :LANES], x_edges[:, edge_count - LANES :]
     ones = jnp.ones((2, LANES), jnp.float32)
-    x_head, x_tail = x_edges[:, :LANES], x_edges[:, edge_count - LANES :]
     via_odd, via_even = swap(
-        jnp.concatenate([jnp.where(is_even, x_head, x_tail), ones], 0),
-        jnp.concatenate([jnp.where(is_even, x_tail, x_head), ones], 0),
+        jnp.concatenate([jnp.where(strip % 2 == 0, x_head, x_tail), ones], 0),
+        jnp.concatenate([jnp.where(strip % 2 == 0, x_tail, x_head), ones], 0),
     )
     nodes = jnp.pad(aux_node.reshape(peers, cap), ((0, 0), (0, LANES - cap)))
     table = (rows, LANES)
@@ -450,51 +487,64 @@
     inner = (2, elem_count)
     moments = (8, elem_count)
     slots = (peers, 2, LANES)
-    hots = ((LANES, 3 * elem_count), jnp.bfloat16)
+    hots = ((3 * elem_count, LANES), jnp.bfloat16)
     lists = (2, 3 * elem_count + LANES)
 
-    own, hot = local_call(
-        functools.partial(own_kernel, rim), [moments, hots], scratch=[table], name="own"
-    )(x_edges, x_inner, elem_edges, live, elem_matrix)
-    y, ends, exists, odd_out, even_out = local_call(
-        functools.partial(residual_kernel, rim), [moments, group, (2, LANES), group, group],
-        name="residual",
+    arguments = (
+        x_edges, x_inner, elem_edges, live, elem_matrix, jnp.transpose(projection, (1, 0, 2)),
+        b_edges, b_inner, w_edges, w_inner, aux_inverse,
+    )
+    *staged, by_moment, own, hot = local_call(
+        functools.partial(stage_kernel, rim, len(arguments)),
+        [(v.shape, v.dtype) for v in arguments] + [(elem_count // 2, LANES), moments, hots],
+        in_place=True, scratch=[table], sems=len(arguments), name="stage",
+    )(*[pltpu.with_memory_space_constraint(v, pltpu.HBM) for v in arguments])
+    x_edges, x_inner, elem_edges, live, elem_matrix, nodal_first = staged[:6]
+    b_edges, b_inner, w_edges, w_inner, aux_inverse = staged[6:]
+    y, ends, odd_out, even_out = local_call(
+        functools.partial(residual_kernel, rim), [moments, group, group, group], name="residual"
     )(
         even, via_odd, via_even, own, b_edges, w_edges, elem_edges, live, elem_matrix, hot
     )
     via_odd, via_even = swap(odd_out, even_out)
-    r, r_inner, a = local_call(
-        functools.partial(partial_kernel, rim), [table, inner, (6, elem_count)], name="partial"
-    )(y, b_edges, b_inner, elem_edges, live, projection, hot)
+    size = 2 * agg
+    r, r_inner, a, slots_hot, parts = local_call(
+        functools.partial(partial_kernel, rim),
+        [
+            table, inner, moments, ((peers * LANES, agg), jnp.bfloat16),
+            ((2 * size, aux_inverse.shape[0] * size), jnp.bfloat16),
+        ],
+        in_smem=(10,), name="partial",
+    )(
+        y, b_edges, b_inner, elem_edges, live, by_moment, hot, nodes, aux_inverse, owner_counts
+    )
     r, s_rim, packed = local_call(
         functools.partial(restrict_kernel, rim, edge_count), [table, (2, LANES), slots],
         in_smem=(10,), scratch=[lists], name="restrict",
     )(
-        even, via_odd, via_even, ends, exists, r, a, elem_edges, live, projection, owner_counts
+        even, via_odd, via_even, ends, exists, r, a, elem_edges, live, by_moment, owner_counts
     )
     arrived = lax.all_to_all(packed, "dom", split_axis=0, concat_axis=0, tiled=True)
-    (slots_hot,) = local_call(
-        slots_kernel, [((agg, peers * LANES), jnp.bfloat16)], name="slots"
-    )(nodes)
-    (outgoing,) = local_call(solve_kernel, [slots], name="solve")(
-        arrived, nodes, slots_hot, aux_inverse
-    )
+    (outgoing,) = local_call(solve_kernel, [(2 * peers, LANES)], name="solve")(
+        arrived.reshape(2 * peers, LANES), nodes, slots_hot, parts
+    )
+    outgoing = outgoing.reshape(slots)
     returned = lax.all_to_all(outgoing, "dom", split_axis=0, concat_axis=0, tiled=True)
     p, ends, odd_out, even_out = local_call(
         functools.partial(prolong_kernel, rim, edge_count),
         [moments, group, (4, LANES), (4, LANES)], in_smem=(5,), scratch=[lists], name="prolong",
-    )(even, returned, elem_edges, live, projection, owner_counts, hot)
+    )(even, returned, elem_edges, live, nodal_first, owner_counts, hot)
     via_odd, via_even = swap(odd_out, even_out)
     z, x1_inner, az = local_call(
         functools.partial(smooth_kernel, rim), [table, inner, moments], name="smooth"
     )(p, r, r_inner, x_inner, w_edges, w_inner, elem_edges, live, elem_matrix, hot)
-    az, change, rims = local_call(
-        functools.partial(update_kernel, rim, edge_count), [moments, group, (2, LANES)],
-        name="update",
+    az, change, odd_out, even_out = local_call(
+        functools.partial(update_kernel, rim, edge_count),
+        [moments, group, (2, LANES), (2, LANES)], name="update",
     )(
         even, via_odd, via_even, ends, exists, s_rim, az, elem_edges, live, elem_matrix, hot
     )
-    via_odd, via_even = swap(rims, rims)
+    via_odd, via_even = swap(odd_out, even_out)
     x1_edges, r1_part, r1_inner = local_call(
         functools.partial(output_kernel, rim), [x_edges.shape, x_edges.shape, inner],
         name="output",

time: 108 us -> 103 us (0.954)
  blocking collectives: 19 us -> 40.5 us
  waiting for transfers between devices: 27.9 us -> 10.4 us
  starting transfers between devices: 47.7 us -> 40.6 us
  local copies, waits for them, and re-layouts: 2.43 us -> 0.84 us
    all_to_all x0 -> x1, blocking collectives: none -> 21.6 us  [shards(): lax.all_to_all(packed, 'dom', split_axis=0, concat_axis=0, tiled=True)]
    all_to_all x1 -> x0, waiting for transfers between devices: 14.9 us -> none  [shards(): lax.all_to_all(packed, 'dom', split_axis=0, concat_axis=0, tiled=True)]
    all_to_all x1 -> x0, starting transfers between devices: 6.66 us -> none  [shards(): lax.all_to_all(packed, 'dom', split_axis=0, concat_axis=0, tiled=True)]
    unnamed x28 -> x2, local copies, waits for them, and re-layouts: 2.33 us -> 0.01 us
    ppermute x4, waiting for transfers between devices: 10.9 us -> 9.05 us  [swap(): lax.ppermute(odd, axis, pairs(1))]
    pallas_call x11 -> x10, Pallas kernels: 9.55 us -> 8.89 us  [call(): pl.pallas_call(kernel, out_shape=shapes, in_specs=[pl.BlockSpec(memory_sp...]
  transfers between devices with their start and end apart: 9 -> 8, of which waited for: 5 -> 5; matrix products, arithmetic and copies ran while one was open for 0% -> 1% of each run, Pallas kernels for 3% -> 4%
where the time goes in v3:
time: 103 us
  starting transfers between devices  40.6 us (39%)
  blocking collectives  40.5 us (39%)
  waiting for transfers between devices  10.4 us (10%)
  Pallas kernels  8.89 us (9%)
    ppermute x4, starting transfers between devices, swap(): lax.ppermute(odd, axis, pairs(1))  31.5 us
    all_to_all x1, blocking collectives, shards(): lax.all_to_all(packed, 'dom', split_axis=0, concat_axis=0, tiled=True)  21.6 us
    all_to_all x1, blocking collectives, shards(): lax.all_to_all(outgoing, 'dom', split_axis=0, concat_axis=0, tiled=True)  19 us
    ppermute x4, starting transfers between devices, swap(): lax.ppermute(even, axis, pairs(0))  9.09 us
    ppermute x4, waiting for transfers between devices, swap(): lax.ppermute(odd, axis, pairs(1))  9.05 us
    pallas_call x10, Pallas kernels, call(): pl.pallas_call(kernel, out_shape=shapes, in_specs=[pl.BlockSpec(memory_sp...  8.89 us
  transfers between devices with their start and end apart: 8, of which 5 were waited for; matrix products, arithmetic and copies ran while one was open for 1% of the time, Pallas kernels for 4%

profile of v3, /device:TPU:32, one launch (start us, length us, event | category | flops | bytes accessed | tf_op | source)
XLA Modules:
  0.0 102.8 jit_solution(8389379544778957275)
XLA Ops:
  0.6 0.0 copy-start
  0.7 0.7 broadcast_select_fusion.1
  1.4 19.7 %collective-permute-start = (f32[4,128]{1,0:T(4,128)S(1)}, f32[4,128]{1,0:T(4,128)S(1)}, u32[]{:S(2)}, u32[]{:S(2)}) collective-permute-start(f32[4,128]{1,0:T(4,128)S(1)} %concatenate.6), channel_id=1, source_target_pairs={{1,2},{3,4},{5,6},{7,8},{9,10},{11,12},{13,14},{15,16},{17,18},{19... | collective-permute-start | bytes 6152 | tf_op jit(solution)/shard_map/ppermute | solution.py:446
  21.1 1.9 %collective-permute-start.1 = (f32[4,128]{1,0:T(4,128)S(1)}, f32[4,128]{1,0:T(4,128)S(1)}, u32[]{:S(2)}, u32[]{:S(2)}) collective-permute-start(f32[4,128]{1,0:T(4,128)S(1)} %concatenate.7), channel_id=1, source_target_pairs={{0,1},{2,3},{4,5},{6,7},{8,9},{10,11},{12,13},{14,15},{16,17},{18,... | collective-permute-start | bytes 6152 | tf_op jit(solution)/shard_map/ppermute | solution.py:446
  23.1 1.5 %stage.1 = (f32[2,1536]{1,0:T(2,128)S(1)}, f32[2,1024]{1,0:T(2,128)S(1)}, s32[3,1024]{1,0:T(4,128)S(1)}, s32[1,1024]{1,0:T(1,128)S(1)}, f32[8,8,1024]{2,1,0:T(8,...) custom-call(f32[2,1536]{1,0:T(2,128)} %refs_0_.1, ...), custom_call_target="tpu_custom_call" | custom-call | flops 100000000 | bytes 2000000 | tf_op jit(solution)/shard_map/stage/pallas_call | solution.py:422
  24.6 0.8 reshape.21
  25.4 0.0 collective-permute-done.via_odd_ref
  25.4 1.2 %collective-permute-done.1.via_even_ref = f32[4,128]{1,0:T(4,128)S(1)} collective-permute-done((f32[4,128]{1,0:T(4,128)S(1)}, f32[4,128]{1,0:T(4,128)S(1)}, u32[]{:S(2)}, u32[]{:S(2)}) %collective-permute-start.1) | collective-permute-done | bytes 2080 | tf_op jit(solution)/shard_map/ppermute | solution.py:446
  26.6 0.4 residual.1
  27.0 4.8 %collective-permute-start.2 = (f32[8,128]{1,0:T(8,128)S(1)}, f32[8,128]{1,0:T(8,128)S(1)}, u32[]{:S(2)}, u32[]{:S(2)}) collective-permute-start(f32[8,128]{1,0:T(8,128)S(1)} %get-tuple-element.51), channel_id=1, source_target_pairs={{1,2},{3,4},{5,6},{7,8},{9,10},{11,12},{13,14},{15,16},{17,18},{19... | collective-permute-start | bytes 12296 | tf_op jit(solution)/shard_map/ppermute | solution.py:446
  31.9 1.9 %collective-permute-start.3 = (f32[8,128]{1,0:T(8,128)S(1)}, f32[8,128]{1,0:T(8,128)S(1)}, u32[]{:S(2)}, u32[]{:S(2)}) collective-permute-start(f32[8,128]{1,0:T(8,128)S(1)} %get-tuple-element.52), channel_id=1, source_target_pairs={{0,1},{2,3},{4,5},{6,7},{8,9},{10,11},{12,13},{14,15},{16,17},{18,... | collective-permute-start | bytes 12296 | tf_op jit(solution)/shard_map/ppermute | solution.py:446
  33.8 0.0 copy-done
  33.8 1.1 %partial.1 = (f32[32,128]{1,0:T(8,128)S(1)}, f32[2,1024]{1,0:T(2,128)S(1)}, f32[8,1024]{1,0:T(8,128)S(1)}, bf16[8192,64]{1,0:T(8,128)(2,1)S(1)}, bf16[256,512]{1,0:T(8,128)(2,1)S(1)}) custom-call(f32[8,1024]{1,0:T(8,128)S(1)} %get-tuple-element.54.y_ref, f32[2,1536]{1,0:T(2,128)S(1)} %get-tuple-element.45.b_ref, ...), custom_call_target="tpu_custom_call" | custom-call | flops 100000000 | bytes 2000000 | tf_op jit(solution)/shard_map/partial/pallas_call | solution.py:422
  34.9 2.5 %collective-permute-done.2.via_odd_ref = f32[8,128]{1,0:T(8,128)S(1)} collective-permute-done((f32[8,128]{1,0:T(8,128)S(1)}, f32[8,128]{1,0:T(8,128)S(1)}, u32[]{:S(2)}, u32[]{:S(2)}) %collective-permute-start.2) | collective-permute-done | bytes 4128 | tf_op jit(solution)/shard_map/ppermute | solution.py:446
  37.4 0.0 collective-permute-done.3.via_even_ref
  37.4 1.1 %restrict.1 = (f32[32,128]{1,0:T(8,128)S(1)}, f32[2,128]{1,0:T(2,128)S(1)}, f32[64,2,128]{2,1,0:T(2,128)S(1)}) custom-call(f32[8,128]{1,0:T(8,128)S(1)} %select_n.49.even_ref, f32[8,128]{1,0:T(8,128)S(1)} %collective-permute-done.2.via_odd_ref, f32[8,128]{1,0:T(8,128)S(1)} %collective-permute-done.3.via_even_ref, f32[8,128]{1,0:T(8,128)S(1)} %get-tuple-element.53.ends_ref, ...), custom_call_target="tpu_custom_call" | custom-call | flops 100000000 | bytes 2000000 | tf_op jit(solution)/shard_map/restrict/pallas_call | solution.py:422
  38.5 21.6 %all_to_all.10 = f32[64,2,128]{2,1,0:T(2,128)S(1)} all-to-all(f32[64,2,128]{2,1,0:T(2,128)S(1)} %get-tuple-element.60), channel_id=1, replica_groups=mesh['grp'=16,'dom'=64] {'dom'}, dimensions={0} | all-to-all | bytes 131072 | tf_op jit(solution)/shard_map/all_to_all | solution.py:527
  60.0 0.8 solve.1
  60.9 19.0 %all_to_all.11.returned_ref = f32[64,2,128]{2,1,0:T(2,128)S(1)} all-to-all(f32[64,2,128]{2,1,0:T(2,128)S(1)} %bitcast.5), channel_id=1, replica_groups=mesh['grp'=16,'dom'=64] {'dom'}, dimensions={0} | all-to-all | bytes 131072 | tf_op jit(solution)/shard_map/all_to_all | solution.py:532
  79.8 1.0 %prolong.1 = (f32[8,1024]{1,0:T(8,128)S(1)}, f32[8,128]{1,0:T(8,128)S(1)}, f32[4,128]{1,0:T(4,128)S(1)}, f32[4,128]{1,0:T(4,128)S(1)}) custom-call(f32[8,128]{1,0:T(8,128)S(1)} %select_n.49.even_ref, f32[64,2,128]{2,1,0:T(2,128)S(1)} %all_to_all.11.returned_ref, s32[3,1024]{1,0:T(4,128)S(1)} %get-tuple-element.47.edges_ref, ...), custom_call_target="tpu_custom_call" | custom-call | flops 100000000 | bytes 2000000 | tf_op jit(solution)/shard_map/prolong/pallas_call | solution.py:422
  80.9 1.9 %collective-permute-start.4 = (f32[4,128]{1,0:T(4,128)S(1)}, f32[4,128]{1,0:T(4,128)S(1)}, u32[]{:S(2)}, u32[]{:S(2)}) collective-permute-start(f32[4,128]{1,0:T(4,128)S(1)} %get-tuple-element.64), channel_id=1, source_target_pairs={{1,2},{3,4},{5,6},{7,8},{9,10},{11,12},{13,14},{15,16},{17,18},{19... | collective-permute-start | bytes 6152 | tf_op jit(solution)/shard_map/ppermute | solution.py:446
  82.8 3.3 %collective-permute-start.5 = (f32[4,128]{1,0:T(4,128)S(1)}, f32[4,128]{1,0:T(4,128)S(1)}, u32[]{:S(2)}, u32[]{:S(2)}) collective-permute-start(f32[4,128]{1,0:T(4,128)S(1)} %get-tuple-element.65), channel_id=1, source_target_pairs={{0,1},{2,3},{4,5},{6,7},{8,9},{10,11},{12,13},{14,15},{16,17},{18,... | collective-permute-start | bytes 6152 | tf_op jit(solution)/shard_map/ppermute | solution.py:446
  86.2 1.1 %smooth.1 = (f32[32,128]{1,0:T(8,128)S(1)}, f32[2,1024]{1,0:T(2,128)}, f32[8,1024]{1,0:T(8,128)S(1)}) custom-call(f32[8,1024]{1,0:T(8,128)S(1)} %get-tuple-element.68.p_ref, f32[32,128]{1,0:T(8,128)S(1)} %get-tuple-element.69.r_ref, f32[2,1024]{1,0:T(2,128)S(1)} %get-tuple-element.70.r_inner_ref, f32[2,1024]{1,0:T(2,128)S(1)} %get-tuple-element.71.inner_ref, ...), custom_call_target="tpu_custom_call" | custom-call | flops 100000000 | bytes 2000000 | tf_op jit(solution)/shard_map/smooth/pallas_call | solution.py:422
  87.2 4.0 %collective-permute-done.4.via_odd_ref = f32[4,128]{1,0:T(4,128)S(1)} collective-permute-done((f32[4,128]{1,0:T(4,128)S(1)}, f32[4,128]{1,0:T(4,128)S(1)}, u32[]{:S(2)}, u32[]{:S(2)}) %collective-permute-start.4) | collective-permute-done | bytes 2080 | tf_op jit(solution)/shard_map/ppermute | solution.py:446
  91.2 0.0 collective-permute-done.5.via_even_ref
  91.2 0.4 update.1
  91.6 5.0 %collective-permute-start.6 = (f32[2,128]{1,0:T(2,128)S(1)}, f32[2,128]{1,0:T(2,128)S(1)}, u32[]{:S(2)}, u32[]{:S(2)}) collective-permute-start(f32[2,128]{1,0:T(2,128)S(1)} %get-tuple-element.81), channel_id=1, source_target_pairs={{1,2},{3,4},{5,6},{7,8},{9,10},{11,12},{13,14},{15,16},{17,18},{19... | collective-permute-start | bytes 3080 | tf_op jit(solution)/shard_map/ppermute | solution.py:446
  96.7 1.9 %collective-permute-start.7 = (f32[2,128]{1,0:T(2,128)S(1)}, f32[2,128]{1,0:T(2,128)S(1)}, u32[]{:S(2)}, u32[]{:S(2)}) collective-permute-start(f32[2,128]{1,0:T(2,128)S(1)} %get-tuple-element.82), channel_id=1, source_target_pairs={{0,1},{2,3},{4,5},{6,7},{8,9},{10,11},{12,13},{14,15},{16,17},{18,... | collective-permute-start | bytes 3080 | tf_op jit(solution)/shard_map/ppermute | solution.py:446
  98.6 0.8 output.1
  99.4 2.6 %collective-permute-done.6.via_odd_ref = f32[2,128]{1,0:T(2,128)S(1)} collective-permute-done((f32[2,128]{1,0:T(2,128)S(1)}, f32[2,128]{1,0:T(2,128)S(1)}, u32[]{:S(2)}, u32[]{:S(2)}) %collective-permute-start.6) | collective-permute-done | bytes 1056 | tf_op jit(solution)/shard_map/ppermute | solution.py:446
  102.0 0.1 collective-permute-done.7.via_even_ref
  102.1 0.7 finish.1
  (7 shorter events, 0.0 us)
Async XLA Ops:
  0.6 33.2 %copy-start = (s32[1,64]{1,0:T(1,128)S(1)}, s32[1,64]{1,0:T(1,128)}, u32[]{:S(2)}) copy-start(s32[1,64]{1,0:T(1,128)} %counts_ref.5) | copy-start | bytes 772
  1.4 24.0 %collective-permute-start = (f32[4,128]{1,0:T(4,128)S(1)}, f32[4,128]{1,0:T(4,128)S(1)}, u32[]{:S(2)}, u32[]{:S(2)}) collective-permute-start(f32[4,128]{1,0:T(4,128)S(1)} %concatenate.6), channel_id=1, source_target_pairs={{1,2},{3,4},{5,6},{7,8},{9,10},{11,12},{13,14},{15,16},{17,18},{19... | collective-permute-start | bytes 6152 | tf_op jit(solution)/shard_map/ppermute | solution.py:446
  21.1 5.5 %collective-permute-start.1 = (f32[4,128]{1,0:T(4,128)S(1)}, f32[4,128]{1,0:T(4,128)S(1)}, u32[]{:S(2)}, u32[]{:S(2)}) collective-permute-start(f32[4,128]{1,0:T(4,128)S(1)} %concatenate.7), channel_id=1, source_target_pairs={{0,1},{2,3},{4,5},{6,7},{8,9},{10,11},{12,13},{14,15},{16,17},{18,... | collective-permute-start | bytes 6152 | tf_op jit(solution)/shard_map/ppermute | solution.py:446
  27.0 10.4 %collective-permute-start.2 = (f32[8,128]{1,0:T(8,128)S(1)}, f32[8,128]{1,0:T(8,128)S(1)}, u32[]{:S(2)}, u32[]{:S(2)}) collective-permute-start(f32[8,128]{1,0:T(8,128)S(1)} %get-tuple-element.51), channel_id=1, source_target_pairs={{1,2},{3,4},{5,6},{7,8},{9,10},{11,12},{13,14},{15,16},{17,18},{19... | collective-permute-start | bytes 12296 | tf_op jit(solution)/shard_map/ppermute | solution.py:446
  31.9 5.5 %collective-permute-start.3 = (f32[8,128]{1,0:T(8,128)S(1)}, f32[8,128]{1,0:T(8,128)S(1)}, u32[]{:S(2)}, u32[]{:S(2)}) collective-permute-start(f32[8,128]{1,0:T(8,128)S(1)} %get-tuple-element.52), channel_id=1, source_target_pairs={{0,1},{2,3},{4,5},{6,7},{8,9},{10,11},{12,13},{14,15},{16,17},{18,... | collective-permute-start | bytes 12296 | tf_op jit(solution)/shard_map/ppermute | solution.py:446
  80.9 10.3 %collective-permute-start.4 = (f32[4,128]{1,0:T(4,128)S(1)}, f32[4,128]{1,0:T(4,128)S(1)}, u32[]{:S(2)}, u32[]{:S(2)}) collective-permute-start(f32[4,128]{1,0:T(4,128)S(1)} %get-tuple-element.64), channel_id=1, source_target_pairs={{1,2},{3,4},{5,6},{7,8},{9,10},{11,12},{13,14},{15,16},{17,18},{19... | collective-permute-start | bytes 6152 | tf_op jit(solution)/shard_map/ppermute | solution.py:446
  82.8 8.4 %collective-permute-start.5 = (f32[4,128]{1,0:T(4,128)S(1)}, f32[4,128]{1,0:T(4,128)S(1)}, u32[]{:S(2)}, u32[]{:S(2)}) collective-permute-start(f32[4,128]{1,0:T(4,128)S(1)} %get-tuple-element.65), channel_id=1, source_target_pairs={{0,1},{2,3},{4,5},{6,7},{8,9},{10,11},{12,13},{14,15},{16,17},{18,... | collective-permute-start | bytes 6152 | tf_op jit(solution)/shard_map/ppermute | solution.py:446
  91.6 10.3 %collective-permute-start.6 = (f32[2,128]{1,0:T(2,128)S(1)}, f32[2,128]{1,0:T(2,128)S(1)}, u32[]{:S(2)}, u32[]{:S(2)}) collective-permute-start(f32[2,128]{1,0:T(2,128)S(1)} %get-tuple-element.81), channel_id=1, source_target_pairs={{1,2},{3,4},{5,6},{7,8},{9,10},{11,12},{13,14},{15,16},{17,18},{19... | collective-permute-start | bytes 3080 | tf_op jit(solution)/shard_map/ppermute | solution.py:446
  96.7 5.5 %collective-permute-start.7 = (f32[2,128]{1,0:T(2,128)S(1)}, f32[2,128]{1,0:T(2,128)S(1)}, u32[]{:S(2)}, u32[]{:S(2)}) collective-permute-start(f32[2,128]{1,0:T(2,128)S(1)} %get-tuple-element.82), channel_id=1, source_target_pairs={{0,1},{2,3},{4,5},{6,7},{8,9},{10,11},{12,13},{14,15},{16,17},{18,... | collective-permute-start | bytes 3080 | tf_op jit(solution)/shard_map/ppermute | solution.py:446

commit v4 on v3

--- a/solution.py
+++ b/solution.py
@@ -174,9 +174,12 @@
     blocks = edge_count // LANES
     count = own_ref.shape[1]
     tail = slice(edge_count - LANES, edge_count)
-    left, right = by_side(even_ref, via_odd_ref[...], via_even_ref[...])
+    heads, tails = via_odd_ref[:, :LANES], via_odd_ref[:, tail]
+    even = even_ref[0:2, :] > 0.5
+    left = jnp.where(even, tails, via_even_ref[...])
+    right = jnp.where(even, via_even_ref[...], heads)
     none = jnp.zeros((2, LANES), jnp.float32)
-    change = jnp.concatenate([none, none, rim_row(left[0:2], right[0:2], rim), none], 0)
+    change = jnp.concatenate([none, none, rim_row(left, right, rim), none], 0)
     places = edge_places(edges_ref, rim, edge_count + 2 * rim)
     highs = end_highs(blocks)
     u = gather_moments([change], highs, jnp.zeros((2, count), jnp.float32), places)
@@ -191,7 +194,7 @@
 
 def partial_kernel(
     rim, y_ref, b_ref, b_inner_ref, edges_ref, live_ref, projection_ref, hot_ref, nodes_ref,
-    inverse_ref, counts_ref, r_ref, r_inner_ref, a_ref, slots_ref, parts_ref,
+    inverse_ref, r_ref, r_inner_ref, a_ref, slots_ref, parts_ref,
 ):
     edge_count = b_ref.shape[1]
     blocks = edge_count // LANES
@@ -205,9 +208,8 @@
     r_inner_ref[...] = r_inner
     u = gather_moments(table_groups(r_ref), highs, r_inner, places)
     a_ref[...] = restrict(projection_ref, live_ref, u)
-    agg = slots_ref.shape[1]
-    place = nodes_ref[...] & (agg - 1)
-    tall = iota((agg, LANES), 0)
+    place = nodes_ref[...] & (LANES - 1)
+    tall = iota((LANES, LANES), 0)
     for d in range(nodes_ref.shape[0]):
         hot = jnp.transpose(jnp.where(tall == place[d : d + 1], 1.0, 0.0))
         slots_ref[d * LANES : (d + 1) * LANES, :] = hot.astype(jnp.bfloat16)
@@ -259,33 +261,34 @@
 
 
 def solve_kernel(arrived_ref, nodes_ref, slots_ref, parts_ref, out_ref):
-    peers, agg = nodes_ref.shape[0], slots_ref.shape[1]
+    peers, agg = nodes_ref.shape[0], parts_ref.shape[0] // 4
     groups = parts_ref.shape[1] // (2 * agg)
     row = iota((8, LANES), 0)
-    block = nodes_ref[...] >> 6
-    total = jnp.zeros((16, agg), jnp.float32)
+    half = nodes_ref[...] >> 7
+    total = jnp.zeros((8, LANES), jnp.float32)
     span = 16
     for first in range(0, peers, span):
-        coarse_parts, fine_parts = [], []
+        spread = []
         for d in range(first, first + span):
             value = jnp.where(
-                row < 4,
+                (row & 2) == 0,
                 jnp.broadcast_to(arrived_ref[2 * d : 2 * d + 1, :], (8, LANES)),
                 jnp.broadcast_to(arrived_ref[2 * d + 1 : 2 * d + 2, :], (8, LANES)),
             )
-            value = jnp.where((row & 3) == block[d : d + 1], value, 0.0)
+            value = jnp.where((row & 1) == half[d : d + 1], value, 0.0)
             coarse = value.astype(jnp.bfloat16).astype(jnp.float32)
-            coarse_parts.append(coarse)
-            fine_parts.append(value - coarse)
-        spread = jnp.concatenate(
-            [jnp.concatenate(coarse_parts, 1), jnp.concatenate(fine_parts, 1)], 0
-        ).astype(jnp.bfloat16)
+            spread.append(jnp.where(row < 4, coarse, value - coarse))
         total = total + lax.dot_general(
-            spread, slots_ref[first * LANES : (first + span) * LANES, :],
+            jnp.concatenate(spread, 1).astype(jnp.bfloat16),
+            slots_ref[first * LANES : (first + span) * LANES, :],
             (((1,), (0,)), ((), ())), preferred_element_type=jnp.float32,
         )
-    g = total[:8] + total[8:]
-    vectors = jnp.concatenate([g, pltpu.roll(g, 4, 0)], 1)
+    g = total + pltpu.roll(total, 4, 0)
+    other = pltpu.roll(g, 2, 0)
+    low = iota((8, LANES), 1) < agg
+    evens = jnp.where(low, g, pltpu.roll(other, agg, 1))
+    odds = jnp.where(low, pltpu.roll(g, agg, 1), other)
+    vectors = jnp.where(row < 2, evens, pltpu.roll(odds, 2, 0))
     coarse = vectors.astype(jnp.bfloat16).astype(jnp.float32)
     fine = vectors - coarse
     sides = jnp.concatenate(
@@ -296,8 +299,8 @@
     )
     solved = solved[:8] + solved[8:]
     tables = [
-        jnp.broadcast_to(solved[b : b + 1, b * LANES : (b + 1) * LANES], (8, LANES))
-        for b in range(groups)
+        jnp.broadcast_to(solved[at : at + 1, b * LANES : (b + 1) * LANES], (8, LANES))
+        for b, at in enumerate((0, 2, 1, 3)[:groups])
     ]
     for first in range(0, peers, 8):
         here = nodes_ref[first : first + 8, :]
@@ -409,11 +412,9 @@
     r1_ref[:, last] = part_ref[:, last] - tail
 
 
-def local_call(kernel, outs, in_smem=(), in_place=False, scratch=(), sems=0, name=None):
+def local_call(kernel, outs, in_place=False, scratch=(), sems=0, name=None):
     def call(*args):
-        spaces = [pltpu.SMEM if i in in_smem else pltpu.VMEM for i in range(len(args))]
-        if in_place:
-            spaces = [pltpu.HBM] * len(args)
+        spaces = [pltpu.HBM if in_place else pltpu.VMEM] * len(args)
         shapes = [
             jax.ShapeDtypeStruct(*(o if isinstance(o[0], tuple) else (o, jnp.float32)))
             for o in outs
@@ -466,7 +467,6 @@
     rim = elem_count // 32
     peers = owner_counts.shape[1]
     cap = aux_node.shape[0] // peers
-    agg = aux_inverse.shape[1] // 2
     rows = -(-2 * (edge_count // LANES + 1) // 8) * 8
     live = element_live.reshape(1, elem_count)
     strip = lax.axis_index(("grp", "dom"))
@@ -476,11 +476,7 @@
     exists = jnp.where(lane < rim, jnp.where(is_last, 0.0, 1.0), jnp.where(strip == 0, 0.0, 1.0))
     exists = jnp.where(lane < 2 * rim, exists, 0.0)
     x_head, x_tail = x_edges[:, :LANES], x_edges[:, edge_count - LANES :]
-    ones = jnp.ones((2, LANES), jnp.float32)
-    via_odd, via_even = swap(
-        jnp.concatenate([jnp.where(strip % 2 == 0, x_head, x_tail), ones], 0),
-        jnp.concatenate([jnp.where(strip % 2 == 0, x_tail, x_head), ones], 0),
-    )
+    via_odd, via_even = swap(x_edges, jnp.where(strip % 2 == 0, x_tail, x_head))
     nodes = jnp.pad(aux_node.reshape(peers, cap), ((0, 0), (0, LANES - cap)))
     table = (rows, LANES)
     group = (8, LANES)
@@ -492,7 +488,7 @@
 
     arguments = (
         x_edges, x_inner, elem_edges, live, elem_matrix, jnp.transpose(projection, (1, 0, 2)),
-        b_edges, b_inner, w_edges, w_inner, aux_inverse,
+        b_edges, b_inner, w_edges, w_inner, aux_inverse, owner_counts,
     )
     *staged, by_moment, own, hot = local_call(
         functools.partial(stage_kernel, rim, len(arguments)),
@@ -500,27 +496,27 @@
         in_place=True, scratch=[table], sems=len(arguments), name="stage",
     )(*[pltpu.with_memory_space_constraint(v, pltpu.HBM) for v in arguments])
     x_edges, x_inner, elem_edges, live, elem_matrix, nodal_first = staged[:6]
-    b_edges, b_inner, w_edges, w_inner, aux_inverse = staged[6:]
+    b_edges, b_inner, w_edges, w_inner, aux_inverse, owner_counts = staged[6:]
     y, ends, odd_out, even_out = local_call(
         functools.partial(residual_kernel, rim), [moments, group, group, group], name="residual"
     )(
         even, via_odd, via_even, own, b_edges, w_edges, elem_edges, live, elem_matrix, hot
     )
     via_odd, via_even = swap(odd_out, even_out)
-    size = 2 * agg
+    size = aux_inverse.shape[1]
     r, r_inner, a, slots_hot, parts = local_call(
         functools.partial(partial_kernel, rim),
         [
-            table, inner, moments, ((peers * LANES, agg), jnp.bfloat16),
+            table, inner, moments, ((peers * LANES, LANES), jnp.bfloat16),
             ((2 * size, aux_inverse.shape[0] * size), jnp.bfloat16),
         ],
-        in_smem=(10,), name="partial",
+        name="partial",
     )(
-        y, b_edges, b_inner, elem_edges, live, by_moment, hot, nodes, aux_inverse, owner_counts
+        y, b_edges, b_inner, elem_edges, live, by_moment, hot, nodes, aux_inverse
     )
     r, s_rim, packed = local_call(
         functools.partial(restrict_kernel, rim, edge_count), [table, (2, LANES), slots],
-        in_smem=(10,), scratch=[lists], name="restrict",
+        scratch=[lists], name="restrict",
     )(
         even, via_odd, via_even, ends, exists, r, a, elem_edges, live, by_moment, owner_counts
     )
@@ -532,7 +528,7 @@
     returned = lax.all_to_all(outgoing, "dom", split_axis=0, concat_axis=0, tiled=True)
     p, ends, odd_out, even_out = local_call(
         functools.partial(prolong_kernel, rim, edge_count),
-        [moments, group, (4, LANES), (4, LANES)], in_smem=(5,), scratch=[lists], name="prolong",
+        [moments, group, (4, LANES), (4, LANES)], scratch=[lists], name="prolong",
     )(even, returned, elem_edges, live, nodal_first, owner_counts, hot)
     via_odd, via_even = swap(odd_out, even_out)
     z, x1_inner, az = local_call(

time: 103 us -> 102 us (level)
  transfers between devices with their start and end apart: 8 -> 8, of which waited for: 5 -> 5; matrix products, arithmetic and copies ran while one was open for 1% -> 2% of each run, Pallas kernels for 4% -> 4%
where the time goes in v4:
time: 102 us
  blocking collectives  40.5 us (40%)
  starting transfers between devices  40.2 us (39%)
  waiting for transfers between devices  10.7 us (10%)
  Pallas kernels  8.03 us (8%)
    ppermute x4, starting transfers between devices, swap(): lax.ppermute(odd, axis, pairs(1))  31.2 us
    all_to_all x1, blocking collectives, shards(): lax.all_to_all(packed, 'dom', split_axis=0, concat_axis=0, tiled=True)  21.6 us
    all_to_all x1, blocking collectives, shards(): lax.all_to_all(outgoing, 'dom', split_axis=0, concat_axis=0, tiled=True)  19 us
    ppermute x4, waiting for transfers between devices, swap(): lax.ppermute(odd, axis, pairs(1))  9.34 us
    ppermute x4, starting transfers between devices, swap(): lax.ppermute(even, axis, pairs(0))  9.08 us
    pallas_call x10, Pallas kernels, call(): pl.pallas_call(kernel, out_shape=shapes, in_specs=[pl.BlockSpec(memory_sp...  8.03 us
  transfers between devices with their start and end apart: 8, of which 5 were waited for; matrix products, arithmetic and copies ran while one was open for 2% of the time, Pallas kernels for 4%

profile of v4, /device:TPU:32, one launch (start us, length us, event | category | flops | bytes accessed | tf_op | source)
XLA Modules:
  0.0 101.8 jit_solution(8839175926479497460)
XLA Ops:
  0.6 19.7 %collective-permute-start = (f32[2,1536]{1,0:T(2,128)}, f32[2,1536]{1,0:T(2,128)S(1)}, u32[]{:S(2)}, u32[]{:S(2)}) collective-permute-start(f32[2,1536]{1,0:T(2,128)} %refs_0_.1), channel_id=1, source_target_pairs={{1,2},{3,4},{5,6},{7,8},{9,10},{11,12},{13,14},{15,16},{17,18},{19... | collective-permute-start | bytes 36872 | tf_op jit(solution)/shard_map/ppermute | solution.py:447
  20.4 0.7 slice_select_fusion
  21.1 1.9 %collective-permute-start.1 = (f32[2,128]{1,0:T(2,128)S(1)}, f32[2,128]{1,0:T(2,128)S(1)}, u32[]{:S(2)}, u32[]{:S(2)}) collective-permute-start(f32[2,128]{1,0:T(2,128)S(1)} %slice_select_fusion), channel_id=1, source_target_pairs={{0,1},{2,3},{4,5},{6,7},{8,9},{10,11},{12,13},{14,15},{16,17},{18,... | collective-permute-start | bytes 3080 | tf_op jit(solution)/shard_map/ppermute | solution.py:447
  23.1 1.5 %stage.1 = (f32[2,1536]{1,0:T(2,128)S(1)}, f32[2,1024]{1,0:T(2,128)S(1)}, s32[3,1024]{1,0:T(4,128)S(1)}, s32[1,1024]{1,0:T(1,128)S(1)}, f32[8,8,1024]{2,1,0:T(8,...) custom-call(f32[2,1536]{1,0:T(2,128)} %refs_0_.1, ...), custom_call_target="tpu_custom_call" | custom-call | flops 100000000 | bytes 2000000 | tf_op jit(solution)/shard_map/stage/pallas_call | solution.py:423
  24.6 0.8 reshape.21
  25.4 1.2 %collective-permute-done.1.via_even_ref = f32[2,128]{1,0:T(2,128)S(1)} collective-permute-done((f32[2,128]{1,0:T(2,128)S(1)}, f32[2,128]{1,0:T(2,128)S(1)}, u32[]{:S(2)}, u32[]{:S(2)}) %collective-permute-start.1) | collective-permute-done | bytes 1056 | tf_op jit(solution)/shard_map/ppermute | solution.py:447
  26.6 0.0 collective-permute-done.via_odd_ref
  26.6 0.4 residual.1
  27.0 4.5 %collective-permute-start.2 = (f32[8,128]{1,0:T(8,128)S(1)}, f32[8,128]{1,0:T(8,128)S(1)}, u32[]{:S(2)}, u32[]{:S(2)}) collective-permute-start(f32[8,128]{1,0:T(8,128)S(1)} %get-tuple-element.52), channel_id=1, source_target_pairs={{1,2},{3,4},{5,6},{7,8},{9,10},{11,12},{13,14},{15,16},{17,18},{19... | collective-permute-start | bytes 12296 | tf_op jit(solution)/shard_map/ppermute | solution.py:447
  31.5 1.9 %collective-permute-start.3 = (f32[8,128]{1,0:T(8,128)S(1)}, f32[8,128]{1,0:T(8,128)S(1)}, u32[]{:S(2)}, u32[]{:S(2)}) collective-permute-start(f32[8,128]{1,0:T(8,128)S(1)} %get-tuple-element.53), channel_id=1, source_target_pairs={{0,1},{2,3},{4,5},{6,7},{8,9},{10,11},{12,13},{14,15},{16,17},{18,... | collective-permute-start | bytes 12296 | tf_op jit(solution)/shard_map/ppermute | solution.py:447
  33.4 1.2 %partial.1 = (f32[32,128]{1,0:T(8,128)S(1)}, f32[2,1024]{1,0:T(2,128)S(1)}, f32[8,1024]{1,0:T(8,128)S(1)}, bf16[8192,128]{1,0:T(8,128)(2,1)S(1)}, bf16[256,512]{1,0:T(8,128)(2,1)S(1)}) custom-call(f32[8,1024]{1,0:T(8,128)S(1)} %get-tuple-element.55.y_ref, f32[2,1536]{1,0:T(2,128)S(1)} %get-tuple-element.46.b_ref, ...), custom_call_target="tpu_custom_call" | custom-call | flops 100000000 | bytes 2000000 | tf_op jit(solution)/shard_map/partial/pallas_call | solution.py:423
  34.6 2.8 %collective-permute-done.2.via_odd_ref = f32[8,128]{1,0:T(8,128)S(1)} collective-permute-done((f32[8,128]{1,0:T(8,128)S(1)}, f32[8,128]{1,0:T(8,128)S(1)}, u32[]{:S(2)}, u32[]{:S(2)}) %collective-permute-start.2) | collective-permute-done | bytes 4128 | tf_op jit(solution)/shard_map/ppermute | solution.py:447
  37.4 0.0 collective-permute-done.3.via_even_ref
  37.4 0.6 restrict.1
  37.9 21.6 %all_to_all.10 = f32[64,2,128]{2,1,0:T(2,128)S(1)} all-to-all(f32[64,2,128]{2,1,0:T(2,128)S(1)} %get-tuple-element.62), channel_id=1, replica_groups=mesh['grp'=16,'dom'=64] {'dom'}, dimensions={0} | all-to-all | bytes 131072 | tf_op jit(solution)/shard_map/all_to_all | solution.py:523
  59.5 0.8 solve.1
  60.3 19.0 %all_to_all.11.returned_ref = f32[64,2,128]{2,1,0:T(2,128)S(1)} all-to-all(f32[64,2,128]{2,1,0:T(2,128)S(1)} %bitcast.5), channel_id=1, replica_groups=mesh['grp'=16,'dom'=64] {'dom'}, dimensions={0} | all-to-all | bytes 131072 | tf_op jit(solution)/shard_map/all_to_all | solution.py:528
  79.3 0.6 prolong.1
  79.9 1.9 %collective-permute-start.4 = (f32[4,128]{1,0:T(4,128)S(1)}, f32[4,128]{1,0:T(4,128)S(1)}, u32[]{:S(2)}, u32[]{:S(2)}) collective-permute-start(f32[4,128]{1,0:T(4,128)S(1)} %get-tuple-element.66), channel_id=1, source_target_pairs={{1,2},{3,4},{5,6},{7,8},{9,10},{11,12},{13,14},{15,16},{17,18},{19... | collective-permute-start | bytes 6152 | tf_op jit(solution)/shard_map/ppermute | solution.py:447
  81.9 3.3 %collective-permute-start.5 = (f32[4,128]{1,0:T(4,128)S(1)}, f32[4,128]{1,0:T(4,128)S(1)}, u32[]{:S(2)}, u32[]{:S(2)}) collective-permute-start(f32[4,128]{1,0:T(4,128)S(1)} %get-tuple-element.67), channel_id=1, source_target_pairs={{0,1},{2,3},{4,5},{6,7},{8,9},{10,11},{12,13},{14,15},{16,17},{18,... | collective-permute-start | bytes 6152 | tf_op jit(solution)/shard_map/ppermute | solution.py:447
  85.2 1.1 %smooth.1 = (f32[32,128]{1,0:T(8,128)S(1)}, f32[2,1024]{1,0:T(2,128)}, f32[8,1024]{1,0:T(8,128)S(1)}) custom-call(f32[8,1024]{1,0:T(8,128)S(1)} %get-tuple-element.70.p_ref, f32[32,128]{1,0:T(8,128)S(1)} %get-tuple-element.71.r_ref, f32[2,1024]{1,0:T(2,128)S(1)} %get-tuple-element.72.r_inner_ref, f32[2,1024]{1,0:T(2,128)S(1)} %get-tuple-element.73.inner_ref, ...), custom_call_target="tpu_custom_call" | custom-call | flops 100000000 | bytes 2000000 | tf_op jit(solution)/shard_map/smooth/pallas_call | solution.py:423
  86.3 4.0 %collective-permute-done.4.via_odd_ref = f32[4,128]{1,0:T(4,128)S(1)} collective-permute-done((f32[4,128]{1,0:T(4,128)S(1)}, f32[4,128]{1,0:T(4,128)S(1)}, u32[]{:S(2)}, u32[]{:S(2)}) %collective-permute-start.4) | collective-permute-done | bytes 2080 | tf_op jit(solution)/shard_map/ppermute | solution.py:447
  90.3 0.0 collective-permute-done.5.via_even_ref
  90.3 0.4 update.1
  90.7 5.0 %collective-permute-start.6 = (f32[2,128]{1,0:T(2,128)S(1)}, f32[2,128]{1,0:T(2,128)S(1)}, u32[]{:S(2)}, u32[]{:S(2)}) collective-permute-start(f32[2,128]{1,0:T(2,128)S(1)} %get-tuple-element.83), channel_id=1, source_target_pairs={{1,2},{3,4},{5,6},{7,8},{9,10},{11,12},{13,14},{15,16},{17,18},{19... | collective-permute-start | bytes 3080 | tf_op jit(solution)/shard_map/ppermute | solution.py:447
  95.7 1.9 %collective-permute-start.7 = (f32[2,128]{1,0:T(2,128)S(1)}, f32[2,128]{1,0:T(2,128)S(1)}, u32[]{:S(2)}, u32[]{:S(2)}) collective-permute-start(f32[2,128]{1,0:T(2,128)S(1)} %get-tuple-element.84), channel_id=1, source_target_pairs={{0,1},{2,3},{4,5},{6,7},{8,9},{10,11},{12,13},{14,15},{16,17},{18,... | collective-permute-start | bytes 3080 | tf_op jit(solution)/shard_map/ppermute | solution.py:447
  97.6 0.8 output.1
  98.4 2.6 %collective-permute-done.6.via_odd_ref = f32[2,128]{1,0:T(2,128)S(1)} collective-permute-done((f32[2,128]{1,0:T(2,128)S(1)}, f32[2,128]{1,0:T(2,128)S(1)}, u32[]{:S(2)}, u32[]{:S(2)}) %collective-permute-start.6) | collective-permute-done | bytes 1056 | tf_op jit(solution)/shard_map/ppermute | solution.py:447
  101.0 0.1 collective-permute-done.7.via_even_ref
  101.1 0.7 finish.1
  (5 shorter events, 0.0 us)
Async XLA Ops:
  0.6 25.9 %collective-permute-start = (f32[2,1536]{1,0:T(2,128)}, f32[2,1536]{1,0:T(2,128)S(1)}, u32[]{:S(2)}, u32[]{:S(2)}) collective-permute-start(f32[2,1536]{1,0:T(2,128)} %refs_0_.1), channel_id=1, source_target_pairs={{1,2},{3,4},{5,6},{7,8},{9,10},{11,12},{13,14},{15,16},{17,18},{19... | collective-permute-start | bytes 36872 | tf_op jit(solution)/shard_map/ppermute | solution.py:447
  21.1 5.5 %collective-permute-start.1 = (f32[2,128]{1,0:T(2,128)S(1)}, f32[2,128]{1,0:T(2,128)S(1)}, u32[]{:S(2)}, u32[]{:S(2)}) collective-permute-start(f32[2,128]{1,0:T(2,128)S(1)} %slice_select_fusion), channel_id=1, source_target_pairs={{0,1},{2,3},{4,5},{6,7},{8,9},{10,11},{12,13},{14,15},{16,17},{18,... | collective-permute-start | bytes 3080 | tf_op jit(solution)/shard_map/ppermute | solution.py:447
  27.0 10.4 %collective-permute-start.2 = (f32[8,128]{1,0:T(8,128)S(1)}, f32[8,128]{1,0:T(8,128)S(1)}, u32[]{:S(2)}, u32[]{:S(2)}) collective-permute-start(f32[8,128]{1,0:T(8,128)S(1)} %get-tuple-element.52), channel_id=1, source_target_pairs={{1,2},{3,4},{5,6},{7,8},{9,10},{11,12},{13,14},{15,16},{17,18},{19... | collective-permute-start | bytes 12296 | tf_op jit(solution)/shard_map/ppermute | solution.py:447
  31.5 5.9 %collective-permute-start.3 = (f32[8,128]{1,0:T(8,128)S(1)}, f32[8,128]{1,0:T(8,128)S(1)}, u32[]{:S(2)}, u32[]{:S(2)}) collective-permute-start(f32[8,128]{1,0:T(8,128)S(1)} %get-tuple-element.53), channel_id=1, source_target_pairs={{0,1},{2,3},{4,5},{6,7},{8,9},{10,11},{12,13},{14,15},{16,17},{18,... | collective-permute-start | bytes 12296 | tf_op jit(solution)/shard_map/ppermute | solution.py:447
  79.9 10.3 %collective-permute-start.4 = (f32[4,128]{1,0:T(4,128)S(1)}, f32[4,128]{1,0:T(4,128)S(1)}, u32[]{:S(2)}, u32[]{:S(2)}) collective-permute-start(f32[4,128]{1,0:T(4,128)S(1)} %get-tuple-element.66), channel_id=1, source_target_pairs={{1,2},{3,4},{5,6},{7,8},{9,10},{11,12},{13,14},{15,16},{17,18},{19... | collective-permute-start | bytes 6152 | tf_op jit(solution)/shard_map/ppermute | solution.py:447
  81.9 8.4 %collective-permute-start.5 = (f32[4,128]{1,0:T(4,128)S(1)}, f32[4,128]{1,0:T(4,128)S(1)}, u32[]{:S(2)}, u32[]{:S(2)}) collective-permute-start(f32[4,128]{1,0:T(4,128)S(1)} %get-tuple-element.67), channel_id=1, source_target_pairs={{0,1},{2,3},{4,5},{6,7},{8,9},{10,11},{12,13},{14,15},{16,17},{18,... | collective-permute-start | bytes 6152 | tf_op jit(solution)/shard_map/ppermute | solution.py:447
  90.7 10.3 %collective-permute-start.6 = (f32[2,128]{1,0:T(2,128)S(1)}, f32[2,128]{1,0:T(2,128)S(1)}, u32[]{:S(2)}, u32[]{:S(2)}) collective-permute-start(f32[2,128]{1,0:T(2,128)S(1)} %get-tuple-element.83), channel_id=1, source_target_pairs={{1,2},{3,4},{5,6},{7,8},{9,10},{11,12},{13,14},{15,16},{17,18},{19... | collective-permute-start | bytes 3080 | tf_op jit(solution)/shard_map/ppermute | solution.py:447
  95.7 5.5 %collective-permute-start.7 = (f32[2,128]{1,0:T(2,128)S(1)}, f32[2,128]{1,0:T(2,128)S(1)}, u32[]{:S(2)}, u32[]{:S(2)}) collective-permute-start(f32[2,128]{1,0:T(2,128)S(1)} %get-tuple-element.84), channel_id=1, source_target_pairs={{0,1},{2,3},{4,5},{6,7},{8,9},{10,11},{12,13},{14,15},{16,17},{18,... | collective-permute-start | bytes 3080 | tf_op jit(solution)/shard_map/ppermute | solution.py:447

commit v5 on v4

--- a/solution.py
+++ b/solution.py
@@ -1,4 +1,5 @@
 import functools
+import math
 
 import jax
 import jax.numpy as jnp
@@ -174,10 +175,8 @@
     blocks = edge_count // LANES
     count = own_ref.shape[1]
     tail = slice(edge_count - LANES, edge_count)
-    heads, tails = via_odd_ref[:, :LANES], via_odd_ref[:, tail]
-    even = even_ref[0:2, :] > 0.5
-    left = jnp.where(even, tails, via_even_ref[...])
-    right = jnp.where(even, via_even_ref[...], heads)
+    left, _ = by_side(even_ref, via_odd_ref[:, tail], via_even_ref[:, tail])
+    _, right = by_side(even_ref, via_odd_ref[:, :LANES], via_even_ref[:, :LANES])
     none = jnp.zeros((2, LANES), jnp.float32)
     change = jnp.concatenate([none, none, rim_row(left, right, rim), none], 0)
     places = edge_places(edges_ref, rim, edge_count + 2 * rim)
@@ -192,9 +191,27 @@
     odd_ref[...], even_out_ref[...] = by_side(even_ref, to_left, to_right)
 
 
+def spread_lists(lists_ref, nodes_ref):
+    peers = nodes_ref.shape[0]
+    cap = lists_ref.shape[0] * LANES // peers
+    period = math.lcm(cap, LANES) // cap
+    rows = period * cap // LANES
+    lane = iota((peers // period, LANES), 1)
+    for d in range(period):
+        row, shift = divmod(d * cap, LANES)
+        back = (LANES - shift) % LANES
+        found = lists_ref[pl.ds(row, peers // period, stride=rows), :]
+        if shift:
+            found = pltpu.roll(found, back, 1)
+        if shift + cap > LANES:
+            more = lists_ref[pl.ds(row + 1, peers // period, stride=rows), :]
+            found = jnp.where(lane < back, found, pltpu.roll(more, back, 1))
+        nodes_ref[pl.ds(d, peers // period, stride=period), :] = found
+
+
 def partial_kernel(
-    rim, y_ref, b_ref, b_inner_ref, edges_ref, live_ref, projection_ref, hot_ref, nodes_ref,
-    inverse_ref, r_ref, r_inner_ref, a_ref, slots_ref, parts_ref,
+    rim, y_ref, b_ref, b_inner_ref, edges_ref, live_ref, projection_ref, hot_ref, lists_ref,
+    inverse_ref, r_ref, r_inner_ref, a_ref, slots_ref, parts_ref, nodes_ref,
 ):
     edge_count = b_ref.shape[1]
     blocks = edge_count // LANES
@@ -208,6 +225,7 @@
     r_inner_ref[...] = r_inner
     u = gather_moments(table_groups(r_ref), highs, r_inner, places)
     a_ref[...] = restrict(projection_ref, live_ref, u)
+    spread_lists(lists_ref, nodes_ref)
     place = nodes_ref[...] & (LANES - 1)
     tall = iota((LANES, LANES), 0)
     for d in range(nodes_ref.shape[0]):
@@ -444,7 +462,8 @@
         lows = range(first, count - 1, 2)
         return [(i, i + 1) for i in lows] + [(i + 1, i) for i in lows]
 
-    return lax.ppermute(odd, axis, pairs(1)), lax.ppermute(even, axis, pairs(0))
+    via_even = lax.ppermute(even, axis, pairs(0))
+    return lax.ppermute(odd, axis, pairs(1)), via_even
 
 
 def shards(
@@ -466,7 +485,6 @@
     elem_count = x_inner.shape[1]
     rim = elem_count // 32
     peers = owner_counts.shape[1]
-    cap = aux_node.shape[0] // peers
     rows = -(-2 * (edge_count // LANES + 1) // 8) * 8
     live = element_live.reshape(1, elem_count)
     strip = lax.axis_index(("grp", "dom"))
@@ -475,9 +493,7 @@
     is_last = strip == lax.axis_size(("grp", "dom")) - 1
     exists = jnp.where(lane < rim, jnp.where(is_last, 0.0, 1.0), jnp.where(strip == 0, 0.0, 1.0))
     exists = jnp.where(lane < 2 * rim, exists, 0.0)
-    x_head, x_tail = x_edges[:, :LANES], x_edges[:, edge_count - LANES :]
-    via_odd, via_even = swap(x_edges, jnp.where(strip % 2 == 0, x_tail, x_head))
-    nodes = jnp.pad(aux_node.reshape(peers, cap), ((0, 0), (0, LANES - cap)))
+    via_odd, via_even = swap(x_edges, x_edges)
     table = (rows, LANES)
     group = (8, LANES)
     inner = (2, elem_count)
@@ -489,6 +505,7 @@
     arguments = (
         x_edges, x_inner, elem_edges, live, elem_matrix, jnp.transpose(projection, (1, 0, 2)),
         b_edges, b_inner, w_edges, w_inner, aux_inverse, owner_counts,
+        aux_node.reshape(-1, LANES),
     )
     *staged, by_moment, own, hot = local_call(
         functools.partial(stage_kernel, rim, len(arguments)),
@@ -496,7 +513,7 @@
         in_place=True, scratch=[table], sems=len(arguments), name="stage",
     )(*[pltpu.with_memory_space_constraint(v, pltpu.HBM) for v in arguments])
     x_edges, x_inner, elem_edges, live, elem_matrix, nodal_first = staged[:6]
-    b_edges, b_inner, w_edges, w_inner, aux_inverse, owner_counts = staged[6:]
+    b_edges, b_inner, w_edges, w_inner, aux_inverse, owner_counts, aux_node = staged[6:]
     y, ends, odd_out, even_out = local_call(
         functools.partial(residual_kernel, rim), [moments, group, group, group], name="residual"
     )(
@@ -504,15 +521,15 @@
     )
     via_odd, via_even = swap(odd_out, even_out)
     size = aux_inverse.shape[1]
-    r, r_inner, a, slots_hot, parts = local_call(
+    r, r_inner, a, slots_hot, parts, nodes = local_call(
         functools.partial(partial_kernel, rim),
         [
             table, inner, moments, ((peers * LANES, LANES), jnp.bfloat16),
-            ((2 * size, aux_inverse.shape[0] * size), jnp.bfloat16),
+            ((2 * size, aux_inverse.shape[0] * size), jnp.bfloat16), ((peers, LANES), jnp.int32),
         ],
         name="partial",
     )(
-        y, b_edges, b_inner, elem_edges, live, by_moment, hot, nodes, aux_inverse
+        y, b_edges, b_inner, elem_edges, live, by_moment, hot, aux_node, aux_inverse
     )
     r, s_rim, packed = local_call(
         functools.partial(restrict_kernel, rim, edge_count), [table, (2, LANES), slots],

time: 102 us -> 102 us (level)
  transfers between devices with their start and end apart: 8 -> 8, of which waited for: 5 -> 5; matrix products, arithmetic and copies ran while one was open for 2% -> 0% of each run, Pallas kernels for 4% -> 4%
where the time goes in v5:
time: 102 us; the launch traced here: 101 us
  starting transfers between devices  40.6 us (40%)
  blocking collectives  40.5 us (40%)
  waiting for transfers between devices  11.5 us (11%)
  Pallas kernels  8 us (8%)
    ppermute x4, starting transfers between devices, swap(): return (lax.ppermute(odd, axis, pairs(1)), via_even)  31.5 us
    all_to_all x1, blocking collectives, shards(): lax.all_to_all(packed, 'dom', split_axis=0, concat_axis=0, tiled=True)  21.5 us
    all_to_all x1, blocking collectives, shards(): lax.all_to_all(outgoing, 'dom', split_axis=0, concat_axis=0, tiled=True)  19 us
    ppermute x4, starting transfers between devices, swap(): via_even = lax.ppermute(even, axis, pairs(0))  9.1 us
    ppermute x4, waiting for transfers between devices, swap(): return (lax.ppermute(odd, axis, pairs(1)), via_even)  9 us
    pallas_call x10, Pallas kernels, call(): pl.pallas_call(kernel, out_shape=shapes, in_specs=[pl.BlockSpec(memory_sp...  8 us
    ppermute x4, waiting for transfers between devices, swap(): via_even = lax.ppermute(even, axis, pairs(0))  2.48 us
  transfers between devices with their start and end apart: 8, of which 5 were waited for; matrix products, arithmetic and copies ran while one was open for 0% of the time, Pallas kernels for 4%

profile of v5, /device:TPU:32, one launch (start us, length us, event | category | flops | bytes accessed | tf_op | source)
XLA Modules:
  0.0 101.4 jit_solution(6348801006387591797)
XLA Ops:
  0.6 19.7 %collective-permute-start = (f32[2,1536]{1,0:T(2,128)}, f32[2,1536]{1,0:T(2,128)S(1)}, u32[]{:S(2)}, u32[]{:S(2)}) collective-permute-start(f32[2,1536]{1,0:T(2,128)} %refs_0_.1), channel_id=1, source_target_pairs={{1,2},{3,4},{5,6},{7,8},{9,10},{11,12},{13,14},{15,16},{17,18},{19... | collective-permute-start | bytes 36872 | tf_op jit(solution)/shard_map/ppermute | solution.py:466
  20.4 1.9 %collective-permute-start.1 = (f32[2,1536]{1,0:T(2,128)}, f32[2,1536]{1,0:T(2,128)S(1)}, u32[]{:S(2)}, u32[]{:S(2)}) collective-permute-start(f32[2,1536]{1,0:T(2,128)} %refs_0_.1), channel_id=1, source_target_pairs={{0,1},{2,3},{4,5},{6,7},{8,9},{10,11},{12,13},{14,15},{16,17},{18,... | collective-permute-start | bytes 36872 | tf_op jit(solution)/shard_map/ppermute | solution.py:465
  22.4 1.5 %stage.1 = (f32[2,1536]{1,0:T(2,128)S(1)}, f32[2,1024]{1,0:T(2,128)S(1)}, s32[3,1024]{1,0:T(4,128)S(1)}, s32[1,1024]{1,0:T(1,128)S(1)}, f32[8,8,1024]{2,1,0:T(8,...) custom-call(f32[2,1536]{1,0:T(2,128)} %refs_0_.1, ...), custom_call_target="tpu_custom_call" | custom-call | flops 100000000 | bytes 2000000 | tf_op jit(solution)/shard_map/stage/pallas_call | solution.py:441
  23.9 0.0 collective-permute-done.via_odd_ref
  23.9 2.3 %collective-permute-done.1.via_even_ref = f32[2,1536]{1,0:T(2,128)S(1)} collective-permute-done((f32[2,1536]{1,0:T(2,128)}, f32[2,1536]{1,0:T(2,128)S(1)}, u32[]{:S(2)}, u32[]{:S(2)}) %collective-permute-start.1) | collective-permute-done | bytes 12320 | tf_op jit(solution)/shard_map/ppermute | solution.py:465
  26.2 0.4 residual.1
  26.6 4.9 %collective-permute-start.2 = (f32[8,128]{1,0:T(8,128)S(1)}, f32[8,128]{1,0:T(8,128)S(1)}, u32[]{:S(2)}, u32[]{:S(2)}) collective-permute-start(f32[8,128]{1,0:T(8,128)S(1)} %get-tuple-element.54), channel_id=1, source_target_pairs={{1,2},{3,4},{5,6},{7,8},{9,10},{11,12},{13,14},{15,16},{17,18},{19... | collective-permute-start | bytes 12296 | tf_op jit(solution)/shard_map/ppermute | solution.py:466
  31.5 1.9 %collective-permute-start.3 = (f32[8,128]{1,0:T(8,128)S(1)}, f32[8,128]{1,0:T(8,128)S(1)}, u32[]{:S(2)}, u32[]{:S(2)}) collective-permute-start(f32[8,128]{1,0:T(8,128)S(1)} %get-tuple-element.55), channel_id=1, source_target_pairs={{0,1},{2,3},{4,5},{6,7},{8,9},{10,11},{12,13},{14,15},{16,17},{18,... | collective-permute-start | bytes 12296 | tf_op jit(solution)/shard_map/ppermute | solution.py:465
  33.4 1.1 %partial.1 = (f32[32,128]{1,0:T(8,128)S(1)}, f32[2,1024]{1,0:T(2,128)S(1)}, f32[8,1024]{1,0:T(8,128)S(1)}, bf16[8192,128]{1,0:T(8,128)(2,1)S(1)}, bf16[256,512]{1,0:T(8,128)(2,1)S(1)}, /*index=5*/s32[64,128]{1,0:T(8,128)S(1)}) custom-call(f32[8,1024]{1,0:T(8,128)S(1)} %get-tuple-element.57.y_ref, f32[2,1536]{1,0:T(2,128)S(1)} %get-tuple-element.48.b_ref, ...), custom_call_target="tpu_custom_call" | custom-call | flops 100000000 | bytes 2000000 | tf_op jit(solution)/shard_map/partial/pallas_call | solution.py:441
  34.6 2.4 %collective-permute-done.2.via_odd_ref = f32[8,128]{1,0:T(8,128)S(1)} collective-permute-done((f32[8,128]{1,0:T(8,128)S(1)}, f32[8,128]{1,0:T(8,128)S(1)}, u32[]{:S(2)}, u32[]{:S(2)}) %collective-permute-start.2) | collective-permute-done | bytes 4128 | tf_op jit(solution)/shard_map/ppermute | solution.py:466
  37.0 0.0 collective-permute-done.3.via_even_ref
  37.0 0.6 restrict.1
  37.6 21.5 %all_to_all.10 = f32[64,2,128]{2,1,0:T(2,128)S(1)} all-to-all(f32[64,2,128]{2,1,0:T(2,128)S(1)} %get-tuple-element.65), channel_id=1, replica_groups=mesh['grp'=16,'dom'=64] {'dom'}, dimensions={0} | all-to-all | bytes 131072 | tf_op jit(solution)/shard_map/all_to_all | solution.py:540
  59.1 0.8 solve.1
  60.0 19.0 %all_to_all.11.returned_ref = f32[64,2,128]{2,1,0:T(2,128)S(1)} all-to-all(f32[64,2,128]{2,1,0:T(2,128)S(1)} %bitcast.6), channel_id=1, replica_groups=mesh['grp'=16,'dom'=64] {'dom'}, dimensions={0} | all-to-all | bytes 131072 | tf_op jit(solution)/shard_map/all_to_all | solution.py:545
  78.9 0.6 prolong.1
  79.5 1.9 %collective-permute-start.4 = (f32[4,128]{1,0:T(4,128)S(1)}, f32[4,128]{1,0:T(4,128)S(1)}, u32[]{:S(2)}, u32[]{:S(2)}) collective-permute-start(f32[4,128]{1,0:T(4,128)S(1)} %get-tuple-element.70), channel_id=1, source_target_pairs={{1,2},{3,4},{5,6},{7,8},{9,10},{11,12},{13,14},{15,16},{17,18},{19... | collective-permute-start | bytes 6152 | tf_op jit(solution)/shard_map/ppermute | solution.py:466
  81.5 3.3 %collective-permute-start.5 = (f32[4,128]{1,0:T(4,128)S(1)}, f32[4,128]{1,0:T(4,128)S(1)}, u32[]{:S(2)}, u32[]{:S(2)}) collective-permute-start(f32[4,128]{1,0:T(4,128)S(1)} %get-tuple-element.71), channel_id=1, source_target_pairs={{0,1},{2,3},{4,5},{6,7},{8,9},{10,11},{12,13},{14,15},{16,17},{18,... | collective-permute-start | bytes 6152 | tf_op jit(solution)/shard_map/ppermute | solution.py:465
  84.8 1.1 %smooth.1 = (f32[32,128]{1,0:T(8,128)S(1)}, f32[2,1024]{1,0:T(2,128)}, f32[8,1024]{1,0:T(8,128)S(1)}) custom-call(f32[8,1024]{1,0:T(8,128)S(1)} %get-tuple-element.74.p_ref, f32[32,128]{1,0:T(8,128)S(1)} %get-tuple-element.75.r_ref, f32[2,1024]{1,0:T(2,128)S(1)} %get-tuple-element.76.r_inner_ref, f32[2,1024]{1,0:T(2,128)S(1)} %get-tuple-element.77.inner_ref, ...), custom_call_target="tpu_custom_call" | custom-call | flops 100000000 | bytes 2000000 | tf_op jit(solution)/shard_map/smooth/pallas_call | solution.py:441
  85.9 4.0 %collective-permute-done.4.via_odd_ref = f32[4,128]{1,0:T(4,128)S(1)} collective-permute-done((f32[4,128]{1,0:T(4,128)S(1)}, f32[4,128]{1,0:T(4,128)S(1)}, u32[]{:S(2)}, u32[]{:S(2)}) %collective-permute-start.4) | collective-permute-done | bytes 2080 | tf_op jit(solution)/shard_map/ppermute | solution.py:466
  89.9 0.0 collective-permute-done.5.via_even_ref
  89.9 0.4 update.1
  90.3 5.0 %collective-permute-start.6 = (f32[2,128]{1,0:T(2,128)S(1)}, f32[2,128]{1,0:T(2,128)S(1)}, u32[]{:S(2)}, u32[]{:S(2)}) collective-permute-start(f32[2,128]{1,0:T(2,128)S(1)} %get-tuple-element.87), channel_id=1, source_target_pairs={{1,2},{3,4},{5,6},{7,8},{9,10},{11,12},{13,14},{15,16},{17,18},{19... | collective-permute-start | bytes 3080 | tf_op jit(solution)/shard_map/ppermute | solution.py:466
  95.3 1.9 %collective-permute-start.7 = (f32[2,128]{1,0:T(2,128)S(1)}, f32[2,128]{1,0:T(2,128)S(1)}, u32[]{:S(2)}, u32[]{:S(2)}) collective-permute-start(f32[2,128]{1,0:T(2,128)S(1)} %get-tuple-element.88), channel_id=1, source_target_pairs={{0,1},{2,3},{4,5},{6,7},{8,9},{10,11},{12,13},{14,15},{16,17},{18,... | collective-permute-start | bytes 3080 | tf_op jit(solution)/shard_map/ppermute | solution.py:465
  97.2 0.8 output.1
  98.0 2.6 %collective-permute-done.6.via_odd_ref = f32[2,128]{1,0:T(2,128)S(1)} collective-permute-done((f32[2,128]{1,0:T(2,128)S(1)}, f32[2,128]{1,0:T(2,128)S(1)}, u32[]{:S(2)}, u32[]{:S(2)}) %collective-permute-start.6) | collective-permute-done | bytes 1056 | tf_op jit(solution)/shard_map/ppermute | solution.py:466
  100.6 0.1 collective-permute-done.7.via_even_ref
  100.8 0.7 finish.1
  (4 shorter events, 0.0 us)
Async XLA Ops:
  0.6 23.2 %collective-permute-start = (f32[2,1536]{1,0:T(2,128)}, f32[2,1536]{1,0:T(2,128)S(1)}, u32[]{:S(2)}, u32[]{:S(2)}) collective-permute-start(f32[2,1536]{1,0:T(2,128)} %refs_0_.1), channel_id=1, source_target_pairs={{1,2},{3,4},{5,6},{7,8},{9,10},{11,12},{13,14},{15,16},{17,18},{19... | collective-permute-start | bytes 36872 | tf_op jit(solution)/shard_map/ppermute | solution.py:466
  20.4 5.8 %collective-permute-start.1 = (f32[2,1536]{1,0:T(2,128)}, f32[2,1536]{1,0:T(2,128)S(1)}, u32[]{:S(2)}, u32[]{:S(2)}) collective-permute-start(f32[2,1536]{1,0:T(2,128)} %refs_0_.1), channel_id=1, source_target_pairs={{0,1},{2,3},{4,5},{6,7},{8,9},{10,11},{12,13},{14,15},{16,17},{18,... | collective-permute-start | bytes 36872 | tf_op jit(solution)/shard_map/ppermute | solution.py:465
  26.6 10.4 %collective-permute-start.2 = (f32[8,128]{1,0:T(8,128)S(1)}, f32[8,128]{1,0:T(8,128)S(1)}, u32[]{:S(2)}, u32[]{:S(2)}) collective-permute-start(f32[8,128]{1,0:T(8,128)S(1)} %get-tuple-element.54), channel_id=1, source_target_pairs={{1,2},{3,4},{5,6},{7,8},{9,10},{11,12},{13,14},{15,16},{17,18},{19... | collective-permute-start | bytes 12296 | tf_op jit(solution)/shard_map/ppermute | solution.py:466
  31.5 5.5 %collective-permute-start.3 = (f32[8,128]{1,0:T(8,128)S(1)}, f32[8,128]{1,0:T(8,128)S(1)}, u32[]{:S(2)}, u32[]{:S(2)}) collective-permute-start(f32[8,128]{1,0:T(8,128)S(1)} %get-tuple-element.55), channel_id=1, source_target_pairs={{0,1},{2,3},{4,5},{6,7},{8,9},{10,11},{12,13},{14,15},{16,17},{18,... | collective-permute-start | bytes 12296 | tf_op jit(solution)/shard_map/ppermute | solution.py:465
  79.5 10.3 %collective-permute-start.4 = (f32[4,128]{1,0:T(4,128)S(1)}, f32[4,128]{1,0:T(4,128)S(1)}, u32[]{:S(2)}, u32[]{:S(2)}) collective-permute-start(f32[4,128]{1,0:T(4,128)S(1)} %get-tuple-element.70), channel_id=1, source_target_pairs={{1,2},{3,4},{5,6},{7,8},{9,10},{11,12},{13,14},{15,16},{17,18},{19... | collective-permute-start | bytes 6152 | tf_op jit(solution)/shard_map/ppermute | solution.py:466
  81.5 8.4 %collective-permute-start.5 = (f32[4,128]{1,0:T(4,128)S(1)}, f32[4,128]{1,0:T(4,128)S(1)}, u32[]{:S(2)}, u32[]{:S(2)}) collective-permute-start(f32[4,128]{1,0:T(4,128)S(1)} %get-tuple-element.71), channel_id=1, source_target_pairs={{0,1},{2,3},{4,5},{6,7},{8,9},{10,11},{12,13},{14,15},{16,17},{18,... | collective-permute-start | bytes 6152 | tf_op jit(solution)/shard_map/ppermute | solution.py:465
  90.3 10.3 %collective-permute-start.6 = (f32[2,128]{1,0:T(2,128)S(1)}, f32[2,128]{1,0:T(2,128)S(1)}, u32[]{:S(2)}, u32[]{:S(2)}) collective-permute-start(f32[2,128]{1,0:T(2,128)S(1)} %get-tuple-element.87), channel_id=1, source_target_pairs={{1,2},{3,4},{5,6},{7,8},{9,10},{11,12},{13,14},{15,16},{17,18},{19... | collective-permute-start | bytes 3080 | tf_op jit(solution)/shard_map/ppermute | solution.py:466
  95.3 5.5 %collective-permute-start.7 = (f32[2,128]{1,0:T(2,128)S(1)}, f32[2,128]{1,0:T(2,128)S(1)}, u32[]{:S(2)}, u32[]{:S(2)}) collective-permute-start(f32[2,128]{1,0:T(2,128)S(1)} %get-tuple-element.88), channel_id=1, source_target_pairs={{0,1},{2,3},{4,5},{6,7},{8,9},{10,11},{12,13},{14,15},{16,17},{18,... | collective-permute-start | bytes 3080 | tf_op jit(solution)/shard_map/ppermute | solution.py:465

commit v6 on v5

--- a/solution.py
+++ b/solution.py
@@ -167,9 +167,53 @@
             by_moment_ref[rows, :] = projection_ref[n, :, at : at + LANES]
 
 
+def end_columns(place, blocks, rim):
+    high, low, _ = place
+    owned = jnp.where((high == blocks - 1) & (low >= LANES - rim), low, -1)
+    owned = jnp.where((high == 0) & (low < rim), low + 2 * rim, owned)
+    return jnp.where(high == blocks, low, owned)
+
+
+def couple_kernel(rim, edge_count, edges_ref, live_ref, matrix_ref, right_ref, left_ref):
+    blocks = edge_count // LANES
+    count = live_ref.shape[1]
+    places = edge_places(edges_ref, rim, edge_count + 2 * rim)
+    columns = [end_columns(place, blocks, rim) for place in places]
+    live = live_ref[...].astype(jnp.float32)
+    wide = iota((8, count), 0)
+    signs = jnp.ones((8, count), jnp.float32)
+    for k, (_, _, flip) in enumerate(places):
+        signs = jnp.where(wide == 2 * k, flip, signs)
+    tall = iota((LANES, count), 0)
+    total = jnp.zeros((LANES, 2 * LANES), jnp.float32)
+    for k in range(3):
+        blocks_of = {}
+        for c in range(2):
+            j = 2 * k + c
+            weights = matrix_ref[j] * signs * (signs[j : j + 1] * live)
+            for d in range(2):
+                for side in range(2):
+                    row = iota((rim, count), 0) + side * rim
+                    block = jnp.zeros((rim, count), jnp.float32)
+                    for m in range(3):
+                        weight = weights[2 * m + d : 2 * m + d + 1]
+                        block = block + jnp.where(row == columns[m], weight, 0.0)
+                    blocks_of[side, c, d] = block
+        rows = jnp.concatenate([blocks_of[key] for key in sorted(blocks_of)], 0)
+        coarse = rows.astype(jnp.bfloat16)
+        fine = (rows - coarse.astype(jnp.float32)).astype(jnp.bfloat16)
+        hot = jnp.where(tall == columns[k], 1.0, 0.0).astype(jnp.bfloat16)
+        for piece in (coarse, fine):
+            total = total + lax.dot_general(
+                hot, piece, (((1,), (1,)), ((), ())), preferred_element_type=jnp.float32
+            )
+    right_ref[...] = total[:, :LANES]
+    left_ref[...] = total[:, LANES:]
+
+
 def residual_kernel(
     rim, even_ref, via_odd_ref, via_even_ref, own_ref, b_ref, w_ref, edges_ref, live_ref,
-    matrix_ref, hot_ref, y_ref, ends_ref, odd_ref, even_out_ref,
+    matrix_ref, hot_ref, to_right_ref, to_left_ref, y_ref, ends_ref, odd_ref, even_out_ref,
 ):
     edge_count = b_ref.shape[1]
     blocks = edge_count // LANES
@@ -188,7 +232,12 @@
     ends_ref[...] = ends
     to_left = jnp.concatenate([ends[0:2], ends[4:6], b_ref[:, :LANES], w_ref[:, :LANES]], 0)
     to_right = jnp.concatenate([ends[2:4], ends[4:6], b_ref[:, tail], w_ref[:, tail]], 0)
-    odd_ref[...], even_out_ref[...] = by_side(even_ref, to_left, to_right)
+    odd_ref[0:8, :], even_out_ref[0:8, :] = by_side(even_ref, to_left, to_right)
+    for at in range(0, LANES, 8):
+        rows, there = slice(at, at + 8), slice(at + 8, at + 16)
+        odd_ref[there, :], even_out_ref[there, :] = by_side(
+            even_ref, to_left_ref[rows, :], to_right_ref[rows, :]
+        )
 
 
 def spread_lists(lists_ref, nodes_ref):
@@ -245,7 +294,7 @@
 ):
     blocks = edge_count // LANES
     count = a_ref.shape[1]
-    left, right = by_side(even_ref, via_odd_ref[...], via_even_ref[...])
+    left, right = by_side(even_ref, via_odd_ref[0:8, :], via_even_ref[0:8, :])
     head, tail = arrivals(left[2:4], right[2:4], rim)
     exists = exists_ref[...]
     settled = ends_ref[4:6, :] + rim_row(left[0:2], right[0:2], rim)
@@ -332,10 +381,15 @@
 
 
 def prolong_kernel(
-    rim, edge_count, even_ref, returned_ref, edges_ref, live_ref, projection_ref, counts_ref,
-    hot_ref, p_ref, ends_ref, odd_ref, even_out_ref, vals_ref,
+    rim, even_ref, low_ref, returned_ref, edges_ref, live_ref, projection_ref, counts_ref,
+    hot_ref, exists_ref, s_rim_ref, r_ref, r_inner_ref, w_ref, w_inner_ref, matrix_ref,
+    z_ref, z_inner_ref, y_ref, ends_ref, two_high_ref, odd_ref, two_low_ref, even_out_ref,
+    vals_ref,
 ):
     count = live_ref.shape[1]
+    edge_count = w_ref.shape[1]
+    blocks = edge_count // LANES
+    last = 2 * blocks - 2
     lane = iota((2, LANES), 1)
     start = jnp.int32(0)
     for q in range(returned_ref.shape[0]):
@@ -351,83 +405,100 @@
     for n in range(1, 6):
         p = p + projection_ref[n] * nodal[n : n + 1]
     p = p * live_ref[...].astype(jnp.float32)
-    p_ref[...] = p
-    places = edge_places(edges_ref, rim, edge_count + 2 * rim)
-    ends = scatter_moments(p, places, hot_ref, end_highs(edge_count // LANES))
+    places = edge_places(edges_ref, rim, edge_count + 2 * rim)
+    highs = row_highs(blocks)
+    total = scatter_moments(p, places, hot_ref, highs)
+    none = jnp.zeros((2, LANES), jnp.float32)
+    ends = jnp.concatenate([total[0:2], total[last : last + 4], none], 0)
     ends_ref[...] = ends
-    to_left = jnp.concatenate([ends[0:2], ends[4:6]], 0)
-    to_right = jnp.concatenate([ends[2:4], ends[4:6]], 0)
+    load_table(z_ref, w_ref)
+    row = iota(total.shape, 0)
+    z_ref[...] = z_ref[...] * r_ref[...] + jnp.where(row < 2 * blocks, total, 0.0)
+    z_ref[last + 2 : last + 4, :] = s_rim_ref[...] + exists_ref[...] * ends[4:6]
+    z_inner = w_inner_ref[...] * r_inner_ref[...] + p[6:8]
+    z_inner_ref[...] = z_inner
+    u = gather_moments(table_groups(z_ref), highs, z_inner, places)
+    y = apply_matrix(matrix_ref, live_ref, u)
+    y_ref[...] = y
+    rims = scatter_moments(y, places, hot_ref, end_highs(blocks))[4:6]
+    to_left = jnp.concatenate([ends[0:2], ends[4:6], rims, none], 0)
+    to_right = jnp.concatenate([ends[2:4], ends[4:6], rims, none], 0)
     odd_ref[...], even_out_ref[...] = by_side(even_ref, to_left, to_right)
-
-
-def smooth_kernel(
-    rim, p_ref, r_ref, r_inner_ref, inner_ref, w_ref, w_inner_ref, edges_ref, live_ref,
-    matrix_ref, hot_ref, z_ref, x1_inner_ref, y_ref,
+    two_high_ref[...], two_low_ref[...] = by_side(low_ref, to_left, to_right)
+
+
+def output_kernel(
+    rim, y_ref, z_inner_ref, r_ref, inner_ref, w_ref, edges_ref, hot_ref, x1_inner_ref, part_ref
 ):
     edge_count = w_ref.shape[1]
-    blocks = edge_count // LANES
-    places = edge_places(edges_ref, rim, edge_count + 2 * rim)
-    highs = row_highs(blocks)
-    total = scatter_moments(p_ref[...], places, hot_ref, highs)
-    row = iota(total.shape, 0)
-    load_table(z_ref, w_ref)
-    z_ref[...] = z_ref[...] * r_ref[...] + jnp.where(row < 2 * blocks, total, 0.0)
-    z_inner = w_inner_ref[...] * r_inner_ref[...] + p_ref[6:8, :]
-    x1_inner_ref[...] = inner_ref[...] + z_inner
-    u = gather_moments(table_groups(z_ref), highs, z_inner, places)
-    y_ref[...] = apply_matrix(matrix_ref, live_ref, u)
-
-
-def update_kernel(
-    rim, edge_count, even_ref, via_odd_ref, via_even_ref, ends_ref, exists_ref, s_rim_ref,
-    part_ref, edges_ref, live_ref, matrix_ref, hot_ref, y_ref, change_ref, odd_ref, even_out_ref,
-):
-    count = part_ref.shape[1]
-    left, right = by_side(even_ref, via_odd_ref[...], via_even_ref[...])
-    head, tail = arrivals(left[2:4], right[2:4], rim)
-    settled = ends_ref[4:6, :] + rim_row(left[0:2], right[0:2], rim)
-    z_rim = s_rim_ref[...] + exists_ref[...] * settled
-    change = jnp.concatenate([head, tail, z_rim, jnp.zeros((2, LANES), jnp.float32)], 0)
-    change_ref[...] = change
-    places = edge_places(edges_ref, rim, edge_count + 2 * rim)
-    highs = end_highs(edge_count // LANES)
-    u = gather_moments([change], highs, jnp.zeros((2, count), jnp.float32), places)
-    y = part_ref[...] + apply_matrix(matrix_ref, live_ref, u)
-    y_ref[...] = y
-    rims = scatter_moments(y, places, hot_ref, highs)[4:6]
-    odd_ref[...] = rims
-    even_out_ref[...] = rims
-
-
-def output_kernel(
-    rim, y_ref, change_ref, z_ref, r_ref, r_inner_ref, x_ref, edges_ref, hot_ref,
-    x1_ref, r1_ref, r1_inner_ref,
+    x1_inner_ref[...] = inner_ref[...] + z_inner_ref[...]
+    places = edge_places(edges_ref, rim, edge_count + 2 * rim)
+    total = scatter_moments(y_ref[...], places, hot_ref, row_highs(edge_count // LANES))
+    part_ref[...] = r_ref[...] - total
+
+
+def coupled(change, coupling, rim):
+    rows = jnp.concatenate([change, jnp.zeros((6, LANES), jnp.float32)], 0)
+    found = lax.dot_general(
+        rows, coupling, (((1,), (0,)), ((), ())),
+        precision=lax.Precision.HIGHEST, preferred_element_type=jnp.float32,
+    )
+    return found[0:1] + pltpu.roll(found[1:2], 64, 1)
+
+
+def finish_kernel(
+    rim, via_two_low_ref, via_two_high_ref, via_odd_ref, via_even_ref, even_ref, low_ref,
+    odd_before_ref, even_before_ref, ends_ref, exists_ref, z_ref, y_ref, part_ref, x_ref,
+    r_inner_ref, edges_ref, live_ref, matrix_ref, hot_ref, x1_ref, r1_ref, r1_inner_ref,
 ):
     edge_count = x_ref.shape[1]
+    count = y_ref.shape[1]
     blocks = edge_count // LANES
-    places = edge_places(edges_ref, rim, edge_count + 2 * rim)
-    total = scatter_moments(y_ref[...], places, hot_ref, row_highs(blocks))
-    r1_inner_ref[...] = r_inner_ref[...] - y_ref[6:8, :]
+    left, right = by_side(even_ref, via_odd_ref[...], via_even_ref[...])
+    left_two, right_two = by_side(low_ref, via_two_high_ref[...], via_two_low_ref[...])
+    head, tail = arrivals(left[2:4], right[2:4], rim)
+    z_rim = exists_ref[...] * rim_row(left[0:2], right[0:2], rim)
+    change = jnp.concatenate([head, tail, z_rim, jnp.zeros((2, LANES), jnp.float32)], 0)
+    places = edge_places(edges_ref, rim, edge_count + 2 * rim)
+    u = gather_moments(
+        [change], end_highs(blocks), jnp.zeros((2, count), jnp.float32), places
+    )
+    more = apply_matrix(matrix_ref, live_ref, u)
+    r1_inner_ref[...] = r_inner_ref[...] - (y_ref[6:8, :] + more[6:8])
+    total = scatter_moments(more, places, hot_ref, row_highs(blocks))
+
+    ends = ends_ref[...]
+    lane = iota((2, LANES), 1)
+
+    def columns(first, second, third, fourth):
+        turned = [pltpu.roll(v, 64, 1) for v in (second, third, fourth)]
+        latter = jnp.where(lane < 3 * rim, turned[1], turned[2])
+        return jnp.where(lane < rim, first, jnp.where(lane < 2 * rim, turned[0], latter))
+
+    unknown_left = columns(ends[0:2], left_two[0:2], left_two[2:4], ends[4:6])
+    unknown_right = columns(right_two[0:2], ends[2:4], ends[4:6], right_two[2:4])
+    is_even = even_ref[0:1, :] > 0.5
+    odd_before, even_before = odd_before_ref[8:, :], even_before_ref[8:, :]
+    from_left = coupled(unknown_left, jnp.where(is_even, odd_before, even_before), rim)
+    from_right = coupled(unknown_right, jnp.where(is_even, even_before, odd_before), rim)
+    head_sum, tail_sum = arrivals(left[4:6], right[4:6], rim)
+    add_head = jnp.concatenate([from_left, pltpu.roll(from_left, LANES - rim, 1)], 0)
+    add_tail = jnp.concatenate(
+        [pltpu.roll(from_right, LANES - rim, 1), pltpu.roll(from_right, LANES - 2 * rim, 1)], 0
+    )
+    head_sum = head_sum + jnp.where(lane < rim, add_head, 0.0)
+    tail_sum = tail_sum + jnp.where(lane >= LANES - rim, add_tail, 0.0)
     for h in range(blocks):
         here = slice(h * LANES, (h + 1) * LANES)
         rows = slice(2 * h, 2 * h + 2)
         z = z_ref[rows, :]
+        r1 = part_ref[rows, :] - total[rows]
         if h == 0:
-            z = z + change_ref[0:2, :]
+            z, r1 = z + head, r1 - head_sum
         if h == blocks - 1:
-            z = z + change_ref[2:4, :]
+            z, r1 = z + tail, r1 - tail_sum
         x1_ref[:, here] = x_ref[:, here] + z
-        r1_ref[:, here] = r_ref[rows, :] - total[rows]
-
-
-def finish_kernel(rim, even_ref, part_ref, via_odd_ref, via_even_ref, r1_ref):
-    edge_count = part_ref.shape[1]
-    left, right = by_side(even_ref, via_odd_ref[...], via_even_ref[...])
-    head, tail = arrivals(left, right, rim)
-    last = slice(edge_count - LANES, edge_count)
-    r1_ref[...] = part_ref[...]
-    r1_ref[:, :LANES] = part_ref[:, :LANES] - head
-    r1_ref[:, last] = part_ref[:, last] - tail
+        r1_ref[:, here] = r1
 
 
 def local_call(kernel, outs, in_place=False, scratch=(), sems=0, name=None):
@@ -454,16 +525,15 @@
     return call
 
 
-def swap(odd, even):
-    axis = ("grp", "dom")
-    count = lax.axis_size(axis)
-
-    def pairs(first):
-        lows = range(first, count - 1, 2)
-        return [(i, i + 1) for i in lows] + [(i + 1, i) for i in lows]
-
-    via_even = lax.ppermute(even, axis, pairs(0))
-    return lax.ppermute(odd, axis, pairs(1)), via_even
+def swap(message, lows):
+    pairs = [pair for low, high in lows for pair in ((low, high), (high, low))]
+    return lax.ppermute(message, ("grp", "dom"), pairs)
+
+
+def strip_pairs(gap, first):
+    count = lax.axis_size(("grp", "dom"))
+    lows = [i for i in range(count - gap) if (i - first) % (2 * gap) < gap]
+    return [(i, i + gap) for i in lows]
 
 
 def shards(
@@ -493,7 +563,10 @@
     is_last = strip == lax.axis_size(("grp", "dom")) - 1
     exists = jnp.where(lane < rim, jnp.where(is_last, 0.0, 1.0), jnp.where(strip == 0, 0.0, 1.0))
     exists = jnp.where(lane < 2 * rim, exists, 0.0)
-    via_odd, via_even = swap(x_edges, x_edges)
+    odd, evens = strip_pairs(1, 1), strip_pairs(1, 0)
+    low = jnp.where(strip % 4 < 2, jnp.ones((8, LANES), jnp.float32), 0.0)
+    via_even = swap(x_edges, evens)
+    via_odd = swap(x_edges, odd)
     table = (rows, LANES)
     group = (8, LANES)
     inner = (2, elem_count)
@@ -514,12 +587,20 @@
     )(*[pltpu.with_memory_space_constraint(v, pltpu.HBM) for v in arguments])
     x_edges, x_inner, elem_edges, live, elem_matrix, nodal_first = staged[:6]
     b_edges, b_inner, w_edges, w_inner, aux_inverse, owner_counts, aux_node = staged[6:]
+    square = (LANES, LANES)
+    to_right, to_left = local_call(
+        functools.partial(couple_kernel, rim, edge_count), [square, square], name="couple"
+    )(elem_edges, live, elem_matrix)
+    message = (8 + LANES, LANES)
     y, ends, odd_out, even_out = local_call(
-        functools.partial(residual_kernel, rim), [moments, group, group, group], name="residual"
+        functools.partial(residual_kernel, rim), [moments, group, message, message],
+        name="residual",
     )(
-        even, via_odd, via_even, own, b_edges, w_edges, elem_edges, live, elem_matrix, hot
-    )
-    via_odd, via_even = swap(odd_out, even_out)
+        even, via_odd, via_even, own, b_edges, w_edges, elem_edges, live, elem_matrix, hot,
+        to_right, to_left,
+    )
+    even_before = swap(even_out, evens)
+    odd_before = swap(odd_out, odd)
     size = aux_inverse.shape[1]
     r, r_inner, a, slots_hot, parts, nodes = local_call(
         functools.partial(partial_kernel, rim),
@@ -535,7 +616,7 @@
         functools.partial(restrict_kernel, rim, edge_count), [table, (2, LANES), slots],
         scratch=[lists], name="restrict",
     )(
-        even, via_odd, via_even, ends, exists, r, a, elem_edges, live, by_moment, owner_counts
+        even, odd_before, even_before, ends, exists, r, a, elem_edges, live, by_moment, owner_counts
     )
     arrived = lax.all_to_all(packed, "dom", split_axis=0, concat_axis=0, tiled=True)
     (outgoing,) = local_call(solve_kernel, [(2 * peers, LANES)], name="solve")(
@@ -543,28 +624,27 @@
     )
     outgoing = outgoing.reshape(slots)
     returned = lax.all_to_all(outgoing, "dom", split_axis=0, concat_axis=0, tiled=True)
-    p, ends, odd_out, even_out = local_call(
-        functools.partial(prolong_kernel, rim, edge_count),
-        [moments, group, (4, LANES), (4, LANES)], scratch=[lists], name="prolong",
-    )(even, returned, elem_edges, live, nodal_first, owner_counts, hot)
-    via_odd, via_even = swap(odd_out, even_out)
-    z, x1_inner, az = local_call(
-        functools.partial(smooth_kernel, rim), [table, inner, moments], name="smooth"
-    )(p, r, r_inner, x_inner, w_edges, w_inner, elem_edges, live, elem_matrix, hot)
-    az, change, odd_out, even_out = local_call(
-        functools.partial(update_kernel, rim, edge_count),
-        [moments, group, (2, LANES), (2, LANES)], name="update",
+    z, z_inner, az, ends, two_high, odd_out, two_low, even_out = local_call(
+        functools.partial(prolong_kernel, rim),
+        [table, inner, moments, group, group, group, group, group],
+        scratch=[lists], name="prolong",
     )(
-        even, via_odd, via_even, ends, exists, s_rim, az, elem_edges, live, elem_matrix, hot
-    )
-    via_odd, via_even = swap(odd_out, even_out)
-    x1_edges, r1_part, r1_inner = local_call(
-        functools.partial(output_kernel, rim), [x_edges.shape, x_edges.shape, inner],
-        name="output",
-    )(az, change, z, r, r_inner, x_edges, elem_edges, hot)
-    (r1_edges,) = local_call(
-        functools.partial(finish_kernel, rim), [x_edges.shape], name="finish"
-    )(even, r1_part, via_odd, via_even)
+        even, low, returned, elem_edges, live, nodal_first, owner_counts, hot, exists, s_rim, r,
+        r_inner, w_edges, w_inner, elem_matrix,
+    )
+    via_even = swap(even_out, evens)
+    via_two_low = swap(two_low, strip_pairs(2, 0))
+    via_odd = swap(odd_out, odd)
+    via_two_high = swap(two_high, strip_pairs(2, 2))
+    x1_inner, part = local_call(
+        functools.partial(output_kernel, rim), [inner, table], name="output"
+    )(az, z_inner, r, x_inner, w_edges, elem_edges, hot)
+    x1_edges, r1_edges, r1_inner = local_call(
+        functools.partial(finish_kernel, rim), [x_edges.shape, x_edges.shape, inner], name="finish"
+    )(
+        via_two_low, via_two_high, via_odd, via_even, even, low, odd_before, even_before, ends,
+        exists, z, az, part, x_edges, r_inner, elem_edges, live, elem_matrix, hot,
+    )
     return x1_edges, x1_inner, r1_edges, r1_inner
 
 

time: 102 us -> 103 us (level)
  blocking collectives: 40.5 us -> 21.6 us
  waiting for transfers between devices: 11.5 us -> 21.6 us
  starting transfers between devices: 40.6 us -> 48.8 us
  Pallas kernels: 8 us -> 10.1 us
    all_to_all x1 -> x0, blocking collectives: 19 us -> none  [shards(): lax.all_to_all(outgoing, 'dom', split_axis=0, concat_axis=0, tiled=True)]
    all_to_all x0 -> x1, waiting for transfers between devices: none -> 15.1 us  [shards(): lax.all_to_all(outgoing, 'dom', split_axis=0, concat_axis=0, tiled=True)]
    ppermute x8, waiting for transfers between devices: 11.5 us -> 6.49 us  [swap(): return lax.ppermute(message, ('grp', 'dom'), pairs)]
    all_to_all x0 -> x1, starting transfers between devices: none -> 4.6 us  [shards(): lax.all_to_all(outgoing, 'dom', split_axis=0, concat_axis=0, tiled=True)]
    ppermute x8, starting transfers between devices: 40.6 us -> 44.2 us  [swap(): return lax.ppermute(message, ('grp', 'dom'), pairs)]
    pallas_call x10 -> x9, Pallas kernels: 8 us -> 10.1 us  [call(): pl.pallas_call(kernel, out_shape=shapes, in_specs=[pl.BlockSpec(memory_sp...]
  transfers between devices with their start and end apart: 8 -> 9, of which waited for: 5 -> 4; matrix products, arithmetic and copies ran while one was open for 0% -> 0% of each run, Pallas kernels for 4% -> 5%
where the time goes in v6:
time: 103 us
  starting transfers between devices  48.8 us (47%)
  waiting for transfers between devices  21.6 us (21%)
  blocking collectives  21.6 us (21%)
  Pallas kernels  10.1 us (10%)
    ppermute x8, starting transfers between devices, swap(): return lax.ppermute(message, ('grp', 'dom'), pairs)  44.2 us
    all_to_all x1, blocking collectives, shards(): lax.all_to_all(packed, 'dom', split_axis=0, concat_axis=0, tiled=True)  21.6 us
    all_to_all x1, waiting for transfers between devices, shards(): lax.all_to_all(outgoing, 'dom', split_axis=0, concat_axis=0, tiled=True)  15.1 us
    pallas_call x9, Pallas kernels, call(): pl.pallas_call(kernel, out_shape=shapes, in_specs=[pl.BlockSpec(memory_sp...  10.1 us
    ppermute x8, waiting for transfers between devices, swap(): return lax.ppermute(message, ('grp', 'dom'), pairs)  6.49 us
    all_to_all x1, starting transfers between devices, shards(): lax.all_to_all(outgoing, 'dom', split_axis=0, concat_axis=0, tiled=True)  4.6 us
  transfers between devices with their start and end apart: 9, of which 4 were waited for; matrix products, arithmetic and copies ran while one was open for 0% of the time, Pallas kernels for 5%

profile of v6, /device:TPU:32, one launch (start us, length us, event | category | flops | bytes accessed | tf_op | source)
XLA Modules:
  0.0 103.0 jit_solution(2106407432388629921)
XLA Ops:
  0.6 19.7 %collective-permute-start = (f32[2,1536]{1,0:T(2,128)}, f32[2,1536]{1,0:T(2,128)S(1)}, u32[]{:S(2)}, u32[]{:S(2)}) collective-permute-start(f32[2,1536]{1,0:T(2,128)} %refs_0_.1), channel_id=1, source_target_pairs={{1,2},{2,1},{3,4},{4,3},{5,6},{6,5},{7,8},{8,7},{9,10},{10,9},{11,... | collective-permute-start | bytes 36872 | tf_op jit(solution)/shard_map/ppermute | solution.py:530
  20.4 1.9 %collective-permute-start.1 = (f32[2,1536]{1,0:T(2,128)}, f32[2,1536]{1,0:T(2,128)S(1)}, u32[]{:S(2)}, u32[]{:S(2)}) collective-permute-start(f32[2,1536]{1,0:T(2,128)} %refs_0_.1), channel_id=1, source_target_pairs={{0,1},{1,0},{2,3},{3,2},{4,5},{5,4},{6,7},{7,6},{8,9},{9,8},{10,11... | collective-permute-start | bytes 36872 | tf_op jit(solution)/shard_map/ppermute | solution.py:530
  22.4 1.5 %stage.1 = (f32[2,1536]{1,0:T(2,128)S(1)}, f32[2,1024]{1,0:T(2,128)S(1)}, s32[3,1024]{1,0:T(4,128)S(1)}, s32[1,1024]{1,0:T(1,128)S(1)}, f32[8,8,1024]{2,1,0:T(8,...) custom-call(f32[2,1536]{1,0:T(2,128)} %refs_0_.1, ...), custom_call_target="tpu_custom_call" | custom-call | flops 100000000 | bytes 2000000 | tf_op jit(solution)/shard_map/stage/pallas_call | solution.py:512
  23.9 1.7 %couple.1 = (f32[128,128]{1,0:T(8,128)S(1)}, f32[128,128]{1,0:T(8,128)S(1)}) custom-call(s32[3,1024]{1,0:T(4,128)S(1)} %get-tuple-element.51.edges_ref, s32[1,1024]{1,0:T(1,128)S(1)} %get-tuple-element.52.live_ref, f32[8,8,1024]{2,1,0:T(8,128)S(1)} %get-tuple-element.53.matrix_ref), custom_call_target="tpu_custom_call" | custom-call | flops 100000000 | bytes 2000000 | tf_op jit(solution)/shard_map/couple/pallas_call | solution.py:512
  25.6 0.0 collective-permute-done.via_odd_ref
  25.6 0.6 collective-permute-done.1.via_even_ref
  26.2 0.4 residual.1
  26.6 4.9 %collective-permute-start.2 = (f32[136,128]{1,0:T(8,128)S(1)}, f32[136,128]{1,0:T(8,128)S(1)}, u32[]{:S(2)}, u32[]{:S(2)}) collective-permute-start(f32[136,128]{1,0:T(8,128)S(1)} %get-tuple-element.57), channel_id=1, source_target_pairs={{1,2},{2,1},{3,4},{4,3},{5,6},{6,5},{7,8},{8,7},{9,10},{10,9},{11,... | collective-permute-start | bytes 208904 | tf_op jit(solution)/shard_map/ppermute | solution.py:530
  31.5 1.9 %collective-permute-start.3 = (f32[136,128]{1,0:T(8,128)S(1)}, f32[136,128]{1,0:T(8,128)S(1)}, u32[]{:S(2)}, u32[]{:S(2)}) collective-permute-start(f32[136,128]{1,0:T(8,128)S(1)} %get-tuple-element.58), channel_id=1, source_target_pairs={{0,1},{1,0},{2,3},{3,2},{4,5},{5,4},{6,7},{7,6},{8,9},{9,8},{10,11... | collective-permute-start | bytes 208904 | tf_op jit(solution)/shard_map/ppermute | solution.py:530
  33.4 1.1 %partial.1 = (f32[32,128]{1,0:T(8,128)S(1)}, f32[2,1024]{1,0:T(2,128)S(1)}, f32[8,1024]{1,0:T(8,128)S(1)}, bf16[8192,128]{1,0:T(8,128)(2,1)S(1)}, bf16[256,512]{1,0:T(8,128)(2,1)S(1)}, /*index=5*/s32[64,128]{1,0:T(8,128)S(1)}) custom-call(f32[8,1024]{1,0:T(8,128)S(1)} %get-tuple-element.60.y_ref, f32[2,1536]{1,0:T(2,128)S(1)} %get-tuple-element.49.b_ref, ...), custom_call_target="tpu_custom_call" | custom-call | flops 100000000 | bytes 2000000 | tf_op jit(solution)/shard_map/partial/pallas_call | solution.py:512
  34.6 3.1 %collective-permute-done.2.via_odd_ref.odd_before_ref = f32[136,128]{1,0:T(8,128)S(1)} collective-permute-done((f32[136,128]{1,0:T(8,128)S(1)}, f32[136,128]{1,0:T(8,128)S(1)}, u32[]{:S(2)}, u32[]{:S(2)}) %collective-permute-start.2) | collective-permute-done | bytes 69664 | tf_op jit(solution)/shard_map/ppermute | solution.py:530
  37.7 0.0 collective-permute-done.3.via_even_ref.even_before_ref
  37.7 0.6 restrict.1
  38.3 21.6 %all_to_all.10 = f32[64,2,128]{2,1,0:T(2,128)S(1)} all-to-all(f32[64,2,128]{2,1,0:T(2,128)S(1)} %get-tuple-element.68), channel_id=1, replica_groups=mesh['grp'=16,'dom'=64] {'dom'}, dimensions={0} | all-to-all | bytes 131072 | tf_op jit(solution)/shard_map/all_to_all | solution.py:621
  59.9 1.5 %solve.1 = f32[128,128]{1,0:T(8,128)} custom-call(f32[128,128]{1,0:T(8,128)S(1)} %bitcast.5, s32[64,128]{1,0:T(8,128)S(1)} %get-tuple-element.69.nodes_ref, bf16[8192,128]{1,0:T(8,128)(2,1)S(1)} %get-tuple-element.70.slots_ref, bf16[256,512]{1,0:T(8,128)(2,1)S(1)} %get-tuple-element.71.parts_ref), custom_call_target="tpu_custom_call" | custom-call | flops 100000000 | bytes 2000000 | tf_op jit(solution)/shard_map/solve/pallas_call | solution.py:512
  61.3 4.6 %all-to-all-start.1 = ((f32[64,2,128]{2,1,0:T(2,128)}), f32[64,2,128]{2,1,0:T(2,128)S(1)}, u32[]{:S(2)}, u32[]{:S(2)}) async-start(f32[64,2,128]{2,1,0:T(2,128)} %bitcast.4), calls=%async_computation.1 | async-start | bytes 131072 | tf_op jit(solution)/shard_map/all_to_all | solution.py:626
  66.0 15.1 %all-to-all-done.1.returned_ref = f32[64,2,128]{2,1,0:T(2,128)S(1)} async-done(((f32[64,2,128]{2,1,0:T(2,128)}), f32[64,2,128]{2,1,0:T(2,128)S(1)}, u32[]{:S(2)}, u32[]{:S(2)}) %all-to-all-start.1) | async-done | bytes 65568 | tf_op jit(solution)/shard_map/all_to_all | solution.py:626
  81.1 1.2 %prolong.1 = (f32[32,128]{1,0:T(8,128)S(1)}, f32[2,1024]{1,0:T(2,128)S(1)}, f32[8,1024]{1,0:T(8,128)S(1)}, f32[8,128]{1,0:T(8,128)S(1)}, f32[8,128]{1,0:T(8,128)...) custom-call(f32[8,128]{1,0:T(8,128)S(1)} %select_n.41.even_ref, ...), custom_call_target="tpu_custom_call" | custom-call | flops 100000000 | bytes 2000000 | tf_op jit(solution)/shard_map/prolong/pallas_call | solution.py:512
  82.3 3.2 %collective-permute-start.4 = (f32[8,128]{1,0:T(8,128)S(1)}, f32[8,128]{1,0:T(8,128)S(1)}, u32[]{:S(2)}, u32[]{:S(2)}) collective-permute-start(f32[8,128]{1,0:T(8,128)S(1)} %get-tuple-element.77), channel_id=1, source_target_pairs={{0,2},{2,0},{1,3},{3,1},{4,6},{6,4},{5,7},{7,5},{8,10},{10,8},{9,1... | collective-permute-start | bytes 12296 | tf_op jit(solution)/shard_map/ppermute | solution.py:530
  85.6 1.9 %collective-permute-start.5 = (f32[8,128]{1,0:T(8,128)S(1)}, f32[8,128]{1,0:T(8,128)S(1)}, u32[]{:S(2)}, u32[]{:S(2)}) collective-permute-start(f32[8,128]{1,0:T(8,128)S(1)} %get-tuple-element.78), channel_id=1, source_target_pairs={{2,4},{4,2},{3,5},{5,3},{6,8},{8,6},{7,9},{9,7},{10,12},{12,10},{1... | collective-permute-start | bytes 12296 | tf_op jit(solution)/shard_map/ppermute | solution.py:530
  87.5 8.7 %collective-permute-start.6 = (f32[8,128]{1,0:T(8,128)S(1)}, f32[8,128]{1,0:T(8,128)S(1)}, u32[]{:S(2)}, u32[]{:S(2)}) collective-permute-start(f32[8,128]{1,0:T(8,128)S(1)} %get-tuple-element.79), channel_id=1, source_target_pairs={{1,2},{2,1},{3,4},{4,3},{5,6},{6,5},{7,8},{8,7},{9,10},{10,9},{11,... | collective-permute-start | bytes 12296 | tf_op jit(solution)/shard_map/ppermute | solution.py:530
  96.2 1.9 %collective-permute-start.7 = (f32[8,128]{1,0:T(8,128)S(1)}, f32[8,128]{1,0:T(8,128)S(1)}, u32[]{:S(2)}, u32[]{:S(2)}) collective-permute-start(f32[8,128]{1,0:T(8,128)S(1)} %get-tuple-element.80), channel_id=1, source_target_pairs={{0,1},{1,0},{2,3},{3,2},{4,5},{5,4},{6,7},{7,6},{8,9},{9,8},{10,11... | collective-permute-start | bytes 12296 | tf_op jit(solution)/shard_map/ppermute | solution.py:530
  98.1 0.8 output.1
  98.9 0.0 collective-permute-done.4.via_two_low_ref
  98.9 0.0 collective-permute-done.5.via_two_high_ref
  98.9 0.0 collective-permute-done.6.via_odd_ref
  98.9 2.8 %collective-permute-done.7.via_even_ref = f32[8,128]{1,0:T(8,128)S(1)} collective-permute-done((f32[8,128]{1,0:T(8,128)S(1)}, f32[8,128]{1,0:T(8,128)S(1)}, u32[]{:S(2)}, u32[]{:S(2)}) %collective-permute-start.7) | collective-permute-done | bytes 4128 | tf_op jit(solution)/shard_map/ppermute | solution.py:530
  101.7 1.3 %finish.1 = (f32[2,1536]{1,0:T(2,128)}, f32[2,1536]{1,0:T(2,128)}, f32[2,1024]{1,0:T(2,128)}) custom-call(f32[8,128]{1,0:T(8,128)S(1)} %collective-permute-done.4.via_two_low_ref, f32[8,128]{1,0:T(8,128)S(1)} %collective-permute-done.5.via_two_high_ref, f32[8,128]{1,0:T(8,128)S(1)} %collective-permute-done.6.via_odd_ref, ...), custom_call_target="tpu_custom_call" | custom-call | flops 100000000 | bytes 2000000 | tf_op jit(solution)/shard_map/finish/pallas_call | solution.py:512
  (5 shorter events, 0.0 us)
Async XLA Ops:
  0.6 25.0 %collective-permute-start = (f32[2,1536]{1,0:T(2,128)}, f32[2,1536]{1,0:T(2,128)S(1)}, u32[]{:S(2)}, u32[]{:S(2)}) collective-permute-start(f32[2,1536]{1,0:T(2,128)} %refs_0_.1), channel_id=1, source_target_pairs={{1,2},{2,1},{3,4},{4,3},{5,6},{6,5},{7,8},{8,7},{9,10},{10,9},{11,... | collective-permute-start | bytes 36872 | tf_op jit(solution)/shard_map/ppermute | solution.py:530
  20.4 5.8 %collective-permute-start.1 = (f32[2,1536]{1,0:T(2,128)}, f32[2,1536]{1,0:T(2,128)S(1)}, u32[]{:S(2)}, u32[]{:S(2)}) collective-permute-start(f32[2,1536]{1,0:T(2,128)} %refs_0_.1), channel_id=1, source_target_pairs={{0,1},{1,0},{2,3},{3,2},{4,5},{5,4},{6,7},{7,6},{8,9},{9,8},{10,11... | collective-permute-start | bytes 36872 | tf_op jit(solution)/shard_map/ppermute | solution.py:530
  26.6 11.1 %collective-permute-start.2 = (f32[136,128]{1,0:T(8,128)S(1)}, f32[136,128]{1,0:T(8,128)S(1)}, u32[]{:S(2)}, u32[]{:S(2)}) collective-permute-start(f32[136,128]{1,0:T(8,128)S(1)} %get-tuple-element.57), channel_id=1, source_target_pairs={{1,2},{2,1},{3,4},{4,3},{5,6},{6,5},{7,8},{8,7},{9,10},{10,9},{11,... | collective-permute-start | bytes 208904 | tf_op jit(solution)/shard_map/ppermute | solution.py:530
  31.5 6.2 %collective-permute-start.3 = (f32[136,128]{1,0:T(8,128)S(1)}, f32[136,128]{1,0:T(8,128)S(1)}, u32[]{:S(2)}, u32[]{:S(2)}) collective-permute-start(f32[136,128]{1,0:T(8,128)S(1)} %get-tuple-element.58), channel_id=1, source_target_pairs={{0,1},{1,0},{2,3},{3,2},{4,5},{5,4},{6,7},{7,6},{8,9},{9,8},{10,11... | collective-permute-start | bytes 208904 | tf_op jit(solution)/shard_map/ppermute | solution.py:530
  61.3 19.8 %all-to-all-start.1 = ((f32[64,2,128]{2,1,0:T(2,128)}), f32[64,2,128]{2,1,0:T(2,128)S(1)}, u32[]{:S(2)}, u32[]{:S(2)}) async-start(f32[64,2,128]{2,1,0:T(2,128)} %bitcast.4), calls=%async_computation.1 | async-start | bytes 131072 | tf_op jit(solution)/shard_map/all_to_all | solution.py:626
  82.3 16.6 %collective-permute-start.4 = (f32[8,128]{1,0:T(8,128)S(1)}, f32[8,128]{1,0:T(8,128)S(1)}, u32[]{:S(2)}, u32[]{:S(2)}) collective-permute-start(f32[8,128]{1,0:T(8,128)S(1)} %get-tuple-element.77), channel_id=1, source_target_pairs={{0,2},{2,0},{1,3},{3,1},{4,6},{6,4},{5,7},{7,5},{8,10},{10,8},{9,1... | collective-permute-start | bytes 12296 | tf_op jit(solution)/shard_map/ppermute | solution.py:530
  85.6 13.4 %collective-permute-start.5 = (f32[8,128]{1,0:T(8,128)S(1)}, f32[8,128]{1,0:T(8,128)S(1)}, u32[]{:S(2)}, u32[]{:S(2)}) collective-permute-start(f32[8,128]{1,0:T(8,128)S(1)} %get-tuple-element.78), channel_id=1, source_target_pairs={{2,4},{4,2},{3,5},{5,3},{6,8},{8,6},{7,9},{9,7},{10,12},{12,10},{1... | collective-permute-start | bytes 12296 | tf_op jit(solution)/shard_map/ppermute | solution.py:530
  87.5 11.4 %collective-permute-start.6 = (f32[8,128]{1,0:T(8,128)S(1)}, f32[8,128]{1,0:T(8,128)S(1)}, u32[]{:S(2)}, u32[]{:S(2)}) collective-permute-start(f32[8,128]{1,0:T(8,128)S(1)} %get-tuple-element.79), channel_id=1, source_target_pairs={{1,2},{2,1},{3,4},{4,3},{5,6},{6,5},{7,8},{8,7},{9,10},{10,9},{11,... | collective-permute-start | bytes 12296 | tf_op jit(solution)/shard_map/ppermute | solution.py:530
  96.2 5.5 %collective-permute-start.7 = (f32[8,128]{1,0:T(8,128)S(1)}, f32[8,128]{1,0:T(8,128)S(1)}, u32[]{:S(2)}, u32[]{:S(2)}) collective-permute-start(f32[8,128]{1,0:T(8,128)S(1)} %get-tuple-element.80), channel_id=1, source_target_pairs={{0,1},{1,0},{2,3},{3,2},{4,5},{5,4},{6,7},{7,6},{8,9},{9,8},{10,11... | collective-permute-start | bytes 12296 | tf_op jit(solution)/shard_map/ppermute | solution.py:530

commit v7 on v5

--- a/solution.py
+++ b/solution.py
@@ -167,9 +167,53 @@
             by_moment_ref[rows, :] = projection_ref[n, :, at : at + LANES]
 
 
+def end_columns(place, blocks, rim):
+    high, low, _ = place
+    owned = jnp.where((high == blocks - 1) & (low >= LANES - rim), low, -1)
+    owned = jnp.where((high == 0) & (low < rim), low + 2 * rim, owned)
+    return jnp.where(high == blocks, low, owned)
+
+
+def couple_kernel(rim, edge_count, even_ref, edges_ref, live_ref, matrix_ref, out_ref):
+    blocks = edge_count // LANES
+    count = live_ref.shape[1]
+    places = edge_places(edges_ref, rim, edge_count + 2 * rim)
+    columns = [end_columns(place, blocks, rim) for place in places]
+    live = live_ref[...].astype(jnp.float32)
+    wide = iota((8, count), 0)
+    signs = jnp.ones((8, count), jnp.float32)
+    for k, (_, _, flip) in enumerate(places):
+        signs = jnp.where(wide == 2 * k, flip, signs)
+    tall = iota((LANES, count), 0)
+    row = iota((rim, count), 0)
+    shift = jnp.where(even_ref[0:1, :] > 0.5, rim, 0)
+    shift = jnp.concatenate([shift] * (count // LANES), 1)
+    total = jnp.zeros((LANES, LANES), jnp.float32)
+    for k in range(3):
+        rows = []
+        for c in range(2):
+            j = 2 * k + c
+            weights = matrix_ref[j] * signs * (signs[j : j + 1] * live)
+            for d in range(2):
+                block = jnp.zeros((rim, count), jnp.float32)
+                for m in range(3):
+                    weight = weights[2 * m + d : 2 * m + d + 1]
+                    block = block + jnp.where(row == columns[m] - shift, weight, 0.0)
+                rows.append(block)
+        rows = jnp.concatenate(rows, 0)
+        coarse = rows.astype(jnp.bfloat16)
+        fine = (rows - coarse.astype(jnp.float32)).astype(jnp.bfloat16)
+        hot = jnp.where(tall == columns[k], 1.0, 0.0).astype(jnp.bfloat16)
+        for piece in (coarse, fine):
+            total = total + lax.dot_general(
+                hot, piece, (((1,), (1,)), ((), ())), preferred_element_type=jnp.float32
+            )
+    out_ref[...] = total
+
+
 def residual_kernel(
     rim, even_ref, via_odd_ref, via_even_ref, own_ref, b_ref, w_ref, edges_ref, live_ref,
-    matrix_ref, hot_ref, y_ref, ends_ref, odd_ref, even_out_ref,
+    matrix_ref, hot_ref, coupling_ref, y_ref, ends_ref, odd_ref, even_out_ref,
 ):
     edge_count = b_ref.shape[1]
     blocks = edge_count // LANES
@@ -188,7 +232,8 @@
     ends_ref[...] = ends
     to_left = jnp.concatenate([ends[0:2], ends[4:6], b_ref[:, :LANES], w_ref[:, :LANES]], 0)
     to_right = jnp.concatenate([ends[2:4], ends[4:6], b_ref[:, tail], w_ref[:, tail]], 0)
-    odd_ref[...], even_out_ref[...] = by_side(even_ref, to_left, to_right)
+    odd_ref[0:8, :], even_out_ref[...] = by_side(even_ref, to_left, to_right)
+    odd_ref[8:, :] = coupling_ref[...]
 
 
 def spread_lists(lists_ref, nodes_ref):
@@ -245,7 +290,7 @@
 ):
     blocks = edge_count // LANES
     count = a_ref.shape[1]
-    left, right = by_side(even_ref, via_odd_ref[...], via_even_ref[...])
+    left, right = by_side(even_ref, via_odd_ref[0:8, :], via_even_ref[...])
     head, tail = arrivals(left[2:4], right[2:4], rim)
     exists = exists_ref[...]
     settled = ends_ref[4:6, :] + rim_row(left[0:2], right[0:2], rim)
@@ -362,7 +407,7 @@
 
 def smooth_kernel(
     rim, p_ref, r_ref, r_inner_ref, inner_ref, w_ref, w_inner_ref, edges_ref, live_ref,
-    matrix_ref, hot_ref, z_ref, x1_inner_ref, y_ref,
+    matrix_ref, hot_ref, ends_ref, exists_ref, s_rim_ref, z_ref, x1_inner_ref, y_ref,
 ):
     edge_count = w_ref.shape[1]
     blocks = edge_count // LANES
@@ -372,6 +417,8 @@
     row = iota(total.shape, 0)
     load_table(z_ref, w_ref)
     z_ref[...] = z_ref[...] * r_ref[...] + jnp.where(row < 2 * blocks, total, 0.0)
+    rims = slice(2 * blocks, 2 * blocks + 2)
+    z_ref[rims, :] = s_rim_ref[...] + exists_ref[...] * ends_ref[4:6, :]
     z_inner = w_inner_ref[...] * r_inner_ref[...] + p_ref[6:8, :]
     x1_inner_ref[...] = inner_ref[...] + z_inner
     u = gather_moments(table_groups(z_ref), highs, z_inner, places)
@@ -379,50 +426,76 @@
 
 
 def update_kernel(
-    rim, edge_count, even_ref, via_odd_ref, via_even_ref, ends_ref, exists_ref, s_rim_ref,
-    part_ref, edges_ref, live_ref, matrix_ref, hot_ref, y_ref, change_ref, odd_ref, even_out_ref,
+    rim, edge_count, from_odd, via_ref, even_ref, exists_ref, part_ref, edges_ref, live_ref,
+    matrix_ref, hot_ref, before_ref, y_ref, change_ref, rims_ref,
 ):
     count = part_ref.shape[1]
-    left, right = by_side(even_ref, via_odd_ref[...], via_even_ref[...])
+    via = via_ref[...]
+    none = jnp.zeros_like(via)
+    sides = (via, none) if from_odd else (none, via)
+    left, right = by_side(even_ref, *sides)
     head, tail = arrivals(left[2:4], right[2:4], rim)
-    settled = ends_ref[4:6, :] + rim_row(left[0:2], right[0:2], rim)
-    z_rim = s_rim_ref[...] + exists_ref[...] * settled
+    z_rim = exists_ref[...] * rim_row(left[0:2], right[0:2], rim)
     change = jnp.concatenate([head, tail, z_rim, jnp.zeros((2, LANES), jnp.float32)], 0)
-    change_ref[...] = change
+    change_ref[...] = before_ref[...] + change
     places = edge_places(edges_ref, rim, edge_count + 2 * rim)
     highs = end_highs(edge_count // LANES)
     u = gather_moments([change], highs, jnp.zeros((2, count), jnp.float32), places)
     y = part_ref[...] + apply_matrix(matrix_ref, live_ref, u)
     y_ref[...] = y
     rims = scatter_moments(y, places, hot_ref, highs)[4:6]
-    odd_ref[...] = rims
-    even_out_ref[...] = rims
+    rims_ref[0:2, :] = rims
+    if rims_ref.shape[0] > 2:
+        rims_ref[2:, :] = jnp.zeros((rims_ref.shape[0] - 2, LANES), jnp.float32)
+
+
+def partner_part(rim, even_ref, ends_ref, coupling):
+    ends = ends_ref[...]
+    lane = iota((2, LANES), 1)
+    even = even_ref[0:2, :] > 0.5
+    turned = pltpu.roll(ends[4:6], 64, 1)
+    for_low = jnp.where(lane < rim, ends[0:2], jnp.where(lane >= 3 * rim, turned, 0.0))
+    for_high = jnp.where(lane < 2 * rim, pltpu.roll(ends[2:4], 64, 1), turned)
+    for_high = jnp.where((lane >= rim) & (lane < 3 * rim), for_high, 0.0)
+    change = jnp.where(even, for_low, for_high)
+    rows = jnp.concatenate([change, jnp.zeros((6, LANES), jnp.float32)], 0)
+    found = lax.dot_general(
+        rows, coupling, (((1,), (0,)), ((), ())),
+        precision=lax.Precision.HIGHEST, preferred_element_type=jnp.float32,
+    )
+    found = found[0:1] + pltpu.roll(found[1:2], 64, 1)
+    head = jnp.concatenate([found, pltpu.roll(found, LANES - rim, 1)], 0)
+    tail = pltpu.roll(head, LANES - rim, 1)
+    head = jnp.where(even & (lane < rim), head, 0.0)
+    return head, jnp.where(even | (lane < LANES - rim), 0.0, tail)
 
 
 def output_kernel(
-    rim, y_ref, change_ref, z_ref, r_ref, r_inner_ref, x_ref, edges_ref, hot_ref,
-    x1_ref, r1_ref, r1_inner_ref,
+    rim, y_ref, change_ref, z_ref, r_ref, r_inner_ref, x_ref, edges_ref, hot_ref, even_ref,
+    ends_ref, odd_before_ref, x1_ref, r1_ref, r1_inner_ref,
 ):
     edge_count = x_ref.shape[1]
     blocks = edge_count // LANES
     places = edge_places(edges_ref, rim, edge_count + 2 * rim)
     total = scatter_moments(y_ref[...], places, hot_ref, row_highs(blocks))
     r1_inner_ref[...] = r_inner_ref[...] - y_ref[6:8, :]
+    head, tail = partner_part(rim, even_ref, ends_ref, odd_before_ref[8:, :])
     for h in range(blocks):
         here = slice(h * LANES, (h + 1) * LANES)
         rows = slice(2 * h, 2 * h + 2)
         z = z_ref[rows, :]
+        r1 = r_ref[rows, :] - total[rows]
         if h == 0:
-            z = z + change_ref[0:2, :]
+            z, r1 = z + change_ref[0:2, :], r1 - head
         if h == blocks - 1:
-            z = z + change_ref[2:4, :]
+            z, r1 = z + change_ref[2:4, :], r1 - tail
         x1_ref[:, here] = x_ref[:, here] + z
-        r1_ref[:, here] = r_ref[rows, :] - total[rows]
+        r1_ref[:, here] = r1
 
 
 def finish_kernel(rim, even_ref, part_ref, via_odd_ref, via_even_ref, r1_ref):
     edge_count = part_ref.shape[1]
-    left, right = by_side(even_ref, via_odd_ref[...], via_even_ref[...])
+    left, right = by_side(even_ref, via_odd_ref[0:2, :], via_even_ref[...])
     head, tail = arrivals(left, right, rim)
     last = slice(edge_count - LANES, edge_count)
     r1_ref[...] = part_ref[...]
@@ -430,7 +503,7 @@
     r1_ref[:, last] = part_ref[:, last] - tail
 
 
-def local_call(kernel, outs, in_place=False, scratch=(), sems=0, name=None):
+def local_call(kernel, outs, in_place=False, scratch=(), sems=0, flops=10**8, name=None):
     def call(*args):
         spaces = [pltpu.HBM if in_place else pltpu.VMEM] * len(args)
         shapes = [
@@ -446,7 +519,7 @@
             scratch_shapes=[pltpu.VMEM(s, jnp.float32) for s in scratch] + extra,
             compiler_params=pltpu.CompilerParams(vmem_limit_bytes=VMEM_LIMIT),
             cost_estimate=pl.CostEstimate(
-                flops=10**8, bytes_accessed=2 * 10**6, transcendentals=0
+                flops=flops, bytes_accessed=flops // 50, transcendentals=0
             ),
             name=name,
         )(*args)
@@ -454,16 +527,11 @@
     return call
 
 
-def swap(odd, even):
+def swap(message, first):
     axis = ("grp", "dom")
-    count = lax.axis_size(axis)
-
-    def pairs(first):
-        lows = range(first, count - 1, 2)
-        return [(i, i + 1) for i in lows] + [(i + 1, i) for i in lows]
-
-    via_even = lax.ppermute(even, axis, pairs(0))
-    return lax.ppermute(odd, axis, pairs(1)), via_even
+    lows = range(first, lax.axis_size(axis) - 1, 2)
+    pairs = [(i, i + 1) for i in lows] + [(i + 1, i) for i in lows]
+    return lax.ppermute(message, axis, pairs)
 
 
 def shards(
@@ -493,7 +561,8 @@
     is_last = strip == lax.axis_size(("grp", "dom")) - 1
     exists = jnp.where(lane < rim, jnp.where(is_last, 0.0, 1.0), jnp.where(strip == 0, 0.0, 1.0))
     exists = jnp.where(lane < 2 * rim, exists, 0.0)
-    via_odd, via_even = swap(x_edges, x_edges)
+    via_even = swap(x_edges, 0)
+    via_odd = swap(x_edges, 1)
     table = (rows, LANES)
     group = (8, LANES)
     inner = (2, elem_count)
@@ -514,12 +583,17 @@
     )(*[pltpu.with_memory_space_constraint(v, pltpu.HBM) for v in arguments])
     x_edges, x_inner, elem_edges, live, elem_matrix, nodal_first = staged[:6]
     b_edges, b_inner, w_edges, w_inner, aux_inverse, owner_counts, aux_node = staged[6:]
+    (coupling,) = local_call(
+        functools.partial(couple_kernel, rim, edge_count), [(LANES, LANES)], name="couple"
+    )(even, elem_edges, live, elem_matrix)
     y, ends, odd_out, even_out = local_call(
-        functools.partial(residual_kernel, rim), [moments, group, group, group], name="residual"
+        functools.partial(residual_kernel, rim), [moments, group, (8 + LANES, LANES), group],
+        name="residual",
     )(
-        even, via_odd, via_even, own, b_edges, w_edges, elem_edges, live, elem_matrix, hot
-    )
-    via_odd, via_even = swap(odd_out, even_out)
+        even, via_odd, via_even, own, b_edges, w_edges, elem_edges, live, elem_matrix, hot, coupling
+    )
+    via_even = swap(even_out, 0)
+    odd_before = swap(odd_out, 1)
     size = aux_inverse.shape[1]
     r, r_inner, a, slots_hot, parts, nodes = local_call(
         functools.partial(partial_kernel, rim),
@@ -535,7 +609,7 @@
         functools.partial(restrict_kernel, rim, edge_count), [table, (2, LANES), slots],
         scratch=[lists], name="restrict",
     )(
-        even, via_odd, via_even, ends, exists, r, a, elem_edges, live, by_moment, owner_counts
+        even, odd_before, via_even, ends, exists, r, a, elem_edges, live, by_moment, owner_counts
     )
     arrived = lax.all_to_all(packed, "dom", split_axis=0, concat_axis=0, tiled=True)
     (outgoing,) = local_call(solve_kernel, [(2 * peers, LANES)], name="solve")(
@@ -547,24 +621,33 @@
         functools.partial(prolong_kernel, rim, edge_count),
         [moments, group, (4, LANES), (4, LANES)], scratch=[lists], name="prolong",
     )(even, returned, elem_edges, live, nodal_first, owner_counts, hot)
-    via_odd, via_even = swap(odd_out, even_out)
+    via_even = swap(even_out, 0)
+    via_odd = swap(odd_out, 1)
     z, x1_inner, az = local_call(
         functools.partial(smooth_kernel, rim), [table, inner, moments], name="smooth"
-    )(p, r, r_inner, x_inner, w_edges, w_inner, elem_edges, live, elem_matrix, hot)
-    az, change, odd_out, even_out = local_call(
-        functools.partial(update_kernel, rim, edge_count),
-        [moments, group, (2, LANES), (2, LANES)], name="update",
     )(
-        even, via_odd, via_even, ends, exists, s_rim, az, elem_edges, live, elem_matrix, hot
-    )
-    via_odd, via_even = swap(odd_out, even_out)
+        p, r, r_inner, x_inner, w_edges, w_inner, elem_edges, live, elem_matrix, hot, ends, exists,
+        s_rim,
+    )
+    shared = (even, exists)
+    element = (elem_edges, live, elem_matrix, hot)
+    az, change, rims = local_call(
+        functools.partial(update_kernel, rim, edge_count, False),
+        [moments, group, (8, LANES)], name="update_even",
+    )(via_even, *shared, az, *element, jnp.zeros(group, jnp.float32))
+    rims_odd = swap(rims, 1)
+    az, change, rims = local_call(
+        functools.partial(update_kernel, rim, edge_count, True),
+        [moments, group, (2, LANES)], flops=10**10, name="update_odd",
+    )(via_odd, *shared, az, *element, change)
+    rims_even = swap(rims, 0)
     x1_edges, r1_part, r1_inner = local_call(
         functools.partial(output_kernel, rim), [x_edges.shape, x_edges.shape, inner],
-        name="output",
-    )(az, change, z, r, r_inner, x_edges, elem_edges, hot)
+        flops=10**4, name="output",
+    )(az, change, z, r, r_inner, x_edges, elem_edges, hot, even, ends, odd_before)
     (r1_edges,) = local_call(
         functools.partial(finish_kernel, rim), [x_edges.shape], name="finish"
-    )(even, r1_part, via_odd, via_even)
+    )(even, r1_part, rims_odd, rims_even)
     return x1_edges, x1_inner, r1_edges, r1_inner
 
 

time: 102 us -> 102 us (level)
  waiting for transfers between devices: 11.5 us -> 6.91 us
  starting transfers between devices: 40.6 us -> 43.8 us
  Pallas kernels: 8 us -> 9.68 us
    ppermute x8, waiting for transfers between devices: 11.5 us -> 6.91 us  [swap(): return lax.ppermute(message, axis, pairs)]
    ppermute x8, starting transfers between devices: 40.6 us -> 43.8 us  [swap(): return lax.ppermute(message, axis, pairs)]
    pallas_call x10 -> x12, Pallas kernels: 8 us -> 9.68 us  [call(): pl.pallas_call(kernel, out_shape=shapes, in_specs=[pl.BlockSpec(memory_sp...]
  transfers between devices with their start and end apart: 8 -> 8, of which waited for: 5 -> 4; matrix products, arithmetic and copies ran while one was open for 0% -> 0% of each run, Pallas kernels for 4% -> 7%
where the time goes in v7:
time: 102 us; the launch traced here: 101 us
  starting transfers between devices  43.8 us (43%)
  blocking collectives  39.9 us (39%)
  Pallas kernels  9.68 us (9%)
  waiting for transfers between devices  6.91 us (7%)
    ppermute x8, starting transfers between devices, swap(): return lax.ppermute(message, axis, pairs)  43.8 us
    all_to_all x1, blocking collectives, shards(): lax.all_to_all(packed, 'dom', split_axis=0, concat_axis=0, tiled=True)  20.9 us
    all_to_all x1, blocking collectives, shards(): lax.all_to_all(outgoing, 'dom', split_axis=0, concat_axis=0, tiled=True)  19 us
    pallas_call x12, Pallas kernels, call(): pl.pallas_call(kernel, out_shape=shapes, in_specs=[pl.BlockSpec(memory_sp...  9.68 us
    ppermute x8, waiting for transfers between devices, swap(): return lax.ppermute(message, axis, pairs)  6.91 us
  transfers between devices with their start and end apart: 8, of which 4 were waited for; matrix products, arithmetic and copies ran while one was open for 0% of the time, Pallas kernels for 7%

profile of v7, /device:TPU:32, one launch (start us, length us, event | category | flops | bytes accessed | tf_op | source)
XLA Modules:
  0.0 101.1 jit_solution(10044251340857521900)
XLA Ops:
  0.6 19.7 %collective-permute-start = (f32[2,1536]{1,0:T(2,128)}, f32[2,1536]{1,0:T(2,128)S(1)}, u32[]{:S(2)}, u32[]{:S(2)}) collective-permute-start(f32[2,1536]{1,0:T(2,128)} %refs_0_.1), channel_id=1, source_target_pairs={{1,2},{3,4},{5,6},{7,8},{9,10},{11,12},{13,14},{15,16},{17,18},{19... | collective-permute-start | bytes 36872 | tf_op jit(solution)/shard_map/ppermute | solution.py:534
  20.4 1.9 %collective-permute-start.1 = (f32[2,1536]{1,0:T(2,128)}, f32[2,1536]{1,0:T(2,128)S(1)}, u32[]{:S(2)}, u32[]{:S(2)}) collective-permute-start(f32[2,1536]{1,0:T(2,128)} %refs_0_.1), channel_id=1, source_target_pairs={{0,1},{2,3},{4,5},{6,7},{8,9},{10,11},{12,13},{14,15},{16,17},{18,... | collective-permute-start | bytes 36872 | tf_op jit(solution)/shard_map/ppermute | solution.py:534
  22.4 1.5 %stage.1 = (f32[2,1536]{1,0:T(2,128)S(1)}, f32[2,1024]{1,0:T(2,128)S(1)}, s32[3,1024]{1,0:T(4,128)S(1)}, s32[1,1024]{1,0:T(1,128)S(1)}, f32[8,8,1024]{2,1,0:T(8,...) custom-call(f32[2,1536]{1,0:T(2,128)} %refs_0_.1, ...), custom_call_target="tpu_custom_call" | custom-call | flops 100000000 | bytes 2000000 | tf_op jit(solution)/shard_map/stage/pallas_call | solution.py:514
  23.9 1.0 %couple.1.coupling_ref = f32[128,128]{1,0:T(8,128)S(1)} custom-call(f32[8,128]{1,0:T(8,128)S(1)} %select_n.33.even_ref, s32[3,1024]{1,0:T(4,128)S(1)} %get-tuple-element.52.edges_ref, s32[1,1024]{1,0:T(1,128)S(1)} %get-tuple-element.53.live_ref, f32[8,8,1024]{2,1,0:T(8,128)S(1)} %get-tuple-element.54.matrix_ref), custom_call_target="tpu_custom_call" | custom-call | flops 100000000 | bytes 2000000 | tf_op jit(solution)/shard_map/couple/pallas_call | solution.py:514
  24.9 0.0 collective-permute-done.via_odd_ref
  24.9 1.3 %collective-permute-done.1.via_even_ref = f32[2,1536]{1,0:T(2,128)S(1)} collective-permute-done((f32[2,1536]{1,0:T(2,128)}, f32[2,1536]{1,0:T(2,128)S(1)}, u32[]{:S(2)}, u32[]{:S(2)}) %collective-permute-start.1) | collective-permute-done | bytes 12320 | tf_op jit(solution)/shard_map/ppermute | solution.py:534
  26.2 0.4 residual.1
  26.6 4.9 %collective-permute-start.2 = (f32[136,128]{1,0:T(8,128)S(1)}, f32[136,128]{1,0:T(8,128)S(1)}, u32[]{:S(2)}, u32[]{:S(2)}) collective-permute-start(f32[136,128]{1,0:T(8,128)S(1)} %get-tuple-element.56), channel_id=1, source_target_pairs={{1,2},{3,4},{5,6},{7,8},{9,10},{11,12},{13,14},{15,16},{17,18},{19... | collective-permute-start | bytes 208904 | tf_op jit(solution)/shard_map/ppermute | solution.py:534
  31.5 1.9 %collective-permute-start.3 = (f32[8,128]{1,0:T(8,128)S(1)}, f32[8,128]{1,0:T(8,128)S(1)}, u32[]{:S(2)}, u32[]{:S(2)}) collective-permute-start(f32[8,128]{1,0:T(8,128)S(1)} %get-tuple-element.57), channel_id=1, source_target_pairs={{0,1},{2,3},{4,5},{6,7},{8,9},{10,11},{12,13},{14,15},{16,17},{18,... | collective-permute-start | bytes 12296 | tf_op jit(solution)/shard_map/ppermute | solution.py:534
  33.4 1.1 %partial.1 = (f32[32,128]{1,0:T(8,128)S(1)}, f32[2,1024]{1,0:T(2,128)S(1)}, f32[8,1024]{1,0:T(8,128)S(1)}, bf16[8192,128]{1,0:T(8,128)(2,1)S(1)}, bf16[256,512]{1,0:T(8,128)(2,1)S(1)}, /*index=5*/s32[64,128]{1,0:T(8,128)S(1)}) custom-call(f32[8,1024]{1,0:T(8,128)S(1)} %get-tuple-element.59.y_ref, f32[2,1536]{1,0:T(2,128)S(1)} %get-tuple-element.50.b_ref, ...), custom_call_target="tpu_custom_call" | custom-call | flops 100000000 | bytes 2000000 | tf_op jit(solution)/shard_map/partial/pallas_call | solution.py:514
  34.6 2.5 %collective-permute-done.3.via_even_ref = f32[8,128]{1,0:T(8,128)S(1)} collective-permute-done((f32[8,128]{1,0:T(8,128)S(1)}, f32[8,128]{1,0:T(8,128)S(1)}, u32[]{:S(2)}, u32[]{:S(2)}) %collective-permute-start.3) | collective-permute-done | bytes 4128 | tf_op jit(solution)/shard_map/ppermute | solution.py:534
  37.0 0.7 collective-permute-done.2.via_odd_ref.odd_before_ref
  37.7 0.6 restrict.1
  38.2 20.9 %all_to_all.10 = f32[64,2,128]{2,1,0:T(2,128)S(1)} all-to-all(f32[64,2,128]{2,1,0:T(2,128)S(1)} %get-tuple-element.67), channel_id=1, replica_groups=mesh['grp'=16,'dom'=64] {'dom'}, dimensions={0} | all-to-all | bytes 131072 | tf_op jit(solution)/shard_map/all_to_all | solution.py:614
  59.1 0.8 solve.1
  60.0 19.0 %all_to_all.11.returned_ref = f32[64,2,128]{2,1,0:T(2,128)S(1)} all-to-all(f32[64,2,128]{2,1,0:T(2,128)S(1)} %bitcast.6), channel_id=1, replica_groups=mesh['grp'=16,'dom'=64] {'dom'}, dimensions={0} | all-to-all | bytes 131072 | tf_op jit(solution)/shard_map/all_to_all | solution.py:619
  78.9 0.6 prolong.1
  79.5 2.4 %collective-permute-start.5 = (f32[4,128]{1,0:T(4,128)S(1)}, f32[4,128]{1,0:T(4,128)S(1)}, u32[]{:S(2)}, u32[]{:S(2)}) collective-permute-start(f32[4,128]{1,0:T(4,128)S(1)} %get-tuple-element.73), channel_id=1, source_target_pairs={{0,1},{2,3},{4,5},{6,7},{8,9},{10,11},{12,13},{14,15},{16,17},{18,... | collective-permute-start | bytes 6152 | tf_op jit(solution)/shard_map/ppermute | solution.py:534
  82.0 1.9 %collective-permute-start.4 = (f32[4,128]{1,0:T(4,128)S(1)}, f32[4,128]{1,0:T(4,128)S(1)}, u32[]{:S(2)}, u32[]{:S(2)}) collective-permute-start(f32[4,128]{1,0:T(4,128)S(1)} %get-tuple-element.72), channel_id=1, source_target_pairs={{1,2},{3,4},{5,6},{7,8},{9,10},{11,12},{13,14},{15,16},{17,18},{19... | collective-permute-start | bytes 6152 | tf_op jit(solution)/shard_map/ppermute | solution.py:534
  83.9 1.1 %smooth.1 = (f32[32,128]{1,0:T(8,128)S(1)}, f32[2,1024]{1,0:T(2,128)}, f32[8,1024]{1,0:T(8,128)S(1)}) custom-call(f32[8,1024]{1,0:T(8,128)S(1)} %get-tuple-element.74.p_ref, f32[32,128]{1,0:T(8,128)S(1)} %get-tuple-element.75.r_ref, f32[2,1024]{1,0:T(2,128)S(1)} %get-tuple-element.76.r_inner_ref, f32[2,1024]{1,0:T(2,128)S(1)} %get-tuple-element.77.inner_ref, ...), custom_call_target="tpu_custom_call" | custom-call | flops 100000000 | bytes 2000000 | tf_op jit(solution)/shard_map/smooth/pallas_call | solution.py:514
  85.0 0.0 collective-permute-done.5.via_ref
  85.0 0.4 update_even.1
  85.4 9.0 %collective-permute-start.6 = (f32[8,128]{1,0:T(8,128)S(1)}, f32[8,128]{1,0:T(8,128)S(1)}, u32[]{:S(2)}, u32[]{:S(2)}) collective-permute-start(f32[8,128]{1,0:T(8,128)S(1)} %get-tuple-element.91), channel_id=1, source_target_pairs={{1,2},{3,4},{5,6},{7,8},{9,10},{11,12},{13,14},{15,16},{17,18},{19... | collective-permute-start | bytes 12296 | tf_op jit(solution)/shard_map/ppermute | solution.py:534
  94.5 0.0 collective-permute-done.4.via_ref
  94.5 0.4 update_odd.1
  94.9 1.9 %collective-permute-start.7 = (f32[2,128]{1,0:T(2,128)S(1)}, f32[2,128]{1,0:T(2,128)S(1)}, u32[]{:S(2)}, u32[]{:S(2)}) collective-permute-start(f32[2,128]{1,0:T(2,128)S(1)} %get-tuple-element.92), channel_id=1, source_target_pairs={{0,1},{2,3},{4,5},{6,7},{8,9},{10,11},{12,13},{14,15},{16,17},{18,... | collective-permute-start | bytes 3080 | tf_op jit(solution)/shard_map/ppermute | solution.py:534
  96.9 1.0 %output.1 = (f32[2,1536]{1,0:T(2,128)}, f32[2,1536]{1,0:T(2,128)S(1)}, f32[2,1024]{1,0:T(2,128)}) custom-call(f32[8,1024]{1,0:T(8,128)S(1)} %get-tuple-element.84.y_ref, f32[8,128]{1,0:T(8,128)S(1)} %get-tuple-element.85.change_ref, f32[32,128]{1,0:T(8,128)S(1)} %get-tuple-element.86.z_ref, f32[32,128]{1,0:T(8,128)S(1)} %get-tuple-element.75.r_ref, ...), custom_call_target="tpu_custom_call" | custom-call | flops 10000 | bytes 200 | tf_op jit(solution)/shard_map/output/pallas_call | solution.py:514
  97.9 2.5 %collective-permute-done.7.via_even_ref = f32[2,128]{1,0:T(2,128)S(1)} collective-permute-done((f32[2,128]{1,0:T(2,128)S(1)}, f32[2,128]{1,0:T(2,128)S(1)}, u32[]{:S(2)}, u32[]{:S(2)}) %collective-permute-start.7) | collective-permute-done | bytes 1056 | tf_op jit(solution)/shard_map/ppermute | solution.py:534
  100.4 0.0 collective-permute-done.6.via_odd_ref
  100.4 0.7 finish.1
  (5 shorter events, 0.0 us)
Async XLA Ops:
  0.6 24.3 %collective-permute-start = (f32[2,1536]{1,0:T(2,128)}, f32[2,1536]{1,0:T(2,128)S(1)}, u32[]{:S(2)}, u32[]{:S(2)}) collective-permute-start(f32[2,1536]{1,0:T(2,128)} %refs_0_.1), channel_id=1, source_target_pairs={{1,2},{3,4},{5,6},{7,8},{9,10},{11,12},{13,14},{15,16},{17,18},{19... | collective-permute-start | bytes 36872 | tf_op jit(solution)/shard_map/ppermute | solution.py:534
  20.4 5.8 %collective-permute-start.1 = (f32[2,1536]{1,0:T(2,128)}, f32[2,1536]{1,0:T(2,128)S(1)}, u32[]{:S(2)}, u32[]{:S(2)}) collective-permute-start(f32[2,1536]{1,0:T(2,128)} %refs_0_.1), channel_id=1, source_target_pairs={{0,1},{2,3},{4,5},{6,7},{8,9},{10,11},{12,13},{14,15},{16,17},{18,... | collective-permute-start | bytes 36872 | tf_op jit(solution)/shard_map/ppermute | solution.py:534
  26.6 11.1 %collective-permute-start.2 = (f32[136,128]{1,0:T(8,128)S(1)}, f32[136,128]{1,0:T(8,128)S(1)}, u32[]{:S(2)}, u32[]{:S(2)}) collective-permute-start(f32[136,128]{1,0:T(8,128)S(1)} %get-tuple-element.56), channel_id=1, source_target_pairs={{1,2},{3,4},{5,6},{7,8},{9,10},{11,12},{13,14},{15,16},{17,18},{19... | collective-permute-start | bytes 208904 | tf_op jit(solution)/shard_map/ppermute | solution.py:534
  31.5 5.5 %collective-permute-start.3 = (f32[8,128]{1,0:T(8,128)S(1)}, f32[8,128]{1,0:T(8,128)S(1)}, u32[]{:S(2)}, u32[]{:S(2)}) collective-permute-start(f32[8,128]{1,0:T(8,128)S(1)} %get-tuple-element.57), channel_id=1, source_target_pairs={{0,1},{2,3},{4,5},{6,7},{8,9},{10,11},{12,13},{14,15},{16,17},{18,... | collective-permute-start | bytes 12296 | tf_op jit(solution)/shard_map/ppermute | solution.py:534
  79.5 5.5 %collective-permute-start.5 = (f32[4,128]{1,0:T(4,128)S(1)}, f32[4,128]{1,0:T(4,128)S(1)}, u32[]{:S(2)}, u32[]{:S(2)}) collective-permute-start(f32[4,128]{1,0:T(4,128)S(1)} %get-tuple-element.73), channel_id=1, source_target_pairs={{0,1},{2,3},{4,5},{6,7},{8,9},{10,11},{12,13},{14,15},{16,17},{18,... | collective-permute-start | bytes 6152 | tf_op jit(solution)/shard_map/ppermute | solution.py:534
  82.0 12.5 %collective-permute-start.4 = (f32[4,128]{1,0:T(4,128)S(1)}, f32[4,128]{1,0:T(4,128)S(1)}, u32[]{:S(2)}, u32[]{:S(2)}) collective-permute-start(f32[4,128]{1,0:T(4,128)S(1)} %get-tuple-element.72), channel_id=1, source_target_pairs={{1,2},{3,4},{5,6},{7,8},{9,10},{11,12},{13,14},{15,16},{17,18},{19... | collective-permute-start | bytes 6152 | tf_op jit(solution)/shard_map/ppermute | solution.py:534
  85.4 14.9 %collective-permute-start.6 = (f32[8,128]{1,0:T(8,128)S(1)}, f32[8,128]{1,0:T(8,128)S(1)}, u32[]{:S(2)}, u32[]{:S(2)}) collective-permute-start(f32[8,128]{1,0:T(8,128)S(1)} %get-tuple-element.91), channel_id=1, source_target_pairs={{1,2},{3,4},{5,6},{7,8},{9,10},{11,12},{13,14},{15,16},{17,18},{19... | collective-permute-start | bytes 12296 | tf_op jit(solution)/shard_map/ppermute | solution.py:534
  94.9 5.5 %collective-permute-start.7 = (f32[2,128]{1,0:T(2,128)S(1)}, f32[2,128]{1,0:T(2,128)S(1)}, u32[]{:S(2)}, u32[]{:S(2)}) collective-permute-start(f32[2,128]{1,0:T(2,128)S(1)} %get-tuple-element.92), channel_id=1, source_target_pairs={{0,1},{2,3},{4,5},{6,7},{8,9},{10,11},{12,13},{14,15},{16,17},{18,... | collective-permute-start | bytes 3080 | tf_op jit(solution)/shard_map/ppermute | solution.py:534

commit v8 on v5

--- a/solution.py
+++ b/solution.py
@@ -168,15 +168,18 @@
 
 
 def residual_kernel(
-    rim, even_ref, via_odd_ref, via_even_ref, own_ref, b_ref, w_ref, edges_ref, live_ref,
-    matrix_ref, hot_ref, y_ref, ends_ref, odd_ref, even_out_ref,
+    rim, via_first_ref, via_odd_ref, via_even_ref, even_ref, own_ref, b_ref, w_ref, edges_ref, live_ref,
+    matrix_ref, hot_ref, y_ref, ends_ref, first_ref, odd_ref, even_out_ref,
 ):
     edge_count = b_ref.shape[1]
     blocks = edge_count // LANES
     count = own_ref.shape[1]
     tail = slice(edge_count - LANES, edge_count)
-    left, _ = by_side(even_ref, via_odd_ref[:, tail], via_even_ref[:, tail])
-    _, right = by_side(even_ref, via_odd_ref[:, :LANES], via_even_ref[:, :LANES])
+    head = slice(0, LANES)
+    near_tail = via_first_ref[:, tail] + via_even_ref[:, tail]
+    near_head = via_first_ref[:, head] + via_even_ref[:, head]
+    left, _ = by_side(even_ref, via_odd_ref[:, tail], near_tail)
+    _, right = by_side(even_ref, via_odd_ref[:, head], near_head)
     none = jnp.zeros((2, LANES), jnp.float32)
     change = jnp.concatenate([none, none, rim_row(left, right, rim), none], 0)
     places = edge_places(edges_ref, rim, edge_count + 2 * rim)
@@ -189,6 +192,7 @@
     to_left = jnp.concatenate([ends[0:2], ends[4:6], b_ref[:, :LANES], w_ref[:, :LANES]], 0)
     to_right = jnp.concatenate([ends[2:4], ends[4:6], b_ref[:, tail], w_ref[:, tail]], 0)
     odd_ref[...], even_out_ref[...] = by_side(even_ref, to_left, to_right)
+    first_ref[...] = even_out_ref[...]
 
 
 def spread_lists(lists_ref, nodes_ref):
@@ -240,12 +244,14 @@
 
 
 def restrict_kernel(
-    rim, edge_count, even_ref, via_odd_ref, via_even_ref, ends_ref, exists_ref, part_ref, a_ref,
+    rim, edge_count, via_first_ref, via_odd_ref, via_even_ref, even_ref, ends_ref, exists_ref,
+    part_ref, a_ref,
     edges_ref, live_ref, projection_ref, counts_ref, r_ref, s_rim_ref, packed_ref, vals_ref,
 ):
     blocks = edge_count // LANES
     count = a_ref.shape[1]
-    left, right = by_side(even_ref, via_odd_ref[...], via_even_ref[...])
+    via_near = via_first_ref[...] + via_even_ref[...]
+    left, right = by_side(even_ref, via_odd_ref[...], via_near)
     head, tail = arrivals(left[2:4], right[2:4], rim)
     exists = exists_ref[...]
     settled = ends_ref[4:6, :] + rim_row(left[0:2], right[0:2], rim)
@@ -454,16 +460,9 @@
     return call
 
 
-def swap(odd, even):
-    axis = ("grp", "dom")
-    count = lax.axis_size(axis)
-
-    def pairs(first):
-        lows = range(first, count - 1, 2)
-        return [(i, i + 1) for i in lows] + [(i + 1, i) for i in lows]
-
-    via_even = lax.ppermute(even, axis, pairs(0))
-    return lax.ppermute(odd, axis, pairs(1)), via_even
+def swap(message, lows):
+    pairs = [(i, i + 1) for i in lows] + [(i + 1, i) for i in lows]
+    return lax.ppermute(message, ("grp", "dom"), pairs)
 
 
 def shards(
@@ -493,7 +492,13 @@
     is_last = strip == lax.axis_size(("grp", "dom")) - 1
     exists = jnp.where(lane < rim, jnp.where(is_last, 0.0, 1.0), jnp.where(strip == 0, 0.0, 1.0))
     exists = jnp.where(lane < 2 * rim, exists, 0.0)
-    via_odd, via_even = swap(x_edges, x_edges)
+    strips, group_size = lax.axis_size(("grp", "dom")), lax.axis_size("dom")
+    odd, evens = range(1, strips - 1, 2), range(0, strips - 1, 2)
+    firsts = [i for i in evens if i % group_size == 0]
+    others = [i for i in evens if i % group_size != 0]
+    via_first = swap(x_edges, firsts)
+    via_odd = swap(x_edges, odd)
+    via_even = swap(x_edges, others)
     table = (rows, LANES)
     group = (8, LANES)
     inner = (2, elem_count)
@@ -514,12 +519,15 @@
     )(*[pltpu.with_memory_space_constraint(v, pltpu.HBM) for v in arguments])
     x_edges, x_inner, elem_edges, live, elem_matrix, nodal_first = staged[:6]
     b_edges, b_inner, w_edges, w_inner, aux_inverse, owner_counts, aux_node = staged[6:]
-    y, ends, odd_out, even_out = local_call(
-        functools.partial(residual_kernel, rim), [moments, group, group, group], name="residual"
+    y, ends, first_out, odd_out, even_out = local_call(
+        functools.partial(residual_kernel, rim), [moments, group, group, group, group],
+        name="residual",
     )(
-        even, via_odd, via_even, own, b_edges, w_edges, elem_edges, live, elem_matrix, hot
-    )
-    via_odd, via_even = swap(odd_out, even_out)
+        via_first, via_odd, via_even, even, own, b_edges, w_edges, elem_edges, live, elem_matrix, hot
+    )
+    via_first = swap(first_out, firsts)
+    via_odd = swap(odd_out, odd)
+    via_even = swap(even_out, others)
     size = aux_inverse.shape[1]
     r, r_inner, a, slots_hot, parts, nodes = local_call(
         functools.partial(partial_kernel, rim),
@@ -535,7 +543,7 @@
         functools.partial(restrict_kernel, rim, edge_count), [table, (2, LANES), slots],
         scratch=[lists], name="restrict",
     )(
-        even, via_odd, via_even, ends, exists, r, a, elem_edges, live, by_moment, owner_counts
+        via_first, via_odd, via_even, even, ends, exists, r, a, elem_edges, live, by_moment, owner_counts
     )
     arrived = lax.all_to_all(packed, "dom", split_axis=0, concat_axis=0, tiled=True)
     (outgoing,) = local_call(solve_kernel, [(2 * peers, LANES)], name="solve")(
@@ -547,7 +555,7 @@
         functools.partial(prolong_kernel, rim, edge_count),
         [moments, group, (4, LANES), (4, LANES)], scratch=[lists], name="prolong",
     )(even, returned, elem_edges, live, nodal_first, owner_counts, hot)
-    via_odd, via_even = swap(odd_out, even_out)
+    via_odd, via_even = swap(odd_out, odd), swap(even_out, evens)
     z, x1_inner, az = local_call(
         functools.partial(smooth_kernel, rim), [table, inner, moments], name="smooth"
     )(p, r, r_inner, x_inner, w_edges, w_inner, elem_edges, live, elem_matrix, hot)
@@ -557,7 +565,7 @@
     )(
         even, via_odd, via_even, ends, exists, s_rim, az, elem_edges, live, elem_matrix, hot
     )
-    via_odd, via_even = swap(odd_out, even_out)
+    via_odd, via_even = swap(odd_out, odd), swap(even_out, evens)
     x1_edges, r1_part, r1_inner = local_call(
         functools.partial(output_kernel, rim), [x_edges.shape, x_edges.shape, inner],
         name="output",

time: 102 us -> 103 us (level)
  waiting for transfers between devices: 11.5 us -> 8.09 us
  starting transfers between devices: 40.6 us -> 43 us
  blocking collectives: 40.5 us -> 42.7 us
    ppermute x8 -> x10, waiting for transfers between devices: 11.5 us -> 8.09 us  [swap(): return lax.ppermute(message, ('grp', 'dom'), pairs)]
    ppermute x8 -> x10, starting transfers between devices: 40.6 us -> 43 us  [swap(): return lax.ppermute(message, ('grp', 'dom'), pairs)]
    all_to_all x1, blocking collectives: 21.5 us -> 23.8 us  [shards(): lax.all_to_all(packed, 'dom', split_axis=0, concat_axis=0, tiled=True)]
  transfers between devices with their start and end apart: 8 -> 10, of which waited for: 5 -> 4; matrix products, arithmetic and copies ran while one was open for 0% -> 0% of each run, Pallas kernels for 4% -> 4%
where the time goes in v8:
time: 103 us
  starting transfers between devices  43 us (42%)
  blocking collectives  42.7 us (41%)
  waiting for transfers between devices  8.09 us (8%)
  Pallas kernels  8.01 us (8%)
    ppermute x10, starting transfers between devices, swap(): return lax.ppermute(message, ('grp', 'dom'), pairs)  43 us
    all_to_all x1, blocking collectives, shards(): lax.all_to_all(packed, 'dom', split_axis=0, concat_axis=0, tiled=True)  23.8 us
    all_to_all x1, blocking collectives, shards(): lax.all_to_all(outgoing, 'dom', split_axis=0, concat_axis=0, tiled=True)  18.9 us
    ppermute x10, waiting for transfers between devices, swap(): return lax.ppermute(message, ('grp', 'dom'), pairs)  8.09 us
    pallas_call x10, Pallas kernels, call(): pl.pallas_call(kernel, out_shape=shapes, in_specs=[pl.BlockSpec(memory_sp...  8.01 us
  transfers between devices with their start and end apart: 10, of which 4 were waited for; matrix products, arithmetic and copies ran while one was open for 0% of the time, Pallas kernels for 4%

profile of v8, /device:TPU:32, one launch (start us, length us, event | category | flops | bytes accessed | tf_op | source)
XLA Modules:
  0.0 102.7 jit_solution(16955635571075571108)
XLA Ops:
  0.6 3.4 %collective-permute-start = (f32[2,1536]{1,0:T(2,128)}, f32[2,1536]{1,0:T(2,128)S(1)}, u32[]{:S(2)}, u32[]{:S(2)}) collective-permute-start(f32[2,1536]{1,0:T(2,128)} %refs_0_.1), channel_id=1, source_target_pairs={{0,1},{64,65},{128,129},{192,193},{256,257},{320,321},{384,385},{4... | collective-permute-start | bytes 36872 | tf_op jit(solution)/shard_map/ppermute | solution.py:465
  4.0 17.0 %collective-permute-start.1 = (f32[2,1536]{1,0:T(2,128)}, f32[2,1536]{1,0:T(2,128)S(1)}, u32[]{:S(2)}, u32[]{:S(2)}) collective-permute-start(f32[2,1536]{1,0:T(2,128)} %refs_0_.1), channel_id=1, source_target_pairs={{1,2},{3,4},{5,6},{7,8},{9,10},{11,12},{13,14},{15,16},{17,18},{19... | collective-permute-start | bytes 36872 | tf_op jit(solution)/shard_map/ppermute | solution.py:465
  21.1 0.7 collective-permute-start.2
  21.8 1.5 %stage.1 = (f32[2,1536]{1,0:T(2,128)S(1)}, f32[2,1024]{1,0:T(2,128)S(1)}, s32[3,1024]{1,0:T(4,128)S(1)}, s32[1,1024]{1,0:T(1,128)S(1)}, f32[8,8,1024]{2,1,0:T(8,...) custom-call(f32[2,1536]{1,0:T(2,128)} %refs_0_.1, ...), custom_call_target="tpu_custom_call" | custom-call | flops 100000000 | bytes 2000000 | tf_op jit(solution)/shard_map/stage/pallas_call | solution.py:447
  23.3 0.0 collective-permute-done.via_first_ref
  23.3 0.0 collective-permute-done.1.via_odd_ref
  23.3 0.0 collective-permute-done.2.via_even_ref
  23.3 0.4 residual.1
  23.8 1.9 %collective-permute-start.3 = (f32[8,128]{1,0:T(8,128)S(1)}, f32[8,128]{1,0:T(8,128)S(1)}, u32[]{:S(2)}, u32[]{:S(2)}) collective-permute-start(f32[8,128]{1,0:T(8,128)S(1)} %get-tuple-element.55), channel_id=1, source_target_pairs={{0,1},{64,65},{128,129},{192,193},{256,257},{320,321},{384,385},{4... | collective-permute-start | bytes 12296 | tf_op jit(solution)/shard_map/ppermute | solution.py:465
  25.7 7.1 %collective-permute-start.4 = (f32[8,128]{1,0:T(8,128)S(1)}, f32[8,128]{1,0:T(8,128)S(1)}, u32[]{:S(2)}, u32[]{:S(2)}) collective-permute-start(f32[8,128]{1,0:T(8,128)S(1)} %get-tuple-element.56), channel_id=1, source_target_pairs={{1,2},{3,4},{5,6},{7,8},{9,10},{11,12},{13,14},{15,16},{17,18},{19... | collective-permute-start | bytes 12296 | tf_op jit(solution)/shard_map/ppermute | solution.py:465
  32.8 0.7 collective-permute-start.5
  33.5 1.1 %partial.1 = (f32[32,128]{1,0:T(8,128)S(1)}, f32[2,1024]{1,0:T(2,128)S(1)}, f32[8,1024]{1,0:T(8,128)S(1)}, bf16[8192,128]{1,0:T(8,128)(2,1)S(1)}, bf16[256,512]{1,0:T(8,128)(2,1)S(1)}, /*index=5*/s32[64,128]{1,0:T(8,128)S(1)}) custom-call(f32[8,1024]{1,0:T(8,128)S(1)} %get-tuple-element.59.y_ref, f32[2,1536]{1,0:T(2,128)S(1)} %get-tuple-element.49.b_ref, ...), custom_call_target="tpu_custom_call" | custom-call | flops 100000000 | bytes 2000000 | tf_op jit(solution)/shard_map/partial/pallas_call | solution.py:447
  34.6 0.0 collective-permute-done.3.via_first_ref
  34.6 1.4 %collective-permute-done.4.via_odd_ref = f32[8,128]{1,0:T(8,128)S(1)} collective-permute-done((f32[8,128]{1,0:T(8,128)S(1)}, f32[8,128]{1,0:T(8,128)S(1)}, u32[]{:S(2)}, u32[]{:S(2)}) %collective-permute-start.4) | collective-permute-done | bytes 4128 | tf_op jit(solution)/shard_map/ppermute | solution.py:465
  36.0 0.0 collective-permute-done.5.via_even_ref
  36.0 0.6 restrict.1
  36.6 23.8 %all_to_all.10 = f32[64,2,128]{2,1,0:T(2,128)S(1)} all-to-all(f32[64,2,128]{2,1,0:T(2,128)S(1)} %get-tuple-element.67), channel_id=1, replica_groups=mesh['grp'=16,'dom'=64] {'dom'}, dimensions={0} | all-to-all | bytes 131072 | tf_op jit(solution)/shard_map/all_to_all | solution.py:548
  60.4 0.8 solve.1
  61.2 18.9 %all_to_all.11.returned_ref = f32[64,2,128]{2,1,0:T(2,128)S(1)} all-to-all(f32[64,2,128]{2,1,0:T(2,128)S(1)} %bitcast.6), channel_id=1, replica_groups=mesh['grp'=16,'dom'=64] {'dom'}, dimensions={0} | all-to-all | bytes 131072 | tf_op jit(solution)/shard_map/all_to_all | solution.py:553
  80.2 0.6 prolong.1
  80.8 1.9 %collective-permute-start.6 = (f32[4,128]{1,0:T(4,128)S(1)}, f32[4,128]{1,0:T(4,128)S(1)}, u32[]{:S(2)}, u32[]{:S(2)}) collective-permute-start(f32[4,128]{1,0:T(4,128)S(1)} %get-tuple-element.72), channel_id=1, source_target_pairs={{1,2},{3,4},{5,6},{7,8},{9,10},{11,12},{13,14},{15,16},{17,18},{19... | collective-permute-start | bytes 6152 | tf_op jit(solution)/shard_map/ppermute | solution.py:465
  82.7 3.4 %collective-permute-start.7 = (f32[4,128]{1,0:T(4,128)S(1)}, f32[4,128]{1,0:T(4,128)S(1)}, u32[]{:S(2)}, u32[]{:S(2)}) collective-permute-start(f32[4,128]{1,0:T(4,128)S(1)} %get-tuple-element.73), channel_id=1, source_target_pairs={{0,1},{2,3},{4,5},{6,7},{8,9},{10,11},{12,13},{14,15},{16,17},{18,... | collective-permute-start | bytes 6152 | tf_op jit(solution)/shard_map/ppermute | solution.py:465
  86.1 1.1 %smooth.1 = (f32[32,128]{1,0:T(8,128)S(1)}, f32[2,1024]{1,0:T(2,128)}, f32[8,1024]{1,0:T(8,128)S(1)}) custom-call(f32[8,1024]{1,0:T(8,128)S(1)} %get-tuple-element.76.p_ref, f32[32,128]{1,0:T(8,128)S(1)} %get-tuple-element.77.r_ref, f32[2,1024]{1,0:T(2,128)S(1)} %get-tuple-element.78.r_inner_ref, f32[2,1024]{1,0:T(2,128)S(1)} %get-tuple-element.79.inner_ref, ...), custom_call_target="tpu_custom_call" | custom-call | flops 100000000 | bytes 2000000 | tf_op jit(solution)/shard_map/smooth/pallas_call | solution.py:447
  87.2 4.0 %collective-permute-done.6.via_odd_ref = f32[4,128]{1,0:T(4,128)S(1)} collective-permute-done((f32[4,128]{1,0:T(4,128)S(1)}, f32[4,128]{1,0:T(4,128)S(1)}, u32[]{:S(2)}, u32[]{:S(2)}) %collective-permute-start.6) | collective-permute-done | bytes 2080 | tf_op jit(solution)/shard_map/ppermute | solution.py:465
  91.1 0.0 collective-permute-done.7.via_even_ref
  91.1 0.4 update.1
  91.5 5.0 %collective-permute-start.8 = (f32[2,128]{1,0:T(2,128)S(1)}, f32[2,128]{1,0:T(2,128)S(1)}, u32[]{:S(2)}, u32[]{:S(2)}) collective-permute-start(f32[2,128]{1,0:T(2,128)S(1)} %get-tuple-element.89), channel_id=1, source_target_pairs={{1,2},{3,4},{5,6},{7,8},{9,10},{11,12},{13,14},{15,16},{17,18},{19... | collective-permute-start | bytes 3080 | tf_op jit(solution)/shard_map/ppermute | solution.py:465
  96.5 1.9 %collective-permute-start.9 = (f32[2,128]{1,0:T(2,128)S(1)}, f32[2,128]{1,0:T(2,128)S(1)}, u32[]{:S(2)}, u32[]{:S(2)}) collective-permute-start(f32[2,128]{1,0:T(2,128)S(1)} %get-tuple-element.90), channel_id=1, source_target_pairs={{0,1},{2,3},{4,5},{6,7},{8,9},{10,11},{12,13},{14,15},{16,17},{18,... | collective-permute-start | bytes 3080 | tf_op jit(solution)/shard_map/ppermute | solution.py:465
  98.5 0.8 output.1
  99.3 2.6 %collective-permute-done.8.via_odd_ref = f32[2,128]{1,0:T(2,128)S(1)} collective-permute-done((f32[2,128]{1,0:T(2,128)S(1)}, f32[2,128]{1,0:T(2,128)S(1)}, u32[]{:S(2)}, u32[]{:S(2)}) %collective-permute-start.8) | collective-permute-done | bytes 1056 | tf_op jit(solution)/shard_map/ppermute | solution.py:465
  101.9 0.1 collective-permute-done.9.via_even_ref
  102.0 0.7 finish.1
  (4 shorter events, 0.0 us)
Async XLA Ops:
  0.6 22.7 %collective-permute-start = (f32[2,1536]{1,0:T(2,128)}, f32[2,1536]{1,0:T(2,128)S(1)}, u32[]{:S(2)}, u32[]{:S(2)}) collective-permute-start(f32[2,1536]{1,0:T(2,128)} %refs_0_.1), channel_id=1, source_target_pairs={{0,1},{64,65},{128,129},{192,193},{256,257},{320,321},{384,385},{4... | collective-permute-start | bytes 36872 | tf_op jit(solution)/shard_map/ppermute | solution.py:465
  4.0 19.3 %collective-permute-start.1 = (f32[2,1536]{1,0:T(2,128)}, f32[2,1536]{1,0:T(2,128)S(1)}, u32[]{:S(2)}, u32[]{:S(2)}) collective-permute-start(f32[2,1536]{1,0:T(2,128)} %refs_0_.1), channel_id=1, source_target_pairs={{1,2},{3,4},{5,6},{7,8},{9,10},{11,12},{13,14},{15,16},{17,18},{19... | collective-permute-start | bytes 36872 | tf_op jit(solution)/shard_map/ppermute | solution.py:465
  21.1 2.3 %collective-permute-start.2 = (f32[2,1536]{1,0:T(2,128)}, f32[2,1536]{1,0:T(2,128)S(1)}, u32[]{:S(2)}, u32[]{:S(2)}) collective-permute-start(f32[2,1536]{1,0:T(2,128)} %refs_0_.1), channel_id=1, source_target_pairs={{2,3},{4,5},{6,7},{8,9},{10,11},{12,13},{14,15},{16,17},{18,19},{2... | collective-permute-start | bytes 36872 | tf_op jit(solution)/shard_map/ppermute | solution.py:465
  23.8 10.9 %collective-permute-start.3 = (f32[8,128]{1,0:T(8,128)S(1)}, f32[8,128]{1,0:T(8,128)S(1)}, u32[]{:S(2)}, u32[]{:S(2)}) collective-permute-start(f32[8,128]{1,0:T(8,128)S(1)} %get-tuple-element.55), channel_id=1, source_target_pairs={{0,1},{64,65},{128,129},{192,193},{256,257},{320,321},{384,385},{4... | collective-permute-start | bytes 12296 | tf_op jit(solution)/shard_map/ppermute | solution.py:465
  25.7 10.4 %collective-permute-start.4 = (f32[8,128]{1,0:T(8,128)S(1)}, f32[8,128]{1,0:T(8,128)S(1)}, u32[]{:S(2)}, u32[]{:S(2)}) collective-permute-start(f32[8,128]{1,0:T(8,128)S(1)} %get-tuple-element.56), channel_id=1, source_target_pairs={{1,2},{3,4},{5,6},{7,8},{9,10},{11,12},{13,14},{15,16},{17,18},{19... | collective-permute-start | bytes 12296 | tf_op jit(solution)/shard_map/ppermute | solution.py:465
  32.8 3.2 %collective-permute-start.5 = (f32[8,128]{1,0:T(8,128)S(1)}, f32[8,128]{1,0:T(8,128)S(1)}, u32[]{:S(2)}, u32[]{:S(2)}) collective-permute-start(f32[8,128]{1,0:T(8,128)S(1)} %get-tuple-element.57), channel_id=1, source_target_pairs={{2,3},{4,5},{6,7},{8,9},{10,11},{12,13},{14,15},{16,17},{18,19},{2... | collective-permute-start | bytes 12296 | tf_op jit(solution)/shard_map/ppermute | solution.py:465
  80.8 10.3 %collective-permute-start.6 = (f32[4,128]{1,0:T(4,128)S(1)}, f32[4,128]{1,0:T(4,128)S(1)}, u32[]{:S(2)}, u32[]{:S(2)}) collective-permute-start(f32[4,128]{1,0:T(4,128)S(1)} %get-tuple-element.72), channel_id=1, source_target_pairs={{1,2},{3,4},{5,6},{7,8},{9,10},{11,12},{13,14},{15,16},{17,18},{19... | collective-permute-start | bytes 6152 | tf_op jit(solution)/shard_map/ppermute | solution.py:465
  82.7 8.4 %collective-permute-start.7 = (f32[4,128]{1,0:T(4,128)S(1)}, f32[4,128]{1,0:T(4,128)S(1)}, u32[]{:S(2)}, u32[]{:S(2)}) collective-permute-start(f32[4,128]{1,0:T(4,128)S(1)} %get-tuple-element.73), channel_id=1, source_target_pairs={{0,1},{2,3},{4,5},{6,7},{8,9},{10,11},{12,13},{14,15},{16,17},{18,... | collective-permute-start | bytes 6152 | tf_op jit(solution)/shard_map/ppermute | solution.py:465
  91.5 10.3 %collective-permute-start.8 = (f32[2,128]{1,0:T(2,128)S(1)}, f32[2,128]{1,0:T(2,128)S(1)}, u32[]{:S(2)}, u32[]{:S(2)}) collective-permute-start(f32[2,128]{1,0:T(2,128)S(1)} %get-tuple-element.89), channel_id=1, source_target_pairs={{1,2},{3,4},{5,6},{7,8},{9,10},{11,12},{13,14},{15,16},{17,18},{19... | collective-permute-start | bytes 3080 | tf_op jit(solution)/shard_map/ppermute | solution.py:465
  96.5 5.5 %collective-permute-start.9 = (f32[2,128]{1,0:T(2,128)S(1)}, f32[2,128]{1,0:T(2,128)S(1)}, u32[]{:S(2)}, u32[]{:S(2)}) collective-permute-start(f32[2,128]{1,0:T(2,128)S(1)} %get-tuple-element.90), channel_id=1, source_target_pairs={{0,1},{2,3},{4,5},{6,7},{8,9},{10,11},{12,13},{14,15},{16,17},{18,... | collective-permute-start | bytes 3080 | tf_op jit(solution)/shard_map/ppermute | solution.py:465

commit v9 on v5

--- a/solution.py
+++ b/solution.py
@@ -361,8 +361,8 @@
 
 
 def smooth_kernel(
-    rim, p_ref, r_ref, r_inner_ref, inner_ref, w_ref, w_inner_ref, edges_ref, live_ref,
-    matrix_ref, hot_ref, z_ref, x1_inner_ref, y_ref,
+    rim, p_ref, r_ref, r_inner_ref, w_ref, w_inner_ref, edges_ref, live_ref, matrix_ref, hot_ref,
+    z_ref, z_inner_ref, y_ref,
 ):
     edge_count = w_ref.shape[1]
     blocks = edge_count // LANES
@@ -373,7 +373,7 @@
     load_table(z_ref, w_ref)
     z_ref[...] = z_ref[...] * r_ref[...] + jnp.where(row < 2 * blocks, total, 0.0)
     z_inner = w_inner_ref[...] * r_inner_ref[...] + p_ref[6:8, :]
-    x1_inner_ref[...] = inner_ref[...] + z_inner
+    z_inner_ref[...] = z_inner
     u = gather_moments(table_groups(z_ref), highs, z_inner, places)
     y_ref[...] = apply_matrix(matrix_ref, live_ref, u)
 
@@ -400,13 +400,14 @@
 
 
 def output_kernel(
-    rim, y_ref, change_ref, z_ref, r_ref, r_inner_ref, x_ref, edges_ref, hot_ref,
-    x1_ref, r1_ref, r1_inner_ref,
+    rim, y_ref, change_ref, z_ref, z_inner_ref, r_ref, r_inner_ref, x_ref, inner_ref, edges_ref,
+    hot_ref, x1_ref, x1_inner_ref, r1_ref, r1_inner_ref,
 ):
     edge_count = x_ref.shape[1]
     blocks = edge_count // LANES
     places = edge_places(edges_ref, rim, edge_count + 2 * rim)
     total = scatter_moments(y_ref[...], places, hot_ref, row_highs(blocks))
+    x1_inner_ref[...] = inner_ref[...] + z_inner_ref[...]
     r1_inner_ref[...] = r_inner_ref[...] - y_ref[6:8, :]
     for h in range(blocks):
         here = slice(h * LANES, (h + 1) * LANES)
@@ -548,9 +549,9 @@
         [moments, group, (4, LANES), (4, LANES)], scratch=[lists], name="prolong",
     )(even, returned, elem_edges, live, nodal_first, owner_counts, hot)
     via_odd, via_even = swap(odd_out, even_out)
-    z, x1_inner, az = local_call(
+    z, z_inner, az = local_call(
         functools.partial(smooth_kernel, rim), [table, inner, moments], name="smooth"
-    )(p, r, r_inner, x_inner, w_edges, w_inner, elem_edges, live, elem_matrix, hot)
+    )(p, r, r_inner, w_edges, w_inner, elem_edges, live, elem_matrix, hot)
     az, change, odd_out, even_out = local_call(
         functools.partial(update_kernel, rim, edge_count),
         [moments, group, (2, LANES), (2, LANES)], name="update",
@@ -558,10 +559,10 @@
         even, via_odd, via_even, ends, exists, s_rim, az, elem_edges, live, elem_matrix, hot
     )
     via_odd, via_even = swap(odd_out, even_out)
-    x1_edges, r1_part, r1_inner = local_call(
-        functools.partial(output_kernel, rim), [x_edges.shape, x_edges.shape, inner],
+    x1_edges, x1_inner, r1_part, r1_inner = local_call(
+        functools.partial(output_kernel, rim), [x_edges.shape, inner, x_edges.shape, inner],
         name="output",
-    )(az, change, z, r, r_inner, x_edges, elem_edges, hot)
+    )(az, change, z, z_inner, r, r_inner, x_edges, x_inner, elem_edges, hot)
     (r1_edges,) = local_call(
         functools.partial(finish_kernel, rim), [x_edges.shape], name="finish"
     )(even, r1_part, via_odd, via_even)

time: 102 us -> 102 us (level)
  no operation moved by 1% of the time
where the time goes in v9:
time: 102 us; the launch traced here: 101 us
  starting transfers between devices  40.6 us (40%)
  blocking collectives  40.5 us (40%)
  waiting for transfers between devices  12 us (12%)
  Pallas kernels  7.49 us (7%)
    ppermute x4, starting transfers between devices, swap(): return (lax.ppermute(odd, axis, pairs(1)), via_even)  31.5 us
    all_to_all x1, blocking collectives, shards(): lax.all_to_all(packed, 'dom', split_axis=0, concat_axis=0, tiled=True)  21.5 us
    all_to_all x1, blocking collectives, shards(): lax.all_to_all(outgoing, 'dom', split_axis=0, concat_axis=0, tiled=True)  19 us
    ppermute x4, waiting for transfers between devices, swap(): return (lax.ppermute(odd, axis, pairs(1)), via_even)  9.5 us
    ppermute x4, starting transfers between devices, swap(): via_even = lax.ppermute(even, axis, pairs(0))  9.1 us
    pallas_call x10, Pallas kernels, call(): pl.pallas_call(kernel, out_shape=shapes, in_specs=[pl.BlockSpec(memory_sp...  7.49 us
    ppermute x4, waiting for transfers between devices, swap(): via_even = lax.ppermute(even, axis, pairs(0))  2.48 us
  transfers between devices with their start and end apart: 8, of which 5 were waited for; matrix products, arithmetic and copies ran while one was open for 0% of the time, Pallas kernels for 4%

profile of v9, /device:TPU:32, one launch (start us, length us, event | category | flops | bytes accessed | tf_op | source)
XLA Modules:
  0.0 101.4 jit_solution(106428143323261075)
XLA Ops:
  0.6 19.7 %collective-permute-start = (f32[2,1536]{1,0:T(2,128)}, f32[2,1536]{1,0:T(2,128)S(1)}, u32[]{:S(2)}, u32[]{:S(2)}) collective-permute-start(f32[2,1536]{1,0:T(2,128)} %refs_0_.1), channel_id=1, source_target_pairs={{1,2},{3,4},{5,6},{7,8},{9,10},{11,12},{13,14},{15,16},{17,18},{19... | collective-permute-start | bytes 36872 | tf_op jit(solution)/shard_map/ppermute | solution.py:467
  20.4 1.9 %collective-permute-start.1 = (f32[2,1536]{1,0:T(2,128)}, f32[2,1536]{1,0:T(2,128)S(1)}, u32[]{:S(2)}, u32[]{:S(2)}) collective-permute-start(f32[2,1536]{1,0:T(2,128)} %refs_0_.1), channel_id=1, source_target_pairs={{0,1},{2,3},{4,5},{6,7},{8,9},{10,11},{12,13},{14,15},{16,17},{18,... | collective-permute-start | bytes 36872 | tf_op jit(solution)/shard_map/ppermute | solution.py:466
  22.4 1.5 %stage.1 = (f32[2,1536]{1,0:T(2,128)S(1)}, f32[2,1024]{1,0:T(2,128)S(1)}, s32[3,1024]{1,0:T(4,128)S(1)}, s32[1,1024]{1,0:T(1,128)S(1)}, f32[8,8,1024]{2,1,0:T(8,...) custom-call(f32[2,1536]{1,0:T(2,128)} %refs_0_.1, ...), custom_call_target="tpu_custom_call" | custom-call | flops 100000000 | bytes 2000000 | tf_op jit(solution)/shard_map/stage/pallas_call | solution.py:442
  23.9 0.0 collective-permute-done.via_odd_ref
  23.9 2.3 %collective-permute-done.1.via_even_ref = f32[2,1536]{1,0:T(2,128)S(1)} collective-permute-done((f32[2,1536]{1,0:T(2,128)}, f32[2,1536]{1,0:T(2,128)S(1)}, u32[]{:S(2)}, u32[]{:S(2)}) %collective-permute-start.1) | collective-permute-done | bytes 12320 | tf_op jit(solution)/shard_map/ppermute | solution.py:466
  26.2 0.4 residual.1
  26.6 4.9 %collective-permute-start.2 = (f32[8,128]{1,0:T(8,128)S(1)}, f32[8,128]{1,0:T(8,128)S(1)}, u32[]{:S(2)}, u32[]{:S(2)}) collective-permute-start(f32[8,128]{1,0:T(8,128)S(1)} %get-tuple-element.55), channel_id=1, source_target_pairs={{1,2},{3,4},{5,6},{7,8},{9,10},{11,12},{13,14},{15,16},{17,18},{19... | collective-permute-start | bytes 12296 | tf_op jit(solution)/shard_map/ppermute | solution.py:467
  31.5 1.9 %collective-permute-start.3 = (f32[8,128]{1,0:T(8,128)S(1)}, f32[8,128]{1,0:T(8,128)S(1)}, u32[]{:S(2)}, u32[]{:S(2)}) collective-permute-start(f32[8,128]{1,0:T(8,128)S(1)} %get-tuple-element.56), channel_id=1, source_target_pairs={{0,1},{2,3},{4,5},{6,7},{8,9},{10,11},{12,13},{14,15},{16,17},{18,... | collective-permute-start | bytes 12296 | tf_op jit(solution)/shard_map/ppermute | solution.py:466
  33.4 1.1 %partial.1 = (f32[32,128]{1,0:T(8,128)S(1)}, f32[2,1024]{1,0:T(2,128)S(1)}, f32[8,1024]{1,0:T(8,128)S(1)}, bf16[8192,128]{1,0:T(8,128)(2,1)S(1)}, bf16[256,512]{1,0:T(8,128)(2,1)S(1)}, /*index=5*/s32[64,128]{1,0:T(8,128)S(1)}) custom-call(f32[8,1024]{1,0:T(8,128)S(1)} %get-tuple-element.58.y_ref, f32[2,1536]{1,0:T(2,128)S(1)} %get-tuple-element.49.b_ref, ...), custom_call_target="tpu_custom_call" | custom-call | flops 100000000 | bytes 2000000 | tf_op jit(solution)/shard_map/partial/pallas_call | solution.py:442
  34.6 2.4 %collective-permute-done.2.via_odd_ref = f32[8,128]{1,0:T(8,128)S(1)} collective-permute-done((f32[8,128]{1,0:T(8,128)S(1)}, f32[8,128]{1,0:T(8,128)S(1)}, u32[]{:S(2)}, u32[]{:S(2)}) %collective-permute-start.2) | collective-permute-done | bytes 4128 | tf_op jit(solution)/shard_map/ppermute | solution.py:467
  37.0 0.0 collective-permute-done.3.via_even_ref
  37.0 0.6 restrict.1
  37.6 21.5 %all_to_all.10 = f32[64,2,128]{2,1,0:T(2,128)S(1)} all-to-all(f32[64,2,128]{2,1,0:T(2,128)S(1)} %get-tuple-element.66), channel_id=1, replica_groups=mesh['grp'=16,'dom'=64] {'dom'}, dimensions={0} | all-to-all | bytes 131072 | tf_op jit(solution)/shard_map/all_to_all | solution.py:541
  59.1 0.8 solve.1
  60.0 19.0 %all_to_all.11.returned_ref = f32[64,2,128]{2,1,0:T(2,128)S(1)} all-to-all(f32[64,2,128]{2,1,0:T(2,128)S(1)} %bitcast.6), channel_id=1, replica_groups=mesh['grp'=16,'dom'=64] {'dom'}, dimensions={0} | all-to-all | bytes 131072 | tf_op jit(solution)/shard_map/all_to_all | solution.py:546
  78.9 0.6 prolong.1
  79.5 1.9 %collective-permute-start.4 = (f32[4,128]{1,0:T(4,128)S(1)}, f32[4,128]{1,0:T(4,128)S(1)}, u32[]{:S(2)}, u32[]{:S(2)}) collective-permute-start(f32[4,128]{1,0:T(4,128)S(1)} %get-tuple-element.71), channel_id=1, source_target_pairs={{1,2},{3,4},{5,6},{7,8},{9,10},{11,12},{13,14},{15,16},{17,18},{19... | collective-permute-start | bytes 6152 | tf_op jit(solution)/shard_map/ppermute | solution.py:467
  81.5 3.3 %collective-permute-start.5 = (f32[4,128]{1,0:T(4,128)S(1)}, f32[4,128]{1,0:T(4,128)S(1)}, u32[]{:S(2)}, u32[]{:S(2)}) collective-permute-start(f32[4,128]{1,0:T(4,128)S(1)} %get-tuple-element.72), channel_id=1, source_target_pairs={{0,1},{2,3},{4,5},{6,7},{8,9},{10,11},{12,13},{14,15},{16,17},{18,... | collective-permute-start | bytes 6152 | tf_op jit(solution)/shard_map/ppermute | solution.py:466
  84.8 0.6 smooth.1
  85.4 4.5 %collective-permute-done.4.via_odd_ref = f32[4,128]{1,0:T(4,128)S(1)} collective-permute-done((f32[4,128]{1,0:T(4,128)S(1)}, f32[4,128]{1,0:T(4,128)S(1)}, u32[]{:S(2)}, u32[]{:S(2)}) %collective-permute-start.4) | collective-permute-done | bytes 2080 | tf_op jit(solution)/shard_map/ppermute | solution.py:467
  89.9 0.0 collective-permute-done.5.via_even_ref
  89.9 0.4 update.1
  90.3 5.0 %collective-permute-start.6 = (f32[2,128]{1,0:T(2,128)S(1)}, f32[2,128]{1,0:T(2,128)S(1)}, u32[]{:S(2)}, u32[]{:S(2)}) collective-permute-start(f32[2,128]{1,0:T(2,128)S(1)} %get-tuple-element.89), channel_id=1, source_target_pairs={{1,2},{3,4},{5,6},{7,8},{9,10},{11,12},{13,14},{15,16},{17,18},{19... | collective-permute-start | bytes 3080 | tf_op jit(solution)/shard_map/ppermute | solution.py:467
  95.3 1.9 %collective-permute-start.7 = (f32[2,128]{1,0:T(2,128)S(1)}, f32[2,128]{1,0:T(2,128)S(1)}, u32[]{:S(2)}, u32[]{:S(2)}) collective-permute-start(f32[2,128]{1,0:T(2,128)S(1)} %get-tuple-element.90), channel_id=1, source_target_pairs={{0,1},{2,3},{4,5},{6,7},{8,9},{10,11},{12,13},{14,15},{16,17},{18,... | collective-permute-start | bytes 3080 | tf_op jit(solution)/shard_map/ppermute | solution.py:466
  97.2 0.8 output.1
  98.0 2.6 %collective-permute-done.6.via_odd_ref = f32[2,128]{1,0:T(2,128)S(1)} collective-permute-done((f32[2,128]{1,0:T(2,128)S(1)}, f32[2,128]{1,0:T(2,128)S(1)}, u32[]{:S(2)}, u32[]{:S(2)}) %collective-permute-start.6) | collective-permute-done | bytes 1056 | tf_op jit(solution)/shard_map/ppermute | solution.py:467
  100.6 0.1 collective-permute-done.7.via_even_ref
  100.8 0.7 finish.1
  (4 shorter events, 0.0 us)
Async XLA Ops:
  0.6 23.2 %collective-permute-start = (f32[2,1536]{1,0:T(2,128)}, f32[2,1536]{1,0:T(2,128)S(1)}, u32[]{:S(2)}, u32[]{:S(2)}) collective-permute-start(f32[2,1536]{1,0:T(2,128)} %refs_0_.1), channel_id=1, source_target_pairs={{1,2},{3,4},{5,6},{7,8},{9,10},{11,12},{13,14},{15,16},{17,18},{19... | collective-permute-start | bytes 36872 | tf_op jit(solution)/shard_map/ppermute | solution.py:467
  20.4 5.8 %collective-permute-start.1 = (f32[2,1536]{1,0:T(2,128)}, f32[2,1536]{1,0:T(2,128)S(1)}, u32[]{:S(2)}, u32[]{:S(2)}) collective-permute-start(f32[2,1536]{1,0:T(2,128)} %refs_0_.1), channel_id=1, source_target_pairs={{0,1},{2,3},{4,5},{6,7},{8,9},{10,11},{12,13},{14,15},{16,17},{18,... | collective-permute-start | bytes 36872 | tf_op jit(solution)/shard_map/ppermute | solution.py:466
  26.6 10.4 %collective-permute-start.2 = (f32[8,128]{1,0:T(8,128)S(1)}, f32[8,128]{1,0:T(8,128)S(1)}, u32[]{:S(2)}, u32[]{:S(2)}) collective-permute-start(f32[8,128]{1,0:T(8,128)S(1)} %get-tuple-element.55), channel_id=1, source_target_pairs={{1,2},{3,4},{5,6},{7,8},{9,10},{11,12},{13,14},{15,16},{17,18},{19... | collective-permute-start | bytes 12296 | tf_op jit(solution)/shard_map/ppermute | solution.py:467
  31.5 5.5 %collective-permute-start.3 = (f32[8,128]{1,0:T(8,128)S(1)}, f32[8,128]{1,0:T(8,128)S(1)}, u32[]{:S(2)}, u32[]{:S(2)}) collective-permute-start(f32[8,128]{1,0:T(8,128)S(1)} %get-tuple-element.56), channel_id=1, source_target_pairs={{0,1},{2,3},{4,5},{6,7},{8,9},{10,11},{12,13},{14,15},{16,17},{18,... | collective-permute-start | bytes 12296 | tf_op jit(solution)/shard_map/ppermute | solution.py:466
  79.5 10.3 %collective-permute-start.4 = (f32[4,128]{1,0:T(4,128)S(1)}, f32[4,128]{1,0:T(4,128)S(1)}, u32[]{:S(2)}, u32[]{:S(2)}) collective-permute-start(f32[4,128]{1,0:T(4,128)S(1)} %get-tuple-element.71), channel_id=1, source_target_pairs={{1,2},{3,4},{5,6},{7,8},{9,10},{11,12},{13,14},{15,16},{17,18},{19... | collective-permute-start | bytes 6152 | tf_op jit(solution)/shard_map/ppermute | solution.py:467
  81.5 8.4 %collective-permute-start.5 = (f32[4,128]{1,0:T(4,128)S(1)}, f32[4,128]{1,0:T(4,128)S(1)}, u32[]{:S(2)}, u32[]{:S(2)}) collective-permute-start(f32[4,128]{1,0:T(4,128)S(1)} %get-tuple-element.72), channel_id=1, source_target_pairs={{0,1},{2,3},{4,5},{6,7},{8,9},{10,11},{12,13},{14,15},{16,17},{18,... | collective-permute-start | bytes 6152 | tf_op jit(solution)/shard_map/ppermute | solution.py:466
  90.3 10.3 %collective-permute-start.6 = (f32[2,128]{1,0:T(2,128)S(1)}, f32[2,128]{1,0:T(2,128)S(1)}, u32[]{:S(2)}, u32[]{:S(2)}) collective-permute-start(f32[2,128]{1,0:T(2,128)S(1)} %get-tuple-element.89), channel_id=1, source_target_pairs={{1,2},{3,4},{5,6},{7,8},{9,10},{11,12},{13,14},{15,16},{17,18},{19... | collective-permute-start | bytes 3080 | tf_op jit(solution)/shard_map/ppermute | solution.py:467
  95.3 5.5 %collective-permute-start.7 = (f32[2,128]{1,0:T(2,128)S(1)}, f32[2,128]{1,0:T(2,128)S(1)}, u32[]{:S(2)}, u32[]{:S(2)}) collective-permute-start(f32[2,128]{1,0:T(2,128)S(1)} %get-tuple-element.90), channel_id=1, source_target_pairs={{0,1},{2,3},{4,5},{6,7},{8,9},{10,11},{12,13},{14,15},{16,17},{18,... | collective-permute-start | bytes 3080 | tf_op jit(solution)/shard_map/ppermute | solution.py:466
